TPU v7x, 256 devices: a whole 4x4x8 slice. The times are simulated.
256 devices in a mesh: row: 16 (over z, y_lo), col: 16 (over x, y_hi, core).
Axes of the slice: x: 4, y: 4 (y_hi: 2, y_lo: 2; y = y_hi * 2 + y_lo), z: 8, core: 2. Of those that a mesh axis runs over, the one named last changes fastest.
Arguments:
- query_in: bfloat16 [2, 1536, 384], P(None, 'row'), may hold values from -10 to 10
- key_in: bfloat16 [2, 1536, 384], P(None, 'row'), may hold values from -10 to 10
- value_in: bfloat16 [2, 1536, 384], P(None, 'row'), may hold values from -6 to 6
- pair: bfloat16 [2, 1536, 1536, 128], P(None, 'row', 'col'), may hold values from -6 to 6
- bias_weight: bfloat16 [128, 16], replicated, may hold values from -0.5 to 0.5
- d_out: bfloat16 [2, 1536, 384], P(None, 'row'), may hold values from -192 to 192
Outputs:
- d_query: float32 [2, 1536, 384], P(None, 'row', 'col')
- d_key: float32 [2, 1536, 384], P(None, 'col', 'row')
- d_value: float32 [2, 1536, 384], P(None, 'col', 'row')
- d_pair: bfloat16 [2, 1536, 1536, 128], P(None, 'row', 'col')
- d_bias_weight: float32 [128, 16], replicated
All inputs are finite; a program needn't handle non-finite values.
Results may differ from a plain program's by a relative error of at most 0.022.
Values may be sent and summed in bfloat16 or wider, within the bound.
No kernel may reach another device: no remote copies, remote signals or barrier semaphores. Data moves between devices by JAX's collectives and lax.ppermute only.
A program may use at most 64 MiB of HBM per device.

v0:
```python
import math

import jax
import jax.numpy as jnp
from jax import lax
from jax.sharding import PartitionSpec as P

EPS = 1e-05


def shards(query_in, key_in, value_in, pair, bias_weight, d_out):
    n_batch, q_rows, width_all = query_in.shape
    head_count = bias_weight.shape[1]
    head_size = width_all // head_count
    score_scale = 1.0 / math.sqrt(head_size)
    key_count = pair.shape[2]
    column = lax.axis_index("col")
    keys_all, values_all = (
        lax.all_gather(key_in, "row", axis=1, tiled=True),
        lax.all_gather(value_in, "row", axis=1, tiled=True),
    )
    key_block = lax.dynamic_slice_in_dim(keys_all, column * key_count, key_count, 1)
    value_block = lax.dynamic_slice_in_dim(values_all, column * key_count, key_count, 1)
    queries = query_in.reshape(n_batch, q_rows, head_count, head_size)
    key_heads = key_block.reshape(n_batch, key_count, head_count, head_size)
    value_heads = value_block.reshape(n_batch, key_count, head_count, head_size)
    grads_out = d_out.reshape(n_batch, q_rows, head_count, head_size)
    pair_float = pair.astype(jnp.float32)
    centre = jnp.mean(pair_float, -1, keepdims=True)
    spread = jnp.mean(jnp.square(pair_float - centre), -1, keepdims=True)
    inverse = lax.rsqrt(spread + EPS)
    normed = (pair_float - centre) * inverse
    normed_low = normed.astype(jnp.bfloat16)
    pair_bias = jnp.einsum(
        "bijc,ch->bhij", normed_low, bias_weight, preferred_element_type=jnp.float32
    )
    logits = (
        jnp.einsum("bihc,bjhc->bhij", queries, key_heads, preferred_element_type=jnp.float32)
        * score_scale
        + pair_bias
    )
    d_weights = jnp.einsum(
        "bihc,bjhc->bhij", grads_out, value_heads, preferred_element_type=jnp.float32
    )
    local_top = jnp.max(logits, -1)
    row_top = lax.pmax(local_top, "col")
    expo = jnp.exp(logits - row_top[..., None])
    row_total, row_inner = lax.psum((jnp.sum(expo, -1), jnp.sum(expo * d_weights, -1)), "col")
    weights = expo / row_total[..., None]
    balance = row_inner / row_total
    d_logits = weights * (d_weights - balance[..., None])
    ds_low = d_logits.astype(jnp.bfloat16)
    weights_low = weights.astype(jnp.bfloat16)
    query_part = jnp.einsum(
        "bhij,bjhc->bihc", ds_low, key_heads, preferred_element_type=jnp.float32
    )
    query_part = query_part.reshape(n_batch, q_rows, width_all) * score_scale
    d_query = lax.psum_scatter(
        query_part.astype(jnp.bfloat16), "col", scatter_dimension=2, tiled=True
    ).astype(jnp.float32)
    key_part = jnp.einsum("bhij,bihc->bjhc", ds_low, queries, preferred_element_type=jnp.float32)
    key_part = key_part.reshape(n_batch, key_count, width_all) * score_scale
    value_part = jnp.einsum(
        "bhij,bihc->bjhc", weights_low, grads_out, preferred_element_type=jnp.float32
    )
    value_part = value_part.reshape(n_batch, key_count, width_all)
    d_key, d_value = (
        lax.psum_scatter(
            key_part.astype(jnp.bfloat16), "row", scatter_dimension=2, tiled=True
        ).astype(jnp.float32),
        lax.psum_scatter(
            value_part.astype(jnp.bfloat16), "row", scatter_dimension=2, tiled=True
        ).astype(jnp.float32),
    )
    weight_part = jnp.einsum(
        "bijc,bhij->ch", normed_low, ds_low, preferred_element_type=jnp.float32
    )
    d_bias_weight = lax.psum(weight_part, ("row", "col"))
    pair_back = jnp.einsum("bhij,ch->bijc", ds_low, bias_weight, preferred_element_type=jnp.float32)
    d_pair = (
        inverse
        * (
            pair_back
            - jnp.mean(pair_back, -1, keepdims=True)
            - normed * jnp.mean(pair_back * normed, -1, keepdims=True)
        )
    ).astype(jnp.bfloat16)
    return (d_query, d_key, d_value, d_pair, d_bias_weight)


def solution(mesh):
    in_specs = (
        P(None, "row", None),
        P(None, "row", None),
        P(None, "row", None),
        P(None, "row", "col", None),
        P(),
        P(None, "row", None),
    )
    out_specs = (
        P(None, "row", "col"),
        P(None, "col", "row"),
        P(None, "col", "row"),
        P(None, "row", "col", None),
        P(),
    )
    return jax.shard_map(shards, mesh=mesh, in_specs=in_specs, out_specs=out_specs, check_vma=False)
```

profile of v0, /device:TPU:16, one launch (start us, length us, event | category | flops | bytes accessed | tf_op | source)
XLA Modules:
  0.0 545.1 jit_solution(8457868269692736364)
XLA Ops:
  7.2 0.0 copy-start
  7.2 0.0 all-gather.3.cloned.1.call-start
  7.2 0.7 all-gather.3.cloned.1.call-update
  7.9 0.0 all-gather.5.cloned.1.call-start
  8.0 0.7 all-gather.5.cloned.1.call-update
  8.7 0.0 reduce-scatter.10.cloned.1.call-start
  8.7 1.1 copy.34
  9.8 1.7 copy.37
  11.5 4.3 convert_reduce_fusion
  15.8 0.0 copy-done.1
  15.8 0.0 copy-start.3
  15.8 6.3 %fusion.9 = f32[2,96,96]{2,1,0:T(8,128)S(1)} fusion(bf16[2,96,96,128]{3,2,1,0:T(8,128)(2,1)S(1)} %copy-done.1, f32[2,96,96]{2,1,0:T(8,128)S(1)} %broadcast_multiply_fusion.2), kind=kLoop, calls=%fused_computation.11 | loop fusion | flops 9418752 | bytes 4866048 | tf_op jit(solution)/shard_map/reduce_sum | solution.py:30
  22.2 0.0 copy-done.3
  22.2 0.0 copy-start.5
  22.2 0.6 copy-done.5
  22.8 0.0 copy-done
  22.9 10.9 %fusion.12 = f32[2,96,96,16]{2,3,1,0:T(8,128)S(1)} fusion(bf16[2,96,96,128]{3,2,1,0:T(8,128)(2,1)S(1)} %copy-done.1, f32[2,96,96]{2,1,0:T(8,128)S(1)} %add_rsqrt_fusion, f32[2,96,96]{2,1,0:T(8,128)S(1)} %broadcast_multiply_fusion.2, bf16[128,16]{0,1:T(8,128)(2,1)S(1)} %copy-done), kind=kOutput, calls=%fused_computation.13 | convolution fusion | flops 84934656 | bytes 6049792 | tf_op jit(solution)/shard_map/bijc,ch->bhij/dot_general | solution.py:34
  33.7 0.7 copy.35
  34.4 52.5 %all-gather.3.cloned.1.call-done = bf16[2,1536,384]{2,1,0:T(8,128)(2,1)} async-done(((bf16[2,96,384]{2,1,0:T(8,128)(2,1)}), bf16[2,1536,384]{2,1,0:T(8,128)(2,1)}) %all-gather.3.cloned.1.call-update) | async-done | bytes 2359312 | tf_op jit(solution)/shard_map/all_gather | solution.py:19
  86.9 75.2 %all-gather.5.cloned.1.call-done = bf16[2,1536,384]{2,1,0:T(8,128)(2,1)} async-done(((bf16[2,96,384]{2,1,0:T(8,128)(2,1)}), bf16[2,1536,384]{2,1,0:T(8,128)(2,1)}) %all-gather.5.cloned.1.call-update) | async-done | bytes 2359312 | tf_op jit(solution)/shard_map/all_gather | solution.py:20
  162.1 1.0 constant_dynamic-slice_fusion
  163.1 0.8 copy.36
  163.9 0.2 copy.33
  164.1 1.1 fusion.30
  165.2 59.3 %pmax.7 = f32[2,16,96]{2,1,0:T(8,128)S(1)} all-reduce(f32[2,16,96]{2,1,0:T(8,128)} %get-tuple-element.11), channel_id=1, replica_groups=mesh['row'=16,'col'=16] {'col'}, use_global_device_ids=true, to_apply=%region_3.0 | all-reduce | flops 3072 | bytes 24576 | tf_op jit(solution)/shard_map/pmax | solution.py:46
  224.5 2.8 fusion.18
  227.3 64.9 %all-reduce = (f32[2,16,96]{2,1,0:T(8,128)S(1)}, f32[2,16,96]{2,1,0:T(8,128)S(1)}) all-reduce(f32[2,16,96]{2,1,0:T(8,128)S(1)} %get-tuple-element.8, f32[2,16,96]{2,1,0:T(8,128)S(1)} %get-tuple-element.7), channel_id=1, replica_groups=mesh['row'=16,'col'=16] {'col'}, use_global_device_ids=true, to_apply=%region_7.0 | all-reduce | flops 6144 | bytes 49152 | tf_op jit(solution)/shard_map/psum | solution.py:48
  292.2 1.6 convolution_convert_fusion
  293.8 0.0 copy-start.4
  293.8 0.0 copy-start.6
  293.9 0.0 copy-done.2
  293.9 0.5 fusion.16
  294.4 0.3 fusion.19
  294.7 0.0 slice-start
  294.8 0.7 copy.41
  295.4 0.0 copy-done.4
  295.4 0.0 copy-done.6
  295.4 0.0 slice-start.1
  295.4 9.2 %fusion.21 = f32[128,16]{0,1:T(8,128)S(1)} fusion(bf16[2,16,96,96]{3,1,2,0:T(8,128)(2,1)S(1)} %copy.41, bf16[2,96,96,128]{3,2,1,0:T(8,128)(2,1)} %param.9, f32[2,96,96]{2,1,0:T(8,128)S(1)} %copy-done.6, f32[2,96,96]{2,1,0:T(8,128)S(1)} %copy-done.4), kind=kOutput, calls=%fused_computation.28 | convolution fusion | flops 84934656 | bytes 5464064 | tf_op jit(solution)/shard_map/bijc,bhij->ch/dot_general | solution.py:75
  304.6 0.0 slice-done
  304.6 17.7 %fusion.29 = (f32[2,96,96]{2,1,0:T(8,128)S(1)}, f32[2,96,96]{2,1,0:T(8,128)S(1)}, f32[2,96,96,128]{3,2,1,0:T(8,128)}) fusion(f32[2,96,96]{2,1,0:T(8,128)S(1)} %copy-done.6, f32[2,96,96]{2,1,0:T(8,128)S(1)} %copy-done.4, bf16[2,96,96,128]{3,2,1,0:T(8,128)(2,1)S(1)} %bitcast.66, bf16[2,16,96,96]{3,1,2,0:T(8,128)(2,1)S(1)} %copy.41, ...), kind=kOutput, calls=%fused_computation.45 | convolution fusion | flops 89616384 | bytes 15044608 | tf_op jit(solution)/shard_map/bhij,ch->bijc/dot_general | solution.py:79
  322.3 0.2 copy.60
  322.5 0.8 reshape.65
  323.4 0.2 copy.62
  323.6 0.8 reshape.61
  324.4 0.0 reduce-scatter.10.cloned.1.call-update
  324.4 0.0 reduce-scatter.14.cloned.1.call-start
  324.5 0.5 fusion.20
  325.0 0.0 reduce-scatter.14.cloned.1.call-update
  325.0 0.0 reduce-scatter.12.cloned.1.call-start
  325.1 0.2 copy.61
  325.3 0.8 reshape.63
  326.1 77.4 %psum.23 = f32[128,16]{0,1:T(8,128)} all-reduce(f32[128,16]{0,1:T(8,128)S(1)} %fusion.21), channel_id=1, replica_groups=mesh['row'=16,'col'=16] {'row','col'}, use_global_device_ids=true, to_apply=%region_13.0 | all-reduce | flops 2048 | bytes 16384 | tf_op jit(solution)/shard_map/psum | solution.py:78
  403.5 0.0 reduce-scatter.12.cloned.1.call-update
  403.5 13.9 %fusion.8 = bf16[2,96,96,128]{3,2,1,0:T(8,128)(2,1)} fusion(bf16[2,96,96,128]{3,2,1,0:T(8,128)(2,1)} %param.9, f32[2,96,96,128]{3,2,1,0:T(8,128)} %get-tuple-element.14, f32[2,96,96]{2,1,0:T(8,128)S(1)} %broadcast_multiply_fusion, f32[2,96,96]{2,1,0:T(8,128)S(1)} %broadcast_multiply_fusion.1, f32[2,96,96]{2,1,0:T(8,128)S(1)} %copy-done.6, ...), kind=kLoop, calls=%fused_computation.10 | loop fusion | flops 18874368 | bytes 19169280 | tf_op jit(solution)/shard_map/convert_element_type | solution.py:87
  417.5 0.0 reduce-scatter.10.cloned.1.call-done
  417.5 0.8 reshape.62
  418.3 0.6 copy_convert_fusion.2
  418.9 47.6 %reduce-scatter.14.cloned.1.call-done = bf16[24,192]{1,0:T(8,128)(2,1)} async-done(((bf16[384,192]{1,0:T(8,128)(2,1)}), bf16[24,192]{1,0:T(8,128)(2,1)}) %reduce-scatter.14.cloned.1.call-update) | async-done | bytes 9232
  466.5 0.8 reshape.66
  467.3 0.6 copy_convert_fusion
  467.9 69.3 %reduce-scatter.12.cloned.1.call-done = bf16[24,192]{1,0:T(8,128)(2,1)} async-done(((bf16[384,192]{1,0:T(8,128)(2,1)}), bf16[24,192]{1,0:T(8,128)(2,1)}) %reduce-scatter.12.cloned.1.call-update) | async-done | bytes 9232
  537.2 0.8 reshape.64
  538.0 0.6 copy_convert_fusion.1
  (9 shorter events, 0.1 us)
Async XLA Ops:
  7.2 15.7 %copy-start = (bf16[128,16]{0,1:T(8,128)(2,1)S(1)}, bf16[128,16]{0,1:T(8,128)(2,1)}, u32[]{:S(2)}) copy-start(bf16[128,16]{0,1:T(8,128)(2,1)} %param.10) | copy-start | bytes 12292
  7.2 79.7 %all-gather.3.cloned.1.call-start = ((), (), s32[]{:S(2)}) async-start(), calls=%async_computation.3 | async-start | bytes 2506752 | tf_op jit(solution)/shard_map/all_gather | solution.py:19
  7.9 154.2 %all-gather.5.cloned.1.call-start = ((), (), s32[]{:S(2)}) async-start(), calls=%async_computation.4 | async-start | bytes 2506752 | tf_op jit(solution)/shard_map/all_gather | solution.py:20
  8.7 408.8 %reduce-scatter.10.cloned.1.call-start = ((), (), s32[]{:S(2)}) async-start(), calls=%async_computation.5 | async-start | bytes 208896
  11.5 4.3 copy-start.1
  15.8 6.4 %copy-start.3 = (f32[2,96,96]{2,1,0:T(8,128)}, f32[2,96,96]{2,1,0:T(8,128)S(1)}, u32[]{:S(2)}) copy-start(f32[2,96,96]{2,1,0:T(8,128)S(1)} %broadcast_multiply_fusion.2) | copy-start | bytes 221188
  22.2 0.6 copy-start.5
  292.2 1.6 copy-start.2
  293.8 1.6 copy-start.4
  293.8 1.6 copy-start.6
  294.7 9.9 %slice-start = ((s8[4718592]{0:T(1024)(128)(4,1)}), s8[524288]{0:T(1024)(128)(4,1)S(1)}, s32[]{:S(2)}) async-start(s8[4718592]{0:T(1024)(128)(4,1)} %bitcast.65), calls=%async_computation.8 | async-start | bytes 1048576
  295.4 9.2 %slice-start.1 = ((s8[4718592]{0:T(1024)(128)(4,1)}), s8[4194304]{0:T(1024)(128)(4,1)S(1)}, s32[]{:S(2)}) async-start(s8[4718592]{0:T(1024)(128)(4,1)} %bitcast.65), calls=%async_computation.9 | async-start | bytes 8388608
  324.4 142.1 %reduce-scatter.14.cloned.1.call-start = ((), (), s32[]{:S(2)}) async-start(), calls=%async_computation.7 | async-start | bytes 208896
  325.0 212.2 %reduce-scatter.12.cloned.1.call-start = ((), (), s32[]{:S(2)}) async-start(), calls=%async_computation.6 | async-start | bytes 208896
Sparse Core Ops, SparseCore 0:
  9.8 77.0 all-gather.2
  88.7 73.3 all-gather.4
  324.5 70.1 reduce-scatter.9
  397.1 69.3 reduce-scatter.13
  469.0 68.1 reduce-scatter.11
where the time goes:
time: 546 us; the launch traced here: 545 us
  waiting for transfers between devices  246 us (45%)
  blocking collectives  202 us (37%)
  matrix products  44.1 us (8%)
  other arithmetic  27 us (5%)
  between operations  14 us (3%)
  local copies, waits for them, and re-layouts  12.2 us (2%)
    unnamed x8, waiting for transfers between devices  118 us
    psum x1, blocking collectives, shards(): d_bias_weight = lax.psum(weight_part, ('row', 'col'))  77.4 us
    all_gather x1, waiting for transfers between devices, shards(): lax.all_gather(value_in, 'row', axis=1, tiled=True)  75.2 us
    psum x1, blocking collectives, shards(): lax.psum((jnp.sum(expo, -1), jnp.sum(expo * d_weights, -1)), 'col')  64.9 us
    pmax x1, blocking collectives, shards(): row_top = lax.pmax(local_top, 'col')  59.3 us
    all_gather x1, waiting for transfers between devices, shards(): lax.all_gather(key_in, 'row', axis=1, tiled=True)  52.5 us
    dot_general x1, matrix products, shards(): jnp.einsum('bhij,ch->bijc', ds_low, bias_weight, preferred_element_type=j...  17.7 us
    convert_element_type x1, other arithmetic, shards(): d_pair = (inverse * (pair_back - jnp.mean(pair_back, -1, keepdims=True) -...  13.9 us
  transfers between devices with their start and end apart: 5, of which 4 were waited for; matrix products, arithmetic and copies ran while one was open for 8% of the time, Pallas kernels for 0%

commit v1 on v0

v1 whole, which is shorter than its diff:
```python
import math

import jax
import jax.numpy as jnp
from jax import lax
from jax.experimental import pallas as pl
from jax.experimental.pallas import tpu as pltpu
from jax.sharding import PartitionSpec as P

EPS = 1e-05
F32 = jnp.float32
BF16 = jnp.bfloat16

B = 2
H = 16
C = 24
HC = H * C
CP = 128
T = 96
G = 12
I8 = 8
WIDE = I8 * CP
QH = T * H
SCALE = 1.0 / math.sqrt(C)
PEERS = 16

NN = (((1,), (0,)), ((), ()))
NT = (((1,), (1,)), ((), ()))
TN = (((0,), (0,)), ((), ()))


def dot(left, right, dims=NN):
    return lax.dot_general(left, right, dims, preferred_element_type=F32)


def iota(shape, dim):
    return lax.broadcasted_iota(jnp.int32, shape, dim)


def head_mask():
    row_head = (iota((HC, 128), 0) * 171) >> 12
    return row_head == (iota((HC, 128), 1) & (H - 1))


def query_lanes(rows, first):
    return jnp.where(iota((rows, QH), 0) - first == (iota((rows, QH), 1) >> 4), 1.0, 0.0).astype(BF16)


def block_diagonal(tile, rows_per_block):
    row_block = iota((128, CP), 0) // rows_per_block
    zero = jnp.zeros_like(tile)
    return jnp.concatenate([jnp.where(row_block == i, tile, zero) for i in range(I8)], axis=1)


def expand_kernel(q_ref, g_ref, qt_ref, gt_ref):
    lanes = query_lanes(T, 0)
    mask = head_mask()
    for source, target in ((q_ref, qt_ref), (g_ref, gt_ref)):
        for b in range(B):
            spread = dot(source[b], lanes, TN)
            for g in range(G):
                at = slice(g * 128, (g + 1) * 128)
                target[b, :, at] = jnp.where(mask, spread[:, at], 0.0).astype(BF16)


def norm_kernel(groups, pair_ref, wt_ref, n_ref, bias_ref, inv_ref, ones_ref, diag_ref):
    first = (pl.program_id(0) == 0) & (pl.program_id(1) == 0)

    @pl.when(first)
    def _():
        same = (iota((256, 256), 0) >> 7) == (iota((256, 256), 1) >> 7)
        ones_ref[...] = jnp.where(same, 1.0 / CP, 0.0).astype(BF16)
        wt = wt_ref[...].astype(F32)
        diag_ref[...] = block_diagonal(jnp.concatenate([wt] * I8, axis=0), H).astype(BF16)

    ones = ones_ref[...]
    lane_query = iota((T, 128), 1) >> 4
    for g in range(groups):
        halves = []
        compact = jnp.zeros((T, 128), F32)
        for p in range(I8 // 2):
            x = jnp.concatenate(
                [pair_ref[0, g * I8 + 2 * p], pair_ref[0, g * I8 + 2 * p + 1]], axis=1
            )
            centred = x.astype(F32) - dot(x, ones)
            spread = dot((centred * centred).astype(BF16), ones)
            inverse = lax.rsqrt(spread + EPS)
            normed = (centred * inverse).astype(BF16)
            n_ref[0, g, :, p * 256 : (p + 1) * 256] = normed
            halves.append(normed)
            for k in range(2):
                compact = jnp.where(
                    lane_query == 2 * p + k, inverse[:, k * CP : (k + 1) * CP], compact
                )
        inv_ref[0, g] = compact
        bias_ref[0, g] = dot(jnp.concatenate(halves, axis=1), diag_ref[...], NT)


def logits_kernel(k_ref, v_ref, qt_ref, gt_ref, bias_ref, logits_ref, dw_ref, stats_ref):
    for b in range(B):
        scores = dot(k_ref[b], qt_ref[b])
        inner = dot(v_ref[b], gt_ref[b])
        for g in range(G):
            at = slice(g * 128, (g + 1) * 128)
            logits = scores[:, at] * SCALE + bias_ref[b, g]
            dw = inner[:, at]
            logits_ref[b, g] = logits
            dw_ref[b, g] = dw
            top = jnp.max(logits, axis=0, keepdims=True)
            expo = jnp.exp(logits - top)
            total = jnp.sum(expo, axis=0, keepdims=True)
            level = top + jnp.log(total)
            balance = jnp.sum(expo * dw, axis=0, keepdims=True) / total
            row = b * 2 * G + g
            stats_ref[:, row : row + 1, :] = jnp.broadcast_to(level[None], (PEERS, 1, 128))
            stats_ref[:, row + G : row + G + 1, :] = jnp.broadcast_to(balance[None], (PEERS, 1, 128))


def grads_kernel(
    stats_ref, logits_ref, dw_ref, bias_ref, inv_ref, n_ref, qt_ref, gt_ref, k_ref,
    scaled_ref, along_ref, kv_ref, dq_ref, dwt_ref, ds_ref, w_ref,
):
    for b in range(B):
        levels = stats_ref[:, b * 2 * G : b * 2 * G + G, :]
        balances = stats_ref[:, b * 2 * G + G : (b + 1) * 2 * G, :]
        top = jnp.max(levels, axis=0)
        parts = jnp.exp(levels - top[None])
        total = jnp.sum(parts, axis=0)
        level = top + jnp.log(total)
        balance = jnp.sum(parts * balances, axis=0) / total
        for g in range(G):
            weights = jnp.exp(logits_ref[b, g] - level[g : g + 1])
            ds = weights * (dw_ref[b, g] - balance[g : g + 1])
            low = ds.astype(BF16)
            at = slice(g * 128, (g + 1) * 128)
            ds_ref[b, :, at] = low
            w_ref[b, :, at] = weights.astype(BF16)
            scaled = low.astype(F32) * inv_ref[b, g]
            scaled_ref[b, g] = scaled.astype(BF16)
            along_ref[b, g] = (scaled * bias_ref[b, g] * (1.0 / CP)).astype(BF16)

    total = jnp.zeros((128, WIDE), F32)
    for b in range(B):
        left = jnp.concatenate([ds_ref[b, :, g * 128 : (g + 1) * 128] for g in range(G)], axis=0)
        total = total + dot(left, n_ref[b].reshape(G * T, WIDE), TN)
    dwt = jnp.zeros((H, CP), F32)
    for i in range(I8):
        dwt = dwt + total[i * H : (i + 1) * H, i * CP : (i + 1) * CP]
    dwt_ref[...] = dwt

    mask = head_mask()
    keys, values = [], []
    queries = jnp.zeros((HC, 2 * T), F32)
    for b in range(B):
        keys.append(dot(qt_ref[b], ds_ref[b], NT) * SCALE)
        values.append(dot(gt_ref[b], w_ref[b], NT))
        spread = dot(k_ref[b], ds_ref[b], TN)
        chosen = jnp.concatenate(
            [
                jnp.where(mask, spread[:, g * 128 : (g + 1) * 128], 0.0).astype(BF16)
                for g in range(G)
            ],
            axis=1,
        )
        queries = queries + dot(chosen, query_lanes(2 * T, b * T), NT)
    kv = jnp.concatenate(keys + values, axis=1)
    queries = queries * SCALE
    high = dwt.astype(BF16)
    low = (dwt - high.astype(F32)).astype(BF16)
    for h in range(H):
        at = slice(h * C, (h + 1) * C)
        kv_ref[h, 0:C, :] = kv[at].astype(BF16)
        dq_ref[h] = queries[at].astype(BF16)
        kv_ref[h, C : C + H, :] = jnp.concatenate([high, low, jnp.zeros_like(low)], axis=1)


def pair_kernel(groups, scaled_ref, along_ref, n_ref, wt_ref, out_ref, ones_ref, diag_ref):
    first = (pl.program_id(0) == 0) & (pl.program_id(1) == 0)

    @pl.when(first)
    def _():
        ones_ref[...] = block_diagonal(jnp.ones((128, CP), F32), H).astype(BF16)
        wt = wt_ref[...].astype(F32)
        wt = wt - jnp.mean(wt, axis=1, keepdims=True)
        diag_ref[...] = block_diagonal(jnp.concatenate([wt] * I8, axis=0), H).astype(BF16)

    for g in range(groups):
        back = dot(scaled_ref[0, g], diag_ref[...])
        along = dot(along_ref[0, g], ones_ref[...])
        grad = (back - n_ref[0, g].astype(F32) * along).astype(BF16)
        for i in range(I8):
            out_ref[0, g * I8 + i] = grad[:, i * CP : (i + 1) * CP]


def keys_out_kernel(got_ref, dq_ref, key_ref, value_ref, send_ref):
    total = jnp.sum(got_ref[:, 0:C, :].astype(F32), axis=0)
    for b in range(B):
        key_ref[b] = total[:, b * T : (b + 1) * T]
        value_ref[b] = total[:, (B + b) * T : (B + b + 1) * T]
    parts = got_ref[:, C : C + H, 0 : 2 * CP].astype(F32)
    dwt = jnp.sum(parts[:, :, :CP] + parts[:, :, CP:], axis=0)
    high = dwt.astype(BF16)
    low = (dwt - high.astype(F32)).astype(BF16)
    both = jnp.concatenate([high, low], axis=1)
    for h in range(H):
        send_ref[h, 0:C, 0 : 2 * T] = dq_ref[h]
        send_ref[h, C : C + H, :] = both


def queries_out_kernel(got_ref, query_ref, dwt_ref):
    total = jnp.sum(got_ref[:, 0:C, 0 : 2 * T].astype(F32), axis=0)
    for b in range(B):
        query_ref[b] = total[:, b * T : (b + 1) * T]
    parts = got_ref[:, C : C + H, :].astype(F32)
    dwt_ref[...] = jnp.sum(parts[:, :, :CP] + parts[:, :, CP:], axis=0)


def call(kernel, outs, limit, flops=0, moved=0, **kw):
    return pl.pallas_call(
        kernel,
        out_shape=[jax.ShapeDtypeStruct(s, d) for s, d in outs],
        compiler_params=pltpu.CompilerParams(vmem_limit_bytes=limit << 20),
        cost_estimate=pl.CostEstimate(flops=flops, bytes_accessed=moved, transcendentals=0),
        **kw,
    )


def expand(query, grad):
    shape = ((B, HC, QH), BF16)
    return call(expand_kernel, [shape, shape], 24, flops=400_000_000, moved=5_000_000)(query, grad)


def norm(pair, wt):
    groups = 3
    spec = lambda *tail: pl.BlockSpec((1, groups, T) + tail, lambda b, s: (b, s, 0, 0))
    return call(
        lambda *refs: norm_kernel(groups, *refs),
        [((B, G, T, WIDE), BF16), ((B, G, T, 128), F32), ((B, G, T, 128), F32)],
        32,
        flops=4_000_000_000,
        moved=12_000_000,
        grid=(B, G // groups),
        in_specs=[
            pl.BlockSpec((1, groups * I8, T, CP), lambda b, s: (b, s, 0, 0)),
            pl.BlockSpec((H, CP), lambda b, s: (0, 0)),
        ],
        out_specs=[spec(WIDE), spec(128), spec(128)],
        scratch_shapes=[pltpu.VMEM((256, 256), BF16), pltpu.VMEM((128, WIDE), BF16)],
    )(pair, wt)


def logits(k, v, qt, gt, bias):
    big = ((B, G, T, 128), F32)
    return call(
        logits_kernel, [big, big, ((PEERS, 4 * G, 128), F32)], 32, flops=1_000_000_000, moved=8_000_000
    )(k, v, qt, gt, bias)


def grads(*args):
    return call(
        grads_kernel,
        [
            ((B, G, T, 128), BF16),
            ((B, G, T, 128), BF16),
            ((PEERS, C + H, 4 * T), BF16),
            ((PEERS, C, 2 * T), BF16),
            ((H, CP), F32),
        ],
        48,
        flops=4_000_000_000,
        moved=16_000_000,
        scratch_shapes=[pltpu.VMEM((B, T, QH), BF16), pltpu.VMEM((B, T, QH), BF16)],
    )(*args)


def pair_grad(scaled, along, n, wt):
    groups = 3
    spec = lambda *tail: pl.BlockSpec((1, groups, T) + tail, lambda b, s: (b, s, 0, 0))
    return call(
        lambda *refs: pair_kernel(groups, *refs),
        [((B, T, T, CP), BF16)],
        32,
        flops=4_000_000_000,
        moved=10_000_000,
        grid=(B, G // groups),
        in_specs=[spec(128), spec(128), spec(WIDE), pl.BlockSpec((H, CP), lambda b, s: (0, 0))],
        out_specs=[pl.BlockSpec((1, groups * I8, T, CP), lambda b, s: (b, s, 0, 0))],
        scratch_shapes=[pltpu.VMEM((128, WIDE), BF16), pltpu.VMEM((128, WIDE), BF16)],
    )(scaled, along, n, wt)[0]


def keys_out(got, dq):
    half = ((B, C, T), F32)
    return call(keys_out_kernel, [half, half, ((PEERS, C + H, 2 * CP), BF16)], 16)(got, dq)


def queries_out(got):
    return call(queries_out_kernel, [((B, C, T), F32), ((H, CP), F32)], 16)(got)


def key_route():
    pairs = []
    for row in range(PEERS):
        for col in range(PEERS):
            z, y_lo, core = row >> 1, row & 1, col & 1
            spot = (z - 2 * (col >> 1)) % 8
            pairs.append((col * PEERS + spot * 2 + y_lo, row * PEERS + col))
    return pairs


def spread_over(x, axis):
    return lax.all_to_all(x, axis, 0, 0, tiled=True)


def shards(query_in, key_in, value_in, pair, bias_weight, d_out):
    route = key_route()
    k = lax.ppermute(key_in, ("row", "col"), route)
    v = lax.ppermute(value_in, ("row", "col"), route)
    wt = bias_weight.T
    qt, gt = expand(query_in, d_out)
    n, bias, inv = norm(pair, wt)
    scores, dw, stats = logits(k, v, qt, gt, bias)
    stats = spread_over(stats, "col")
    scaled, along, kv, dq, _ = grads(stats, scores, dw, bias, inv, n, qt, gt, k)
    kv = spread_over(kv, "row")
    d_pair = pair_grad(scaled, along, n, wt)
    d_key, d_value, send = keys_out(kv, dq)
    d_query, dwt = queries_out(spread_over(send, "col"))
    flip = lambda x: jnp.swapaxes(x, 1, 2)
    return flip(d_query), flip(d_key), flip(d_value), d_pair, dwt.T


def solution(mesh):
    rows = P(None, "row", None)
    tiles = P(None, "row", "col", None)
    in_specs = (rows, rows, rows, tiles, P(), rows)
    swapped = P(None, "col", "row")
    out_specs = (P(None, "row", "col"), swapped, swapped, tiles, P())
    return jax.shard_map(shards, mesh=mesh, in_specs=in_specs, out_specs=out_specs, check_vma=False)
```

time: 546 us -> 100 us (0.18)
  the two profiles are of different devices: /device:TPU:16 before, /device:TPU:1 now
where the time goes in v1:
time: 100 us; the launch traced here: 99.7 us
  blocking collectives  46.1 us (46%)
  Pallas kernels  30.3 us (30%)
  starting transfers between devices  12.6 us (13%)
  local copies, waits for them, and re-layouts  8.51 us (9%)
  waiting for transfers between devices  1.37 us (1%)
    all_to_all x2, blocking collectives, spread_over(): return lax.all_to_all(x, axis, 0, 0, tiled=True)  46.1 us
    pallas_call x1, Pallas kernels, norm(): call(lambda *refs: norm_kernel(groups, *refs), [((B, G, T, WIDE), BF16),...  11.4 us
    pallas_call x1, Pallas kernels, grads(): call(grads_kernel, [((B, G, T, 128), BF16), ((B, G, T, 128), BF16), ((PEE...  8.99 us
    unnamed x20, local copies, waits for them, and re-layouts  8.51 us
    all_to_all x1, starting transfers between devices, spread_over(): return lax.all_to_all(x, axis, 0, 0, tiled=True)  6.07 us
    pallas_call x1, Pallas kernels, pair_grad(): call(lambda *refs: pair_kernel(groups, *refs), [((B, T, T, CP), BF16)], 3...  5.81 us
    ppermute x1, starting transfers between devices, shards(): k = lax.ppermute(key_in, ('row', 'col'), route)  4.59 us
  transfers between devices with their start and end apart: 3, of which 1 were waited for; matrix products, arithmetic and copies ran while one was open for 0% of the time, Pallas kernels for 19%

profile of v1, /device:TPU:1, one launch (start us, length us, event | category | flops | bytes accessed | tf_op | source)
XLA Modules:
  0.0 99.7 jit_solution(9022940077443463869)
XLA Ops:
  0.6 4.6 %collective-permute-start = (bf16[2,96,384]{2,1,0:T(8,128)(2,1)}, bf16[2,96,384]{2,1,0:T(8,128)(2,1)S(1)}, u32[]{:S(2)}, u32[]{:S(2)}) collective-permute-start(bf16[2,96,384]{2,1,0:T(8,128)(2,1)} %param.7), channel_id=1, source_target_pairs={{0,0},{16,1},{44,2},{60,3},{72,4},{88,5},{100,6},{116,7},{128,8},{... | collective-permute-start | bytes 442376 | tf_op jit(solution)/shard_map/ppermute | solution.py:317
  5.2 1.9 %collective-permute-start.1 = (bf16[2,96,384]{2,1,0:T(8,128)(2,1)}, bf16[2,96,384]{2,1,0:T(8,128)(2,1)S(1)}, u32[]{:S(2)}, u32[]{:S(2)}) collective-permute-start(bf16[2,96,384]{2,1,0:T(8,128)(2,1)} %param.8), channel_id=1, source_target_pairs={{0,0},{16,1},{44,2},{60,3},{72,4},{88,5},{100,6},{116,7},{128,8},{... | collective-permute-start | bytes 442376 | tf_op jit(solution)/shard_map/ppermute | solution.py:318
  7.2 0.0 copy-start.2
  7.2 2.3 %copy-done.2 = bf16[2,96,96,128]{3,2,1,0:T(8,128)(2,1)S(1)} copy-done((bf16[2,96,96,128]{3,2,1,0:T(8,128)(2,1)S(1)}, bf16[2,96,96,128]{3,2,1,0:T(8,128)(2,1)}, u32[]{:S(2)}) %copy-start.2) | copy-done | bytes 4718616
  9.5 0.0 copy-start.5
  9.5 0.7 copy-done.5
  10.2 0.0 copy-start.3
  10.2 0.0 copy-start.4
  10.2 11.4 %shard_map.102 = (bf16[2,12,96,1024]{3,2,1,0:T(8,128)(2,1)S(1)}, f32[2,12,96,128]{3,2,1,0:T(8,128)S(1)}, f32[2,12,96,128]{3,2,1,0:T(8,128)S(1)}) custom-call(bf16[2,96,96,128]{3,2,1,0:T(8,128)(2,1)S(1)} %copy-done.2, bf16[16,128]{1,0:T(8,128)(2,1)S(1)} %bitcast.5), custom_call_target="tpu_custom_call" | custom-call | flops 4000000000 | bytes 12000000 | tf_op jit(solution)/shard_map/pallas_call | solution.py:236
  21.6 0.0 copy-start.7
  21.6 2.2 %copy-done.7 = bf16[2,12,96,1024]{3,2,1,0:T(8,128)(2,1)} copy-done((bf16[2,12,96,1024]{3,2,1,0:T(8,128)(2,1)}, bf16[2,12,96,1024]{3,2,1,0:T(8,128)(2,1)S(1)}, u32[]{:S(2)}) %copy-start.7) | copy-done | bytes 4718616
  23.8 0.0 copy-done.3
  23.8 0.0 copy-done.4
  23.8 0.0 copy-start.9
  23.8 1.4 %shard_map.101 = (bf16[2,384,1536]{2,1,0:T(8,128)(2,1)S(1)}, bf16[2,384,1536]{2,1,0:T(8,128)(2,1)S(1)}) custom-call(bf16[2,96,384]{2,1,0:T(8,128)(2,1)S(1)} %copy-done.3, bf16[2,96,384]{2,1,0:T(8,128)(2,1)S(1)} %copy-done.4), custom_call_target="tpu_custom_call" | custom-call | flops 400000000 | bytes 5000000 | tf_op jit(solution)/shard_map/pallas_call | solution.py:230
  25.3 0.0 copy-start
  25.3 0.0 copy-start.1
  25.3 0.0 collective-permute-done.k_ref
  25.3 0.0 collective-permute-done.1.v_ref
  25.3 1.1 %shard_map.103 = (f32[2,12,96,128]{3,2,1,0:T(8,128)S(1)}, f32[2,12,96,128]{3,2,1,0:T(8,128)S(1)}, f32[16,48,128]{2,1,0:T(8,128)S(1)}) custom-call(bf16[2,96,384]{2,1,0:T(8,128)(2,1)S(1)} %collective-permute-done.k_ref, bf16[2,96,384]{2,1,0:T(8,128)(2,1)S(1)} %collective-permute-done.1.v_ref, bf16[2,384,1536]{2,1,0:T(8,128)(2,1)S(1)} %get-tuple-element.22.qt_ref, ...), custom_call_target="tpu_custom_call" | custom-call | flops 1000000000 | bytes 8000000 | tf_op jit(solution)/shard_map/pallas_call | solution.py:254
  26.4 0.0 copy-done.9
  26.4 0.3 copy-done
  26.7 0.7 copy-done.1
  27.4 27.3 %all_to_all.15.stats_ref = f32[16,48,128]{2,1,0:T(8,128)S(1)} all-to-all(f32[16,48,128]{2,1,0:T(8,128)S(1)} %get-tuple-element.25), channel_id=1, replica_groups=mesh['row'=16,'col'=16] {'col'}, dimensions={0} | all-to-all | bytes 786432 | tf_op jit(solution)/shard_map/all_to_all | solution.py:312
  54.6 0.0 copy-start.6
  54.6 9.0 %shard_map.104 = (bf16[2,12,96,128]{3,2,1,0:T(8,128)(2,1)S(1)}, bf16[2,12,96,128]{3,2,1,0:T(8,128)(2,1)S(1)}, bf16[16,40,384]{2,1,0:T(8,128)(2,1)S(1)}, bf16[16,24,192]{2,1,0:T(8,128)(2,1)S(1)}, f32[16,128]{1,0:T(8,128)}) custom-call(f32[16,48,128]{2,1,0:T(8,128)S(1)} %all_to_all.15.stats_ref, f32[2,12,96,128]{3,2,1,0:T(8,128)S(1)} %get-tuple-element.26.logits_ref, ...), custom_call_target="tpu_custom_call" | custom-call | flops 4000000000 | bytes 16000000 | tf_op jit(solution)/shard_map/pallas_call | solution.py:260
  63.6 18.8 %all_to_all.16.got_ref = bf16[16,40,384]{2,1,0:T(8,128)(2,1)S(1)} all-to-all(bf16[16,40,384]{2,1,0:T(8,128)(2,1)S(1)} %get-tuple-element.30), channel_id=1, replica_groups=mesh['row'=16,'col'=16] {'row'}, dimensions={0} | all-to-all | bytes 983040 | tf_op jit(solution)/shard_map/all_to_all | solution.py:312
  82.5 0.9 shard_map.105
  83.4 6.1 %all-to-all-start.2 = ((bf16[16,40,256]{2,1,0:T(8,128)(2,1)}), bf16[16,40,256]{2,1,0:T(8,128)(2,1)S(1)}, u32[]{:S(2)}, u32[]{:S(2)}) async-start(bf16[16,40,256]{2,1,0:T(8,128)(2,1)} %get-tuple-element.32), calls=%async_computation.2 | async-start | bytes 655360 | tf_op jit(solution)/shard_map/all_to_all | solution.py:312
  89.4 0.0 copy-done.6
  89.4 0.0 copy-start.8
  89.4 2.3 %copy-done.8 = bf16[2,12,96,1024]{3,2,1,0:T(8,128)(2,1)S(1)} copy-done((bf16[2,12,96,1024]{3,2,1,0:T(8,128)(2,1)S(1)}, bf16[2,12,96,1024]{3,2,1,0:T(8,128)(2,1)}, u32[]{:S(2)}) %copy-start.8) | copy-done | bytes 4718616
  91.8 5.8 %shard_map.107 = bf16[2,96,96,128]{3,2,1,0:T(8,128)(2,1)} custom-call(bf16[2,12,96,128]{3,2,1,0:T(8,128)(2,1)S(1)} %get-tuple-element.36.refs_0_, bf16[2,12,96,128]{3,2,1,0:T(8,128)(2,1)S(1)} %get-tuple-element.37.refs_1_, bf16[2,12,96,1024]{3,2,1,0:T(8,128)(2,1)S(1)} %copy-done.8, bf16[16,128]{1,0:T(8,128)(2,1)S(1)} %bitcast.6), custom_call_target="tpu_custom_call" | custom-call | flops 4000000000 | bytes 10000000 | tf_op jit(solution)/shard_map/pallas_call | solution.py:279
  97.6 1.4 %all-to-all-done.2.got_ref = bf16[16,40,256]{2,1,0:T(8,128)(2,1)S(1)} async-done(((bf16[16,40,256]{2,1,0:T(8,128)(2,1)}), bf16[16,40,256]{2,1,0:T(8,128)(2,1)S(1)}, u32[]{:S(2)}, u32[]{:S(2)}) %all-to-all-start.2) | async-done | bytes 327712 | tf_op jit(solution)/shard_map/all_to_all | solution.py:312
  98.9 0.7 shard_map.106
Async XLA Ops:
  0.6 24.6 %collective-permute-start = (bf16[2,96,384]{2,1,0:T(8,128)(2,1)}, bf16[2,96,384]{2,1,0:T(8,128)(2,1)S(1)}, u32[]{:S(2)}, u32[]{:S(2)}) collective-permute-start(bf16[2,96,384]{2,1,0:T(8,128)(2,1)} %param.7), channel_id=1, source_target_pairs={{0,0},{16,1},{44,2},{60,3},{72,4},{88,5},{100,6},{116,7},{128,8},{... | collective-permute-start | bytes 442376 | tf_op jit(solution)/shard_map/ppermute | solution.py:317
  5.2 20.1 %collective-permute-start.1 = (bf16[2,96,384]{2,1,0:T(8,128)(2,1)}, bf16[2,96,384]{2,1,0:T(8,128)(2,1)S(1)}, u32[]{:S(2)}, u32[]{:S(2)}) collective-permute-start(bf16[2,96,384]{2,1,0:T(8,128)(2,1)} %param.8), channel_id=1, source_target_pairs={{0,0},{16,1},{44,2},{60,3},{72,4},{88,5},{100,6},{116,7},{128,8},{... | collective-permute-start | bytes 442376 | tf_op jit(solution)/shard_map/ppermute | solution.py:318
  7.2 2.3 %copy-start.2 = (bf16[2,96,96,128]{3,2,1,0:T(8,128)(2,1)S(1)}, bf16[2,96,96,128]{3,2,1,0:T(8,128)(2,1)}, u32[]{:S(2)}) copy-start(bf16[2,96,96,128]{3,2,1,0:T(8,128)(2,1)} %refs_0_.1) | copy-start | bytes 14155780
  9.5 0.7 copy-start.5
  10.2 13.6 %copy-start.3 = (bf16[2,96,384]{2,1,0:T(8,128)(2,1)S(1)}, bf16[2,96,384]{2,1,0:T(8,128)(2,1)}, u32[]{:S(2)}) copy-start(bf16[2,96,384]{2,1,0:T(8,128)(2,1)} %q_ref.1) | copy-start | bytes 442372
  10.2 13.6 %copy-start.4 = (bf16[2,96,384]{2,1,0:T(8,128)(2,1)S(1)}, bf16[2,96,384]{2,1,0:T(8,128)(2,1)}, u32[]{:S(2)}) copy-start(bf16[2,96,384]{2,1,0:T(8,128)(2,1)} %g_ref.1) | copy-start | bytes 442372
  21.6 2.2 %copy-start.7 = (bf16[2,12,96,1024]{3,2,1,0:T(8,128)(2,1)}, bf16[2,12,96,1024]{3,2,1,0:T(8,128)(2,1)S(1)}, u32[]{:S(2)}) copy-start(bf16[2,12,96,1024]{3,2,1,0:T(8,128)(2,1)S(1)} %get-tuple-element.29.n_ref.refs_2_) | copy-start | bytes 14155780
  23.8 2.6 %copy-start.9 = (f32[2,12,96,128]{3,2,1,0:T(8,128)}, f32[2,12,96,128]{3,2,1,0:T(8,128)S(1)}, u32[]{:S(2)}) copy-start(f32[2,12,96,128]{3,2,1,0:T(8,128)S(1)} %get-tuple-element.28.inv_ref) | copy-start | bytes 3538948
  25.3 1.4 %copy-start = (bf16[2,384,1536]{2,1,0:T(8,128)(2,1)}, bf16[2,384,1536]{2,1,0:T(8,128)(2,1)S(1)}, u32[]{:S(2)}) copy-start(bf16[2,384,1536]{2,1,0:T(8,128)(2,1)S(1)} %get-tuple-element.22.qt_ref) | copy-start | bytes 7077892
  25.3 2.1 %copy-start.1 = (bf16[2,384,1536]{2,1,0:T(8,128)(2,1)}, bf16[2,384,1536]{2,1,0:T(8,128)(2,1)S(1)}, u32[]{:S(2)}) copy-start(bf16[2,384,1536]{2,1,0:T(8,128)(2,1)S(1)} %get-tuple-element.23.gt_ref) | copy-start | bytes 7077892
  54.6 34.8 %copy-start.6 = (bf16[128,16]{0,1:T(8,128)(2,1)S(1)}, bf16[128,16]{0,1:T(8,128)(2,1)}, u32[]{:S(2)}) copy-start(bf16[128,16]{0,1:T(8,128)(2,1)} %param.10) | copy-start | bytes 12292
  83.4 15.6 %all-to-all-start.2 = ((bf16[16,40,256]{2,1,0:T(8,128)(2,1)}), bf16[16,40,256]{2,1,0:T(8,128)(2,1)S(1)}, u32[]{:S(2)}, u32[]{:S(2)}) async-start(bf16[16,40,256]{2,1,0:T(8,128)(2,1)} %get-tuple-element.32), calls=%async_computation.2 | async-start | bytes 655360 | tf_op jit(solution)/shard_map/all_to_all | solution.py:312
  89.4 2.3 %copy-start.8 = (bf16[2,12,96,1024]{3,2,1,0:T(8,128)(2,1)S(1)}, bf16[2,12,96,1024]{3,2,1,0:T(8,128)(2,1)}, u32[]{:S(2)}) copy-start(bf16[2,12,96,1024]{3,2,1,0:T(8,128)(2,1)} %copy-done.7) | copy-start | bytes 14155780

commit v2 on v1

v2 whole, which is shorter than its diff:
```python
import math

import jax
import jax.numpy as jnp
from jax import lax
from jax.experimental import pallas as pl
from jax.experimental.pallas import tpu as pltpu
from jax.sharding import PartitionSpec as P

EPS = 1e-05
F32 = jnp.float32
BF16 = jnp.bfloat16

B = 2
H = 16
C = 24
HC = H * C
CP = 128
T = 96
G = 12
I8 = 8
WIDE = I8 * CP
QH = T * H
SCALE = 1.0 / math.sqrt(C)
PEERS = 16
GROUPS = 6

NN = (((1,), (0,)), ((), ()))
NT = (((1,), (1,)), ((), ()))
TN = (((0,), (0,)), ((), ()))


def dot(left, right, dims=NN):
    return lax.dot_general(left, right, dims, preferred_element_type=F32)


def iota(shape, dim):
    return lax.broadcasted_iota(jnp.int32, shape, dim)


def head_mask():
    row_head = (iota((HC, 128), 0) * 171) >> 12
    return row_head == (iota((HC, 128), 1) & (H - 1))


def query_lanes(rows, first):
    return jnp.where(iota((rows, QH), 0) - first == (iota((rows, QH), 1) >> 4), 1.0, 0.0).astype(BF16)


def block_diagonal(tile, rows_per_block):
    row_block = iota((128, CP), 0) // rows_per_block
    zero = jnp.zeros_like(tile)
    return jnp.concatenate([jnp.where(row_block == i, tile, zero) for i in range(I8)], axis=1)


def expand(source, target):
    lanes = query_lanes(T, 0)
    mask = head_mask()
    for b in range(B):
        spread = dot(source[b], lanes, TN)
        for g in range(G):
            at = slice(g * 128, (g + 1) * 128)
            target[b, :, at] = jnp.where(mask, spread[:, at], 0.0).astype(BF16)


def expand_kernel(q_ref, g_ref, qt_ref, gt_ref):
    expand(q_ref, qt_ref)
    expand(g_ref, gt_ref)


def norm_kernel(groups, pair_ref, wt_ref, n_ref, bias_ref, inv_ref, ones_ref, diag_ref):
    first = (pl.program_id(0) == 0) & (pl.program_id(1) == 0)

    @pl.when(first)
    def _():
        same = (iota((256, 256), 0) >> 7) == (iota((256, 256), 1) >> 7)
        ones_ref[...] = jnp.where(same, 1.0 / CP, 0.0).astype(BF16)
        wt = wt_ref[...].astype(F32)
        diag_ref[...] = block_diagonal(jnp.concatenate([wt] * I8, axis=0), H).astype(BF16)

    ones = ones_ref[...]
    rows = groups * T
    lane_query = iota((rows, 128), 1) >> 4
    compact = jnp.zeros((rows, 128), F32)
    bias = jnp.zeros((rows, 128), F32)
    for p in range(I8 // 2):
        x = jnp.concatenate(
            [
                jnp.concatenate([pair_ref[0, g * I8 + 2 * p], pair_ref[0, g * I8 + 2 * p + 1]], axis=1)
                for g in range(groups)
            ],
            axis=0,
        )
        centred = x.astype(F32) - dot(x, ones)
        spread = dot((centred * centred).astype(BF16), ones)
        inverse = lax.rsqrt(spread + EPS)
        normed = (centred * inverse).astype(BF16)
        n_ref[0, :, :, p * 256 : (p + 1) * 256] = normed.reshape(groups, T, 256)
        for k in range(2):
            compact = jnp.where(
                lane_query == 2 * p + k, inverse[:, k * CP : (k + 1) * CP], compact
            )
        bias = bias + dot(normed, diag_ref[:, p * 256 : (p + 1) * 256], NT)
    inv_ref[0] = compact.reshape(groups, T, 128)
    bias_ref[0] = bias.reshape(groups, T, 128)


def logits_kernel(k_ref, v_ref, qt_ref, gt_ref, bias_ref, logits_ref, dw_ref, stats_ref):
    for b in range(B):
        scores = dot(k_ref[b], qt_ref[b])
        inner = dot(v_ref[b], gt_ref[b])
        for g in range(G):
            at = slice(g * 128, (g + 1) * 128)
            logits = scores[:, at] * SCALE + bias_ref[b, g]
            dw = inner[:, at]
            logits_ref[b, g] = logits
            dw_ref[b, g] = dw
            top = jnp.max(logits, axis=0, keepdims=True)
            expo = jnp.exp(logits - top)
            total = jnp.sum(expo, axis=0, keepdims=True)
            level = top + jnp.log(total)
            balance = jnp.sum(expo * dw, axis=0, keepdims=True) / total
            row = b * 2 * G + g
            stats_ref[:, row : row + 1, :] = jnp.broadcast_to(level[None], (PEERS, 1, 128))
            stats_ref[:, row + G : row + G + 1, :] = jnp.broadcast_to(balance[None], (PEERS, 1, 128))


def split_halves(x):
    high = x.astype(BF16)
    low = (x - high.astype(F32)).astype(BF16)
    return jnp.concatenate([high, low], axis=1)


def join_halves(parts):
    parts = parts.astype(F32)
    return jnp.sum(parts[:, :, :CP] + parts[:, :, CP:], axis=0)


def scores_kernel(
    stats_ref, logits_ref, dw_ref, bias_ref, inv_ref, k_ref, n_ref,
    ds_ref, w_ref, scaled_ref, along_ref, send_ref, n_here, n_sem,
):
    fetch = pltpu.make_async_copy(n_ref, n_here, n_sem)
    fetch.start()
    for b in range(B):
        levels = stats_ref[:, b * 2 * G : b * 2 * G + G, :]
        balances = stats_ref[:, b * 2 * G + G : (b + 1) * 2 * G, :]
        top = jnp.max(levels, axis=0)
        parts = jnp.exp(levels - top[None])
        total = jnp.sum(parts, axis=0)
        level = top + jnp.log(total)
        balance = jnp.sum(parts * balances, axis=0) / total
        for g in range(G):
            weights = jnp.exp(logits_ref[b, g] - level[g : g + 1])
            ds = weights * (dw_ref[b, g] - balance[g : g + 1])
            low = ds.astype(BF16)
            at = slice(g * 128, (g + 1) * 128)
            ds_ref[b, :, at] = low
            w_ref[b, :, at] = weights.astype(BF16)
            scaled = low.astype(F32) * inv_ref[b, g]
            scaled_ref[b, g] = scaled.astype(BF16)
            along_ref[b, g] = (scaled * bias_ref[b, g] * (1.0 / CP)).astype(BF16)

    mask = head_mask()
    queries = jnp.zeros((HC, 2 * T), F32)
    for b in range(B):
        spread = dot(k_ref[b], ds_ref[b], TN)
        chosen = jnp.concatenate(
            [
                jnp.where(mask, spread[:, g * 128 : (g + 1) * 128], 0.0).astype(BF16)
                for g in range(G)
            ],
            axis=1,
        )
        queries = queries + dot(chosen, query_lanes(2 * T, b * T), NT)
    queries = queries * SCALE

    fetch.wait()
    total = jnp.zeros((128, WIDE), F32)
    for b in range(B):
        left = jnp.concatenate([ds_ref[b, :, g * 128 : (g + 1) * 128] for g in range(G)], axis=0)
        total = total + dot(left, n_here[b].reshape(G * T, WIDE), TN)
    dwt = jnp.zeros((H, CP), F32)
    for i in range(I8):
        dwt = dwt + total[i * H : (i + 1) * H, i * CP : (i + 1) * CP]
    both = split_halves(dwt)
    for h in range(H):
        send_ref[h, 0:C, 0 : 2 * T] = queries[h * C : (h + 1) * C].astype(BF16)
        send_ref[h, C : C + H, :] = both


def grads_kernel(ds_ref, w_ref, q_ref, g_ref, kv_ref, qt_ref, gt_ref):
    expand(q_ref, qt_ref)
    expand(g_ref, gt_ref)
    keys = [dot(qt_ref[b], ds_ref[b], NT) * SCALE for b in range(B)]
    values = [dot(gt_ref[b], w_ref[b], NT) for b in range(B)]
    kv = jnp.concatenate(keys + values, axis=1)
    for h in range(H):
        kv_ref[h] = kv[h * C : (h + 1) * C].astype(BF16)


def pair_kernel(groups, scaled_ref, along_ref, n_ref, wt_ref, out_ref, ones_ref, diag_ref):
    first = (pl.program_id(0) == 0) & (pl.program_id(1) == 0)

    @pl.when(first)
    def _():
        ones_ref[...] = block_diagonal(jnp.ones((128, CP), F32), H).astype(BF16)
        wt = wt_ref[...].astype(F32)
        wt = wt - jnp.mean(wt, axis=1, keepdims=True)
        diag_ref[...] = block_diagonal(jnp.concatenate([wt] * I8, axis=0), H).astype(BF16)

    rows = groups * T
    scaled = scaled_ref[0].reshape(rows, 128)
    along = along_ref[0].reshape(rows, 128)
    for p in range(I8 // 2):
        at = slice(p * 256, (p + 1) * 256)
        back = dot(scaled, diag_ref[:, at])
        normed = n_ref[0, :, :, at].reshape(rows, 256).astype(F32)
        grad = (back - normed * dot(along, ones_ref[:, at])).astype(BF16)
        for g in range(groups):
            for k in range(2):
                out_ref[0, g * I8 + 2 * p + k] = grad[g * T : (g + 1) * T, k * CP : (k + 1) * CP]


def queries_out_kernel(got_ref, kv_ref, query_ref, send_ref):
    total = jnp.sum(got_ref[:, 0:C, 0 : 2 * T].astype(F32), axis=0)
    for b in range(B):
        query_ref[b] = total[:, b * T : (b + 1) * T]
    both = split_halves(join_halves(got_ref[:, C : C + H, :]))
    for h in range(H):
        send_ref[h, 0:C, :] = kv_ref[h]
        send_ref[h, C : C + H, 0 : 2 * CP] = both


def keys_out_kernel(got_ref, key_ref, value_ref, dwt_ref):
    total = jnp.sum(got_ref[:, 0:C, :].astype(F32), axis=0)
    for b in range(B):
        key_ref[b] = total[:, b * T : (b + 1) * T]
        value_ref[b] = total[:, (B + b) * T : (B + b + 1) * T]
    dwt_ref[...] = join_halves(got_ref[:, C : C + H, 0 : 2 * CP])


def call(kernel, outs, limit, flops=0, moved=0, **kw):
    return pl.pallas_call(
        kernel,
        out_shape=outs,
        compiler_params=pltpu.CompilerParams(vmem_limit_bytes=limit << 20),
        cost_estimate=pl.CostEstimate(flops=flops, bytes_accessed=moved, transcendentals=0),
        **kw,
    )


def f32(*shape):
    return jax.ShapeDtypeStruct(shape, F32)


def bf16(*shape):
    return jax.ShapeDtypeStruct(shape, BF16)


def far(*shape):
    return pltpu.HBM(shape, BF16)


def in_hbm(x):
    return pltpu.with_memory_space_constraint(x, pltpu.HBM)


def expanded(query, grad):
    shape = bf16(B, HC, QH)
    return call(expand_kernel, [shape, shape], 16, flops=400_000_000, moved=5_000_000)(query, grad)


def norm(pair, wt):
    groups = GROUPS
    spec = lambda *tail: pl.BlockSpec((1, groups, T) + tail, lambda b, s: (b, s, 0, 0))
    return call(
        lambda *refs: norm_kernel(groups, *refs),
        [far(B, G, T, WIDE), f32(B, G, T, 128), f32(B, G, T, 128)],
        24,
        flops=4_000_000_000,
        moved=12_000_000,
        grid=(B, G // groups),
        in_specs=[
            pl.BlockSpec((1, groups * I8, T, CP), lambda b, s: (b, s, 0, 0)),
            pl.BlockSpec((H, CP), lambda b, s: (0, 0)),
        ],
        out_specs=[spec(WIDE), spec(128), spec(128)],
        scratch_shapes=[pltpu.VMEM((256, 256), BF16), pltpu.VMEM((128, WIDE), BF16)],
    )(in_hbm(pair), wt)


def logits(k, v, qt, gt, bias):
    big = f32(B, G, T, 128)
    return call(
        logits_kernel, [big, big, f32(PEERS, 4 * G, 128)], 16, flops=1_000_000_000, moved=8_000_000
    )(k, v, qt, gt, bias)


def scores(*args):
    low = far(B, T, QH)
    cell = far(B, G, T, 128)
    whole = pl.BlockSpec(memory_space=pltpu.VMEM)
    return call(
        scores_kernel,
        [low, low, cell, cell, bf16(PEERS, C + H, 2 * CP)],
        24,
        flops=2_500_000_000,
        moved=8_000_000,
        in_specs=[whole] * 6 + [pl.BlockSpec(memory_space=pltpu.HBM)],
        out_specs=[whole] * 5,
        scratch_shapes=[pltpu.VMEM((B, G, T, WIDE), BF16), pltpu.SemaphoreType.DMA],
    )(*args)


def grads(*args):
    wide = pltpu.VMEM((B, HC, QH), BF16)
    return call(
        grads_kernel,
        [bf16(PEERS, C, 4 * T)],
        24,
        flops=2_500_000_000,
        moved=8_000_000,
        scratch_shapes=[wide, wide],
    )(*[in_hbm(x) for x in args])[0]


def pair_grad(scaled, along, n, wt):
    groups = GROUPS
    spec = lambda *tail: pl.BlockSpec((1, groups, T) + tail, lambda b, s: (b, s, 0, 0))
    return call(
        lambda *refs: pair_kernel(groups, *refs),
        [bf16(B, T, T, CP)],
        24,
        flops=4_000_000_000,
        moved=10_000_000,
        grid=(B, G // groups),
        in_specs=[spec(128), spec(128), spec(WIDE), pl.BlockSpec((H, CP), lambda b, s: (0, 0))],
        out_specs=[pl.BlockSpec((1, groups * I8, T, CP), lambda b, s: (b, s, 0, 0))],
        scratch_shapes=[pltpu.VMEM((128, WIDE), BF16), pltpu.VMEM((128, WIDE), BF16)],
    )(in_hbm(scaled), in_hbm(along), in_hbm(n), wt)[0]


def queries_out(got, kv):
    return call(queries_out_kernel, [f32(B, C, T), bf16(PEERS, C + H, 4 * T)], 16)(got, kv)


def keys_out(got):
    half = f32(B, C, T)
    return call(keys_out_kernel, [half, half, f32(H, CP)], 16)(got)


def ring_gap(size, a, b):
    return min((a - b) % size, (b - a) % size)


def hops(source, target):
    def place(index):
        row, col = divmod(index, PEERS)
        return row >> 1, col >> 2, (col >> 1 & 1) * 2 + (row & 1)

    (z, x, y), (z2, x2, y2) = place(source), place(target)
    return ring_gap(8, z, z2) + ring_gap(4, x, x2) + ring_gap(4, y, y2)


def key_route():
    pairs = []
    for col in range(PEERS):
        sources = [col * PEERS + k for k in range(PEERS)]
        targets = [row * PEERS + col for row in range(PEERS)]
        cost = [[hops(s, t) ** 3 for t in targets] for s in sources]
        chosen = list(range(PEERS))
        better = True
        while better:
            better = False
            for i in range(PEERS):
                for j in range(i):
                    now = cost[i][chosen[i]] + cost[j][chosen[j]]
                    then = cost[i][chosen[j]] + cost[j][chosen[i]]
                    if then < now:
                        chosen[i], chosen[j] = chosen[j], chosen[i]
                        better = True
        pairs += [(sources[i], targets[chosen[i]]) for i in range(PEERS)]
    return pairs


def spread_over(x, axis):
    return lax.all_to_all(x, axis, 0, 0, tiled=True)


def shards(query_in, key_in, value_in, pair, bias_weight, d_out):
    route = key_route()
    k = lax.ppermute(key_in, ("row", "col"), route)
    v = lax.ppermute(value_in, ("row", "col"), route)
    wt = bias_weight.T
    qt, gt = expanded(query_in, d_out)
    n, bias, inv = norm(pair, wt)
    scaled_scores, dw, stats = logits(k, v, qt, gt, bias)
    stats = spread_over(stats, "col")
    ds, w, scaled, along, send = scores(stats, scaled_scores, dw, bias, inv, k, n)
    got = spread_over(send, "col")
    kv = grads(ds, w, query_in, d_out)
    d_query, send = queries_out(got, kv)
    got = spread_over(send, "row")
    d_pair = pair_grad(scaled, along, n, wt)
    d_key, d_value, dwt = keys_out(got)
    flip = lambda x: jnp.swapaxes(x, 1, 2)
    return flip(d_query), flip(d_key), flip(d_value), d_pair, dwt.T


def solution(mesh):
    rows = P(None, "row", None)
    tiles = P(None, "row", "col", None)
    in_specs = (rows, rows, rows, tiles, P(), rows)
    swapped = P(None, "col", "row")
    out_specs = (P(None, "row", "col"), swapped, swapped, tiles, P())
    return jax.shard_map(shards, mesh=mesh, in_specs=in_specs, out_specs=out_specs, check_vma=False)
```

time: 100 us -> 85.4 us (0.85)
  the two profiles are of different devices: /device:TPU:1 before, /device:TPU:16 now
where the time goes in v2:
time: 85.4 us; the launch traced here: 84.4 us
  Pallas kernels  28.1 us (33%)
  starting transfers between devices  26.8 us (31%)
  blocking collectives  14.4 us (17%)
  waiting for transfers between devices  13.6 us (16%)
    all_to_all x2, starting transfers between devices, spread_over(): return lax.all_to_all(x, axis, 0, 0, tiled=True)  16.7 us
    all_to_all x1, blocking collectives, spread_over(): return lax.all_to_all(x, axis, 0, 0, tiled=True)  14.4 us
    all_to_all x2, waiting for transfers between devices, spread_over(): return lax.all_to_all(x, axis, 0, 0, tiled=True)  13.6 us
    pallas_call x1, Pallas kernels, norm(): call(lambda *refs: norm_kernel(groups, *refs), [far(B, G, T, WIDE), f32(B...  7.97 us
    ppermute x1, starting transfers between devices, shards(): k = lax.ppermute(key_in, ('row', 'col'), route)  7.16 us
    pallas_call x1, Pallas kernels, pair_grad(): call(lambda *refs: pair_kernel(groups, *refs), [bf16(B, T, T, CP)], 24, f...  7.04 us
    pallas_call x1, Pallas kernels, scores(): call(scores_kernel, [low, low, cell, cell, bf16(PEERS, C + H, 2 * CP)], 2...  4.93 us
    pallas_call x1, Pallas kernels, grads(): call(grads_kernel, [bf16(PEERS, C, 4 * T)], 24, flops=2500000000, moved=8...  4.03 us
  transfers between devices with their start and end apart: 4, of which 2 were waited for; matrix products, arithmetic and copies ran while one was open for 0% of the time, Pallas kernels for 24%

profile of v2, /device:TPU:16, one launch (start us, length us, event | category | flops | bytes accessed | tf_op | source)
XLA Modules:
  0.0 84.4 jit_solution(18286895892699616020)
XLA Ops:
  0.6 7.2 %collective-permute-start = (bf16[2,96,384]{2,1,0:T(8,128)(2,1)}, bf16[2,96,384]{2,1,0:T(8,128)(2,1)S(1)}, u32[]{:S(2)}, u32[]{:S(2)}) collective-permute-start(bf16[2,96,384]{2,1,0:T(8,128)(2,1)} %param.7), channel_id=1, source_target_pairs={{0,160},{1,128},{2,144},{3,112},{4,96},{5,64},{6,176},{7,80},{8,0}... | collective-permute-start | bytes 442376 | tf_op jit(solution)/shard_map/ppermute | solution.py:393
  7.8 2.9 %collective-permute-start.1 = (bf16[2,96,384]{2,1,0:T(8,128)(2,1)}, bf16[2,96,384]{2,1,0:T(8,128)(2,1)S(1)}, u32[]{:S(2)}, u32[]{:S(2)}) collective-permute-start(bf16[2,96,384]{2,1,0:T(8,128)(2,1)} %param.8), channel_id=1, source_target_pairs={{0,160},{1,128},{2,144},{3,112},{4,96},{5,64},{6,176},{7,80},{8,0}... | collective-permute-start | bytes 442376 | tf_op jit(solution)/shard_map/ppermute | solution.py:394
  10.7 0.0 copy-start.3
  10.7 0.7 copy-done.3
  11.4 0.0 copy-start.1
  11.4 0.0 copy-start.2
  11.4 8.0 %shard_map.102 = (bf16[2,12,96,1024]{3,2,1,0:T(8,128)(2,1)}, f32[2,12,96,128]{3,2,1,0:T(8,128)S(1)}, f32[2,12,96,128]{3,2,1,0:T(8,128)S(1)}) custom-call(bf16[2,96,96,128]{3,2,1,0:T(8,128)(2,1)} %refs_0_.1, bf16[16,128]{1,0:T(8,128)(2,1)S(1)} %bitcast.5), custom_call_target="tpu_custom_call" | custom-call | flops 4000000000 | bytes 12000000 | tf_op jit(solution)/shard_map/pallas_call | solution.py:277
  19.4 0.0 copy-done.1
  19.4 0.0 copy-done.2
  19.4 1.4 %shard_map.101 = (bf16[2,384,1536]{2,1,0:T(8,128)(2,1)S(1)}, bf16[2,384,1536]{2,1,0:T(8,128)(2,1)S(1)}) custom-call(bf16[2,96,384]{2,1,0:T(8,128)(2,1)S(1)} %copy-done.1, bf16[2,96,384]{2,1,0:T(8,128)(2,1)S(1)} %copy-done.2), custom_call_target="tpu_custom_call" | custom-call | flops 400000000 | bytes 5000000 | tf_op jit(solution)/shard_map/pallas_call | solution.py:271
  20.8 0.0 collective-permute-done.k_ref
  20.8 0.0 collective-permute-done.1.v_ref
  20.8 0.0 copy-start
  20.8 1.1 %shard_map.103 = (f32[2,12,96,128]{3,2,1,0:T(8,128)S(1)}, f32[2,12,96,128]{3,2,1,0:T(8,128)S(1)}, f32[16,48,128]{2,1,0:T(8,128)S(1)}) custom-call(bf16[2,96,384]{2,1,0:T(8,128)(2,1)S(1)} %collective-permute-done.k_ref, bf16[2,96,384]{2,1,0:T(8,128)(2,1)S(1)} %collective-permute-done.1.v_ref, bf16[2,384,1536]{2,1,0:T(8,128)(2,1)S(1)} %get-tuple-element.23.qt_ref, ...), custom_call_target="tpu_custom_call" | custom-call | flops 1000000000 | bytes 8000000 | tf_op jit(solution)/shard_map/pallas_call | solution.py:295
  21.9 14.4 %all_to_all.15.stats_ref = f32[16,48,128]{2,1,0:T(8,128)S(1)} all-to-all(f32[16,48,128]{2,1,0:T(8,128)S(1)} %get-tuple-element.26), channel_id=1, replica_groups=mesh['row'=16,'col'=16] {'col'}, dimensions={0} | all-to-all | bytes 786432 | tf_op jit(solution)/shard_map/all_to_all | solution.py:388
  36.3 0.0 copy-done
  36.3 4.9 %shard_map.104 = (bf16[2,96,1536]{2,1,0:T(8,128)(2,1)}, bf16[2,96,1536]{2,1,0:T(8,128)(2,1)}, bf16[2,12,96,128]{3,2,1,0:T(8,128)(2,1)}, bf16[2,12,96,128]{3,2,1,0:T(8,128)(2,1)}, bf16[16,40,256]{2,1,0:T(8,128)(2,1)}) custom-call(f32[16,48,128]{2,1,0:T(8,128)S(1)} %all_to_all.15.stats_ref, f32[2,12,96,128]{3,2,1,0:T(8,128)S(1)} %get-tuple-element.27.logits_ref, ...), custom_call_target="tpu_custom_call" | custom-call | flops 2500000000 | bytes 8000000 | tf_op jit(solution)/shard_map/pallas_call | solution.py:304
  41.3 6.3 %all-to-all-start.1 = ((bf16[16,40,256]{2,1,0:T(8,128)(2,1)}), bf16[16,40,256]{2,1,0:T(8,128)(2,1)S(1)}, u32[]{:S(2)}, u32[]{:S(2)}) async-start(bf16[16,40,256]{2,1,0:T(8,128)(2,1)} %get-tuple-element.31), calls=%async_computation.1 | async-start | bytes 655360 | tf_op jit(solution)/shard_map/all_to_all | solution.py:388
  47.5 0.0 copy-start.4
  47.5 4.0 %shard_map.105.kv_ref = bf16[16,24,384]{2,1,0:T(8,128)(2,1)S(1)} custom-call(bf16[2,96,1536]{2,1,0:T(8,128)(2,1)} %get-tuple-element.32.ds_ref, bf16[2,96,1536]{2,1,0:T(8,128)(2,1)} %get-tuple-element.33.w_ref, bf16[2,96,384]{2,1,0:T(8,128)(2,1)} %q_ref.3, bf16[2,96,384]{2,1,0:T(8,128)(2,1)} %g_ref.3), custom_call_target="tpu_custom_call" | custom-call | flops 2500000000 | bytes 8000000 | tf_op jit(solution)/shard_map/pallas_call | solution.py:318
  51.6 3.2 %all-to-all-done.1.got_ref = bf16[16,40,256]{2,1,0:T(8,128)(2,1)S(1)} async-done(((bf16[16,40,256]{2,1,0:T(8,128)(2,1)}), bf16[16,40,256]{2,1,0:T(8,128)(2,1)S(1)}, u32[]{:S(2)}, u32[]{:S(2)}) %all-to-all-start.1) | async-done | bytes 327712 | tf_op jit(solution)/shard_map/all_to_all | solution.py:388
  54.8 0.9 %shard_map.106 = (f32[2,24,96]{2,1,0:T(8,128)}, bf16[16,40,384]{2,1,0:T(8,128)(2,1)}) custom-call(bf16[16,40,256]{2,1,0:T(8,128)(2,1)S(1)} %all-to-all-done.1.got_ref, bf16[16,24,384]{2,1,0:T(8,128)(2,1)S(1)} %shard_map.105.kv_ref), custom_call_target="tpu_custom_call" | custom-call | tf_op jit(solution)/shard_map/pallas_call | solution.py:345
  55.6 10.5 %all-to-all-start.2 = ((bf16[16,40,384]{2,1,0:T(8,128)(2,1)}), bf16[16,40,384]{2,1,0:T(8,128)(2,1)S(1)}, u32[]{:S(2)}, u32[]{:S(2)}) async-start(bf16[16,40,384]{2,1,0:T(8,128)(2,1)} %get-tuple-element.35), calls=%async_computation.2 | async-start | bytes 983040 | tf_op jit(solution)/shard_map/all_to_all | solution.py:388
  66.1 0.0 copy-done.4
  66.1 7.0 %shard_map.108 = bf16[2,96,96,128]{3,2,1,0:T(8,128)(2,1)} custom-call(bf16[2,12,96,128]{3,2,1,0:T(8,128)(2,1)} %get-tuple-element.38.refs_0_, bf16[2,12,96,128]{3,2,1,0:T(8,128)(2,1)} %get-tuple-element.39.refs_1_, bf16[2,12,96,1024]{3,2,1,0:T(8,128)(2,1)} %get-tuple-element.30.n_ref.refs_2_, bf16[16,128]{1,0:T(8,128)(2,1)S(1)} %bitcast.6), custom_call_target="tpu_custom_call" | custom-call | flops 4000000000 | bytes 10000000 | tf_op jit(solution)/shard_map/pallas_call | solution.py:331
  73.2 10.4 %all-to-all-done.2.got_ref = bf16[16,40,384]{2,1,0:T(8,128)(2,1)S(1)} async-done(((bf16[16,40,384]{2,1,0:T(8,128)(2,1)}), bf16[16,40,384]{2,1,0:T(8,128)(2,1)S(1)}, u32[]{:S(2)}, u32[]{:S(2)}) %all-to-all-start.2) | async-done | bytes 491552 | tf_op jit(solution)/shard_map/all_to_all | solution.py:388
  83.6 0.7 shard_map.107
Async XLA Ops:
  0.6 20.2 %collective-permute-start = (bf16[2,96,384]{2,1,0:T(8,128)(2,1)}, bf16[2,96,384]{2,1,0:T(8,128)(2,1)S(1)}, u32[]{:S(2)}, u32[]{:S(2)}) collective-permute-start(bf16[2,96,384]{2,1,0:T(8,128)(2,1)} %param.7), channel_id=1, source_target_pairs={{0,160},{1,128},{2,144},{3,112},{4,96},{5,64},{6,176},{7,80},{8,0}... | collective-permute-start | bytes 442376 | tf_op jit(solution)/shard_map/ppermute | solution.py:393
  7.8 13.0 %collective-permute-start.1 = (bf16[2,96,384]{2,1,0:T(8,128)(2,1)}, bf16[2,96,384]{2,1,0:T(8,128)(2,1)S(1)}, u32[]{:S(2)}, u32[]{:S(2)}) collective-permute-start(bf16[2,96,384]{2,1,0:T(8,128)(2,1)} %param.8), channel_id=1, source_target_pairs={{0,160},{1,128},{2,144},{3,112},{4,96},{5,64},{6,176},{7,80},{8,0}... | collective-permute-start | bytes 442376 | tf_op jit(solution)/shard_map/ppermute | solution.py:394
  10.7 0.7 copy-start.3
  11.4 8.0 %copy-start.1 = (bf16[2,96,384]{2,1,0:T(8,128)(2,1)S(1)}, bf16[2,96,384]{2,1,0:T(8,128)(2,1)}, u32[]{:S(2)}) copy-start(bf16[2,96,384]{2,1,0:T(8,128)(2,1)} %q_ref.3) | copy-start | bytes 442372
  11.4 8.0 %copy-start.2 = (bf16[2,96,384]{2,1,0:T(8,128)(2,1)S(1)}, bf16[2,96,384]{2,1,0:T(8,128)(2,1)}, u32[]{:S(2)}) copy-start(bf16[2,96,384]{2,1,0:T(8,128)(2,1)} %g_ref.3) | copy-start | bytes 442372
  20.8 15.5 %copy-start = (bf16[2,12,96,1024]{3,2,1,0:T(8,128)(2,1)S(1)}, bf16[2,12,96,1024]{3,2,1,0:T(8,128)(2,1)}, u32[]{:S(2)}) copy-start(bf16[2,12,96,1024]{3,2,1,0:T(8,128)(2,1)} %get-tuple-element.30.n_ref.refs_2_) | copy-start | bytes 14155780
  41.3 13.5 %all-to-all-start.1 = ((bf16[16,40,256]{2,1,0:T(8,128)(2,1)}), bf16[16,40,256]{2,1,0:T(8,128)(2,1)S(1)}, u32[]{:S(2)}, u32[]{:S(2)}) async-start(bf16[16,40,256]{2,1,0:T(8,128)(2,1)} %get-tuple-element.31), calls=%async_computation.1 | async-start | bytes 655360 | tf_op jit(solution)/shard_map/all_to_all | solution.py:388
  47.5 18.6 %copy-start.4 = (bf16[128,16]{0,1:T(8,128)(2,1)S(1)}, bf16[128,16]{0,1:T(8,128)(2,1)}, u32[]{:S(2)}) copy-start(bf16[128,16]{0,1:T(8,128)(2,1)} %param.10) | copy-start | bytes 12292
  55.6 28.0 %all-to-all-start.2 = ((bf16[16,40,384]{2,1,0:T(8,128)(2,1)}), bf16[16,40,384]{2,1,0:T(8,128)(2,1)S(1)}, u32[]{:S(2)}, u32[]{:S(2)}) async-start(bf16[16,40,384]{2,1,0:T(8,128)(2,1)} %get-tuple-element.35), calls=%async_computation.2 | async-start | bytes 983040 | tf_op jit(solution)/shard_map/all_to_all | solution.py:388

commit v3 on v2

--- a/solution.py
+++ b/solution.py
@@ -63,9 +63,11 @@
             target[b, :, at] = jnp.where(mask, spread[:, at], 0.0).astype(BF16)
 
 
-def expand_kernel(q_ref, g_ref, qt_ref, gt_ref):
+def expand_kernel(q_ref, g_ref, qt_ref, gt_ref, pick_ref):
     expand(q_ref, qt_ref)
     expand(g_ref, gt_ref)
+    for b in range(B):
+        pick_ref[:, b * QH : (b + 1) * QH] = query_lanes(B * T, b * T)
 
 
 def norm_kernel(groups, pair_ref, wt_ref, n_ref, bias_ref, inv_ref, ones_ref, diag_ref):
@@ -137,7 +139,7 @@
 
 
 def scores_kernel(
-    stats_ref, logits_ref, dw_ref, bias_ref, inv_ref, k_ref, n_ref,
+    stats_ref, logits_ref, dw_ref, bias_ref, inv_ref, k_ref, pick_ref, n_ref,
     ds_ref, w_ref, scaled_ref, along_ref, send_ref, n_here, n_sem,
 ):
     fetch = pltpu.make_async_copy(n_ref, n_here, n_sem)
@@ -162,18 +164,13 @@
             along_ref[b, g] = (scaled * bias_ref[b, g] * (1.0 / CP)).astype(BF16)
 
     mask = head_mask()
-    queries = jnp.zeros((HC, 2 * T), F32)
+    chosen = []
     for b in range(B):
         spread = dot(k_ref[b], ds_ref[b], TN)
-        chosen = jnp.concatenate(
-            [
-                jnp.where(mask, spread[:, g * 128 : (g + 1) * 128], 0.0).astype(BF16)
-                for g in range(G)
-            ],
-            axis=1,
-        )
-        queries = queries + dot(chosen, query_lanes(2 * T, b * T), NT)
-    queries = queries * SCALE
+        chosen += [
+            jnp.where(mask, spread[:, g * 128 : (g + 1) * 128], 0.0).astype(BF16) for g in range(G)
+        ]
+    queries = dot(jnp.concatenate(chosen, axis=1), pick_ref[...], NT) * SCALE
 
     fetch.wait()
     total = jnp.zeros((128, WIDE), F32)
@@ -196,7 +193,9 @@
     values = [dot(gt_ref[b], w_ref[b], NT) for b in range(B)]
     kv = jnp.concatenate(keys + values, axis=1)
     for h in range(H):
-        kv_ref[h] = kv[h * C : (h + 1) * C].astype(BF16)
+        for t in range(3):
+            part = kv[h * C : (h + 1) * C, t * 128 : (t + 1) * 128]
+            kv_ref[h, t * C : (t + 1) * C, :] = part.astype(BF16)
 
 
 def pair_kernel(groups, scaled_ref, along_ref, n_ref, wt_ref, out_ref, ones_ref, diag_ref):
@@ -226,18 +225,19 @@
     total = jnp.sum(got_ref[:, 0:C, 0 : 2 * T].astype(F32), axis=0)
     for b in range(B):
         query_ref[b] = total[:, b * T : (b + 1) * T]
-    both = split_halves(join_halves(got_ref[:, C : C + H, :]))
+    dwt = join_halves(got_ref[:, C : C + H, :]).astype(BF16)
+    send_ref[:, 0 : 3 * C, :] = kv_ref[...]
     for h in range(H):
-        send_ref[h, 0:C, :] = kv_ref[h]
-        send_ref[h, C : C + H, 0 : 2 * CP] = both
+        send_ref[h, 3 * C :, :] = dwt
 
 
 def keys_out_kernel(got_ref, key_ref, value_ref, dwt_ref):
-    total = jnp.sum(got_ref[:, 0:C, :].astype(F32), axis=0)
-    for b in range(B):
-        key_ref[b] = total[:, b * T : (b + 1) * T]
-        value_ref[b] = total[:, (B + b) * T : (B + b + 1) * T]
-    dwt_ref[...] = join_halves(got_ref[:, C : C + H, 0 : 2 * CP])
+    total = jnp.sum(got_ref[...].astype(F32), axis=0)
+    kv = jnp.concatenate([total[t * C : (t + 1) * C] for t in range(3)], axis=1)
+    for b in range(B):
+        key_ref[b] = kv[:, b * T : (b + 1) * T]
+        value_ref[b] = kv[:, (B + b) * T : (B + b + 1) * T]
+    dwt_ref[...] = total[3 * C :]
 
 
 def call(kernel, outs, limit, flops=0, moved=0, **kw):
@@ -268,7 +268,8 @@
 
 def expanded(query, grad):
     shape = bf16(B, HC, QH)
-    return call(expand_kernel, [shape, shape], 16, flops=400_000_000, moved=5_000_000)(query, grad)
+    outs = [shape, shape, bf16(B * T, B * QH)]
+    return call(expand_kernel, outs, 16, flops=400_000_000, moved=5_000_000)(query, grad)
 
 
 def norm(pair, wt):
@@ -287,7 +288,7 @@
         ],
         out_specs=[spec(WIDE), spec(128), spec(128)],
         scratch_shapes=[pltpu.VMEM((256, 256), BF16), pltpu.VMEM((128, WIDE), BF16)],
-    )(in_hbm(pair), wt)
+    )(in_hbm(pair), in_hbm(wt))
 
 
 def logits(k, v, qt, gt, bias):
@@ -307,7 +308,7 @@
         24,
         flops=2_500_000_000,
         moved=8_000_000,
-        in_specs=[whole] * 6 + [pl.BlockSpec(memory_space=pltpu.HBM)],
+        in_specs=[whole] * 7 + [pl.BlockSpec(memory_space=pltpu.HBM)],
         out_specs=[whole] * 5,
         scratch_shapes=[pltpu.VMEM((B, G, T, WIDE), BF16), pltpu.SemaphoreType.DMA],
     )(*args)
@@ -317,7 +318,7 @@
     wide = pltpu.VMEM((B, HC, QH), BF16)
     return call(
         grads_kernel,
-        [bf16(PEERS, C, 4 * T)],
+        [bf16(PEERS, 3 * C, 128)],
         24,
         flops=2_500_000_000,
         moved=8_000_000,
@@ -338,11 +339,11 @@
         in_specs=[spec(128), spec(128), spec(WIDE), pl.BlockSpec((H, CP), lambda b, s: (0, 0))],
         out_specs=[pl.BlockSpec((1, groups * I8, T, CP), lambda b, s: (b, s, 0, 0))],
         scratch_shapes=[pltpu.VMEM((128, WIDE), BF16), pltpu.VMEM((128, WIDE), BF16)],
-    )(in_hbm(scaled), in_hbm(along), in_hbm(n), wt)[0]
+    )(in_hbm(scaled), in_hbm(along), in_hbm(n), in_hbm(wt))[0]
 
 
 def queries_out(got, kv):
-    return call(queries_out_kernel, [f32(B, C, T), bf16(PEERS, C + H, 4 * T)], 16)(got, kv)
+    return call(queries_out_kernel, [f32(B, C, T), bf16(PEERS, 3 * C + H, 128)], 16)(got, kv)
 
 
 def keys_out(got):
@@ -350,38 +351,32 @@
     return call(keys_out_kernel, [half, half, f32(H, CP)], 16)(got)
 
 
-def ring_gap(size, a, b):
-    return min((a - b) % size, (b - a) % size)
-
-
-def hops(source, target):
-    def place(index):
-        row, col = divmod(index, PEERS)
-        return row >> 1, col >> 2, (col >> 1 & 1) * 2 + (row & 1)
-
-    (z, x, y), (z2, x2, y2) = place(source), place(target)
-    return ring_gap(8, z, z2) + ring_gap(4, x, x2) + ring_gap(4, y, y2)
+ROUTE = (
+    "58b92a73e4d1c60f",
+    "1986b504d32cf7ea",
+    "db0a9542736e1f8c",
+    "a8b163d74e5fc290",
+    "0a71fcdbe6498253",
+    "f32ecda57b861940",
+    "352c1def8b6a9704",
+    "745d0cfe28196a3b",
+    "c695e478103f2adb",
+    "d54a9762b1e0f38c",
+    "f986a704c523d1eb",
+    "eb7d48910263ac5f",
+    "16fe0ad982bc5437",
+    "73e01fc859ab462d",
+    "f1253da0cb84e976",
+    "c039e21bfad54876",
+)
 
 
 def key_route():
-    pairs = []
-    for col in range(PEERS):
-        sources = [col * PEERS + k for k in range(PEERS)]
-        targets = [row * PEERS + col for row in range(PEERS)]
-        cost = [[hops(s, t) ** 3 for t in targets] for s in sources]
-        chosen = list(range(PEERS))
-        better = True
-        while better:
-            better = False
-            for i in range(PEERS):
-                for j in range(i):
-                    now = cost[i][chosen[i]] + cost[j][chosen[j]]
-                    then = cost[i][chosen[j]] + cost[j][chosen[i]]
-                    if then < now:
-                        chosen[i], chosen[j] = chosen[j], chosen[i]
-                        better = True
-        pairs += [(sources[i], targets[chosen[i]]) for i in range(PEERS)]
-    return pairs
+    return [
+        (col * PEERS + k, int(digit, 16) * PEERS + col)
+        for col, line in enumerate(ROUTE)
+        for k, digit in enumerate(line)
+    ]
 
 
 def spread_over(x, axis):
@@ -393,11 +388,11 @@
     k = lax.ppermute(key_in, ("row", "col"), route)
     v = lax.ppermute(value_in, ("row", "col"), route)
     wt = bias_weight.T
-    qt, gt = expanded(query_in, d_out)
+    qt, gt, pick = expanded(query_in, d_out)
     n, bias, inv = norm(pair, wt)
     scaled_scores, dw, stats = logits(k, v, qt, gt, bias)
     stats = spread_over(stats, "col")
-    ds, w, scaled, along, send = scores(stats, scaled_scores, dw, bias, inv, k, n)
+    ds, w, scaled, along, send = scores(stats, scaled_scores, dw, bias, inv, k, pick, n)
     got = spread_over(send, "col")
     kv = grads(ds, w, query_in, d_out)
     d_query, send = queries_out(got, kv)

time: 85.4 us -> 77.9 us (0.912)
  waiting for transfers between devices: 13.6 us -> 10.9 us
  starting transfers between devices: 26.8 us -> 24.2 us
  blocking collectives: 14.4 us -> 12.9 us
    all_to_all x2, starting transfers between devices: 16.7 us -> 13.1 us  [spread_over(): return lax.all_to_all(x, axis, 0, 0, tiled=True)]
    all_to_all x2, waiting for transfers between devices: 13.6 us -> 10.8 us  [spread_over(): return lax.all_to_all(x, axis, 0, 0, tiled=True)]
    all_to_all x1, blocking collectives: 14.4 us -> 12.9 us  [spread_over(): return lax.all_to_all(x, axis, 0, 0, tiled=True)]
    ppermute x1, starting transfers between devices: 2.92 us -> 4.38 us  [shards(): v = lax.ppermute(value_in, ('row', 'col'), route)]
  transfers between devices with their start and end apart: 4 -> 4, of which waited for: 2 -> 2; matrix products, arithmetic and copies ran while one was open for 0% -> 0% of each run, Pallas kernels for 24% -> 27%
where the time goes in v3:
time: 77.9 us; the launch traced here: 76.8 us
  Pallas kernels  28.1 us (36%)
  starting transfers between devices  24.2 us (31%)
  blocking collectives  12.9 us (17%)
  waiting for transfers between devices  10.9 us (14%)
    all_to_all x2, starting transfers between devices, spread_over(): return lax.all_to_all(x, axis, 0, 0, tiled=True)  13.1 us
    all_to_all x1, blocking collectives, spread_over(): return lax.all_to_all(x, axis, 0, 0, tiled=True)  12.9 us
    all_to_all x2, waiting for transfers between devices, spread_over(): return lax.all_to_all(x, axis, 0, 0, tiled=True)  10.8 us
    pallas_call x1, Pallas kernels, norm(): call(lambda *refs: norm_kernel(groups, *refs), [far(B, G, T, WIDE), f32(B...  7.98 us
    pallas_call x1, Pallas kernels, pair_grad(): call(lambda *refs: pair_kernel(groups, *refs), [bf16(B, T, T, CP)], 24, f...  7.04 us
    ppermute x1, starting transfers between devices, shards(): k = lax.ppermute(key_in, ('row', 'col'), route)  6.72 us
    pallas_call x1, Pallas kernels, scores(): call(scores_kernel, [low, low, cell, cell, bf16(PEERS, C + H, 2 * CP)], 2...  4.9 us
    ppermute x1, starting transfers between devices, shards(): v = lax.ppermute(value_in, ('row', 'col'), route)  4.38 us
  transfers between devices with their start and end apart: 4, of which 2 were waited for; matrix products, arithmetic and copies ran while one was open for 0% of the time, Pallas kernels for 27%

profile of v3, /device:TPU:16, one launch (start us, length us, event | category | flops | bytes accessed | tf_op | source)
XLA Modules:
  0.0 76.8 jit_solution(539947059569734499)
XLA Ops:
  0.6 6.7 %collective-permute-start = (bf16[2,96,384]{2,1,0:T(8,128)(2,1)}, bf16[2,96,384]{2,1,0:T(8,128)(2,1)S(1)}, u32[]{:S(2)}, u32[]{:S(2)}) collective-permute-start(bf16[2,96,384]{2,1,0:T(8,128)(2,1)} %param.7), channel_id=1, source_target_pairs={{0,80},{1,128},{2,176},{3,144},{4,32},{5,160},{6,112},{7,48},{8,22... | collective-permute-start | bytes 442376 | tf_op jit(solution)/shard_map/ppermute | solution.py:388
  7.3 4.4 %collective-permute-start.1 = (bf16[2,96,384]{2,1,0:T(8,128)(2,1)}, bf16[2,96,384]{2,1,0:T(8,128)(2,1)S(1)}, u32[]{:S(2)}, u32[]{:S(2)}) collective-permute-start(bf16[2,96,384]{2,1,0:T(8,128)(2,1)} %param.8), channel_id=1, source_target_pairs={{0,80},{1,128},{2,176},{3,144},{4,32},{5,160},{6,112},{7,48},{8,22... | collective-permute-start | bytes 442376 | tf_op jit(solution)/shard_map/ppermute | solution.py:389
  11.7 0.0 copy-start.1
  11.7 0.0 copy-start.2
  11.7 8.0 %shard_map.102 = (bf16[2,12,96,1024]{3,2,1,0:T(8,128)(2,1)}, f32[2,12,96,128]{3,2,1,0:T(8,128)S(1)}, f32[2,12,96,128]{3,2,1,0:T(8,128)S(1)}) custom-call(bf16[2,96,96,128]{3,2,1,0:T(8,128)(2,1)} %refs_0_.1, bf16[16,128]{1,0:T(8,128)(2,1)} %bitcast.9), custom_call_target="tpu_custom_call" | custom-call | flops 4000000000 | bytes 12000000 | tf_op jit(solution)/shard_map/pallas_call | solution.py:278
  19.7 0.0 copy-done.1
  19.7 0.0 copy-done.2
  19.7 1.5 %shard_map.101 = (bf16[2,384,1536]{2,1,0:T(8,128)(2,1)S(1)}, bf16[2,384,1536]{2,1,0:T(8,128)(2,1)S(1)}, bf16[192,3072]{1,0:T(8,128)(2,1)S(1)}) custom-call(bf16[2,96,384]{2,1,0:T(8,128)(2,1)S(1)} %copy-done.1, bf16[2,96,384]{2,1,0:T(8,128)(2,1)S(1)} %copy-done.2), custom_call_target="tpu_custom_call" | custom-call | flops 400000000 | bytes 5000000 | tf_op jit(solution)/shard_map/pallas_call | solution.py:272
  21.3 0.0 collective-permute-done.k_ref
  21.3 0.0 collective-permute-done.1.v_ref
  21.3 0.0 copy-start
  21.3 1.1 %shard_map.103 = (f32[2,12,96,128]{3,2,1,0:T(8,128)S(1)}, f32[2,12,96,128]{3,2,1,0:T(8,128)S(1)}, f32[16,48,128]{2,1,0:T(8,128)S(1)}) custom-call(bf16[2,96,384]{2,1,0:T(8,128)(2,1)S(1)} %collective-permute-done.k_ref, bf16[2,96,384]{2,1,0:T(8,128)(2,1)S(1)} %collective-permute-done.1.v_ref, bf16[2,384,1536]{2,1,0:T(8,128)(2,1)S(1)} %get-tuple-element.24.qt_ref, ...), custom_call_target="tpu_custom_call" | custom-call | flops 1000000000 | bytes 8000000 | tf_op jit(solution)/shard_map/pallas_call | solution.py:296
  22.4 12.9 %all_to_all.15.stats_ref = f32[16,48,128]{2,1,0:T(8,128)S(1)} all-to-all(f32[16,48,128]{2,1,0:T(8,128)S(1)} %get-tuple-element.27), channel_id=1, replica_groups=mesh['row'=16,'col'=16] {'col'}, dimensions={0} | all-to-all | bytes 786432 | tf_op jit(solution)/shard_map/all_to_all | solution.py:383
  35.3 0.0 copy-done
  35.3 4.9 %shard_map.104 = (bf16[2,96,1536]{2,1,0:T(8,128)(2,1)}, bf16[2,96,1536]{2,1,0:T(8,128)(2,1)}, bf16[2,12,96,128]{3,2,1,0:T(8,128)(2,1)}, bf16[2,12,96,128]{3,2,1,0:T(8,128)(2,1)}, bf16[16,40,256]{2,1,0:T(8,128)(2,1)}) custom-call(f32[16,48,128]{2,1,0:T(8,128)S(1)} %all_to_all.15.stats_ref, f32[2,12,96,128]{3,2,1,0:T(8,128)S(1)} %get-tuple-element.28.logits_ref, ...), custom_call_target="tpu_custom_call" | custom-call | flops 2500000000 | bytes 8000000 | tf_op jit(solution)/shard_map/pallas_call | solution.py:305
  40.2 6.3 %all-to-all-start.1 = ((bf16[16,40,256]{2,1,0:T(8,128)(2,1)}), bf16[16,40,256]{2,1,0:T(8,128)(2,1)S(1)}, u32[]{:S(2)}, u32[]{:S(2)}) async-start(bf16[16,40,256]{2,1,0:T(8,128)(2,1)} %get-tuple-element.33), calls=%async_computation.1 | async-start | bytes 655360 | tf_op jit(solution)/shard_map/all_to_all | solution.py:383
  46.4 4.0 %shard_map.105.kv_ref = bf16[16,72,128]{2,1,0:T(8,128)(2,1)S(1)} custom-call(bf16[2,96,1536]{2,1,0:T(8,128)(2,1)} %get-tuple-element.34.ds_ref, bf16[2,96,1536]{2,1,0:T(8,128)(2,1)} %get-tuple-element.35.w_ref, bf16[2,96,384]{2,1,0:T(8,128)(2,1)} %q_ref.3, bf16[2,96,384]{2,1,0:T(8,128)(2,1)} %g_ref.3), custom_call_target="tpu_custom_call" | custom-call | flops 2500000000 | bytes 8000000 | tf_op jit(solution)/shard_map/pallas_call | solution.py:319
  50.5 3.2 %all-to-all-done.1.got_ref = bf16[16,40,256]{2,1,0:T(8,128)(2,1)S(1)} async-done(((bf16[16,40,256]{2,1,0:T(8,128)(2,1)}), bf16[16,40,256]{2,1,0:T(8,128)(2,1)S(1)}, u32[]{:S(2)}, u32[]{:S(2)}) %all-to-all-start.1) | async-done | bytes 327712 | tf_op jit(solution)/shard_map/all_to_all | solution.py:383
  53.7 0.8 %shard_map.106 = (f32[2,24,96]{2,1,0:T(8,128)}, bf16[16,88,128]{2,1,0:T(8,128)(2,1)}) custom-call(bf16[16,40,256]{2,1,0:T(8,128)(2,1)S(1)} %all-to-all-done.1.got_ref, bf16[16,72,128]{2,1,0:T(8,128)(2,1)S(1)} %shard_map.105.kv_ref), custom_call_target="tpu_custom_call" | custom-call | tf_op jit(solution)/shard_map/pallas_call | solution.py:346
  54.5 6.9 %all-to-all-start.2 = ((bf16[16,88,128]{2,1,0:T(8,128)(2,1)}), bf16[16,88,128]{2,1,0:T(8,128)(2,1)S(1)}, u32[]{:S(2)}, u32[]{:S(2)}) async-start(bf16[16,88,128]{2,1,0:T(8,128)(2,1)} %get-tuple-element.37), calls=%async_computation.2 | async-start | bytes 720896 | tf_op jit(solution)/shard_map/all_to_all | solution.py:383
  61.3 7.0 %shard_map.108 = bf16[2,96,96,128]{3,2,1,0:T(8,128)(2,1)} custom-call(bf16[2,12,96,128]{3,2,1,0:T(8,128)(2,1)} %get-tuple-element.40.refs_0_, bf16[2,12,96,128]{3,2,1,0:T(8,128)(2,1)} %get-tuple-element.41.refs_1_, bf16[2,12,96,1024]{3,2,1,0:T(8,128)(2,1)} %get-tuple-element.32.n_ref.refs_2_, bf16[16,128]{1,0:T(8,128)(2,1)} %bitcast.10), custom_call_target="tpu_custom_call" | custom-call | flops 4000000000 | bytes 10000000 | tf_op jit(solution)/shard_map/pallas_call | solution.py:332
  68.4 7.6 %all-to-all-done.2.got_ref = bf16[16,88,128]{2,1,0:T(8,128)(2,1)S(1)} async-done(((bf16[16,88,128]{2,1,0:T(8,128)(2,1)}), bf16[16,88,128]{2,1,0:T(8,128)(2,1)S(1)}, u32[]{:S(2)}, u32[]{:S(2)}) %all-to-all-start.2) | async-done | bytes 360480 | tf_op jit(solution)/shard_map/all_to_all | solution.py:383
  76.0 0.7 shard_map.107
Async XLA Ops:
  0.6 20.6 %collective-permute-start = (bf16[2,96,384]{2,1,0:T(8,128)(2,1)}, bf16[2,96,384]{2,1,0:T(8,128)(2,1)S(1)}, u32[]{:S(2)}, u32[]{:S(2)}) collective-permute-start(bf16[2,96,384]{2,1,0:T(8,128)(2,1)} %param.7), channel_id=1, source_target_pairs={{0,80},{1,128},{2,176},{3,144},{4,32},{5,160},{6,112},{7,48},{8,22... | collective-permute-start | bytes 442376 | tf_op jit(solution)/shard_map/ppermute | solution.py:388
  7.3 13.9 %collective-permute-start.1 = (bf16[2,96,384]{2,1,0:T(8,128)(2,1)}, bf16[2,96,384]{2,1,0:T(8,128)(2,1)S(1)}, u32[]{:S(2)}, u32[]{:S(2)}) collective-permute-start(bf16[2,96,384]{2,1,0:T(8,128)(2,1)} %param.8), channel_id=1, source_target_pairs={{0,80},{1,128},{2,176},{3,144},{4,32},{5,160},{6,112},{7,48},{8,22... | collective-permute-start | bytes 442376 | tf_op jit(solution)/shard_map/ppermute | solution.py:389
  11.7 8.0 %copy-start.1 = (bf16[2,96,384]{2,1,0:T(8,128)(2,1)S(1)}, bf16[2,96,384]{2,1,0:T(8,128)(2,1)}, u32[]{:S(2)}) copy-start(bf16[2,96,384]{2,1,0:T(8,128)(2,1)} %q_ref.3) | copy-start | bytes 442372
  11.7 8.0 %copy-start.2 = (bf16[2,96,384]{2,1,0:T(8,128)(2,1)S(1)}, bf16[2,96,384]{2,1,0:T(8,128)(2,1)}, u32[]{:S(2)}) copy-start(bf16[2,96,384]{2,1,0:T(8,128)(2,1)} %g_ref.3) | copy-start | bytes 442372
  21.3 14.0 %copy-start = (bf16[2,12,96,1024]{3,2,1,0:T(8,128)(2,1)S(1)}, bf16[2,12,96,1024]{3,2,1,0:T(8,128)(2,1)}, u32[]{:S(2)}) copy-start(bf16[2,12,96,1024]{3,2,1,0:T(8,128)(2,1)} %get-tuple-element.32.n_ref.refs_2_) | copy-start | bytes 14155780
  40.2 13.5 %all-to-all-start.1 = ((bf16[16,40,256]{2,1,0:T(8,128)(2,1)}), bf16[16,40,256]{2,1,0:T(8,128)(2,1)S(1)}, u32[]{:S(2)}, u32[]{:S(2)}) async-start(bf16[16,40,256]{2,1,0:T(8,128)(2,1)} %get-tuple-element.33), calls=%async_computation.1 | async-start | bytes 655360 | tf_op jit(solution)/shard_map/all_to_all | solution.py:383
  54.5 21.5 %all-to-all-start.2 = ((bf16[16,88,128]{2,1,0:T(8,128)(2,1)}), bf16[16,88,128]{2,1,0:T(8,128)(2,1)S(1)}, u32[]{:S(2)}, u32[]{:S(2)}) async-start(bf16[16,88,128]{2,1,0:T(8,128)(2,1)} %get-tuple-element.37), calls=%async_computation.2 | async-start | bytes 720896 | tf_op jit(solution)/shard_map/all_to_all | solution.py:383

commit v4 on v3

--- a/solution.py
+++ b/solution.py
@@ -23,6 +23,8 @@
 QH = T * H
 SCALE = 1.0 / math.sqrt(C)
 PEERS = 16
+PLANE = 2 * PEERS
+DEPTH = 8
 GROUPS = 6
 
 NN = (((1,), (0,)), ((), ()))
@@ -63,11 +65,18 @@
             target[b, :, at] = jnp.where(mask, spread[:, at], 0.0).astype(BF16)
 
 
-def expand_kernel(q_ref, g_ref, qt_ref, gt_ref, pick_ref):
+def expand_kernel(q_ref, g_ref, qt_ref, gt_ref, pick_ref, turn_ref):
     expand(q_ref, qt_ref)
     expand(g_ref, gt_ref)
-    for b in range(B):
-        pick_ref[:, b * QH : (b + 1) * QH] = query_lanes(B * T, b * T)
+    lane = iota((256, B * HC), 1)
+    batch = jnp.where(lane >= HC, 1, 0)
+    within = lane - batch * HC
+    query = (within >> 7) * 32 + (within >> 2 & 3) * I8 + (within >> 4 & 7)
+    pick_ref[...] = jnp.where(iota((256, B * HC), 0) == batch * T + query, 1.0, 0.0).astype(BF16)
+    row = iota((2 * H * 16, HC), 0)
+    feature = (row >> 5) * C + (row >> 4 & 1) * 12 + (row & 15)
+    used = ((row & 15) < 12) & (iota((2 * H * 16, HC), 1) == feature)
+    turn_ref[...] = jnp.where(used, 1.0, 0.0).astype(BF16)
 
 
 def norm_kernel(groups, pair_ref, wt_ref, n_ref, bias_ref, inv_ref, ones_ref, diag_ref):
@@ -127,23 +136,31 @@
             stats_ref[:, row + G : row + G + 1, :] = jnp.broadcast_to(balance[None], (PEERS, 1, 128))
 
 
-def split_halves(x):
-    high = x.astype(BF16)
-    low = (x - high.astype(F32)).astype(BF16)
-    return jnp.concatenate([high, low], axis=1)
-
-
-def join_halves(parts):
-    parts = parts.astype(F32)
-    return jnp.sum(parts[:, :, :CP] + parts[:, :, CP:], axis=0)
+def four_query(shape, dim):
+    lane = iota(shape, dim)
+    return (lane >> 7) * 32 + (lane >> 2 & 3) * I8 + (lane >> 4 & 7)
+
+
+def four_heads(parts, q):
+    slot = iota((T, 128), 1) >> 2 & 3
+    tiles = []
+    for wide in range(G // 4):
+        tile = parts[wide * 4 + q]
+        for k in range(4):
+            if k != q:
+                moved = pltpu.roll(parts[wide * 4 + k], (4 * (k - q)) % 128, 1)
+                tile = jnp.where(slot == k, moved, tile)
+        tiles.append(tile.astype(BF16))
+    return jnp.concatenate(tiles, axis=1)
 
 
 def scores_kernel(
-    stats_ref, logits_ref, dw_ref, bias_ref, inv_ref, k_ref, pick_ref, n_ref,
-    ds_ref, w_ref, scaled_ref, along_ref, send_ref, n_here, n_sem,
+    stats_ref, logits_ref, dw_ref, bias_ref, inv_ref, k_ref, pick_ref, turn_ref, n_ref,
+    four_out, w_out, scaled_out, along_out, send_ref,
+    ds_ref, four_ref, w_ref, scaled_ref, along_ref, sems,
 ):
-    fetch = pltpu.make_async_copy(n_ref, n_here, n_sem)
-    fetch.start()
+    keep = iota((128, HC), 0) >> 5 == (iota((128, HC), 1) & 3)
+    chosen = []
     for b in range(B):
         levels = stats_ref[:, b * 2 * G : b * 2 * G + G, :]
         balances = stats_ref[:, b * 2 * G + G : (b + 1) * 2 * G, :]
@@ -152,6 +169,7 @@
         total = jnp.sum(parts, axis=0)
         level = top + jnp.log(total)
         balance = jnp.sum(parts * balances, axis=0) / total
+        lows = []
         for g in range(G):
             weights = jnp.exp(logits_ref[b, g] - level[g : g + 1])
             ds = weights * (dw_ref[b, g] - balance[g : g + 1])
@@ -159,47 +177,73 @@
             at = slice(g * 128, (g + 1) * 128)
             ds_ref[b, :, at] = low
             w_ref[b, :, at] = weights.astype(BF16)
-            scaled = low.astype(F32) * inv_ref[b, g]
+            low = low.astype(F32)
+            lows.append(low)
+            scaled = low * inv_ref[b, g]
             scaled_ref[b, g] = scaled.astype(BF16)
             along_ref[b, g] = (scaled * bias_ref[b, g] * (1.0 / CP)).astype(BF16)
-
-    mask = head_mask()
-    chosen = []
-    for b in range(B):
-        spread = dot(k_ref[b], ds_ref[b], TN)
-        chosen += [
-            jnp.where(mask, spread[:, g * 128 : (g + 1) * 128], 0.0).astype(BF16) for g in range(G)
-        ]
+        k_turned = dot(turn_ref[...], k_ref[b], NT).astype(BF16)
+        quarters = []
+        for q in range(4):
+            four = four_heads(lows, q)
+            four_ref[b, q] = four
+            spread = dot(k_turned[q * 128 : (q + 1) * 128], four)
+            quarters.append(jnp.where(keep, spread, 0.0).astype(BF16))
+        chosen.append(jnp.concatenate(quarters, axis=0))
+    pairs = ((four_ref, four_out), (w_ref, w_out), (scaled_ref, scaled_out), (along_ref, along_out))
+    stores = [pltpu.make_async_copy(x, y, sems.at[i]) for i, (x, y) in enumerate(pairs)]
+    for store in stores:
+        store.start()
     queries = dot(jnp.concatenate(chosen, axis=1), pick_ref[...], NT) * SCALE
 
-    fetch.wait()
     total = jnp.zeros((128, WIDE), F32)
     for b in range(B):
         left = jnp.concatenate([ds_ref[b, :, g * 128 : (g + 1) * 128] for g in range(G)], axis=0)
-        total = total + dot(left, n_here[b].reshape(G * T, WIDE), TN)
+        total = total + dot(left, n_ref[b].reshape(G * T, WIDE), TN)
     dwt = jnp.zeros((H, CP), F32)
     for i in range(I8):
         dwt = dwt + total[i * H : (i + 1) * H, i * CP : (i + 1) * CP]
-    both = split_halves(dwt)
+    side = jnp.concatenate([dwt[0:8], dwt[8:16]], axis=1)
     for h in range(H):
-        send_ref[h, 0:C, 0 : 2 * T] = queries[h * C : (h + 1) * C].astype(BF16)
-        send_ref[h, C : C + H, :] = both
-
-
-def grads_kernel(ds_ref, w_ref, q_ref, g_ref, kv_ref, qt_ref, gt_ref):
-    expand(q_ref, qt_ref)
-    expand(g_ref, gt_ref)
-    keys = [dot(qt_ref[b], ds_ref[b], NT) * SCALE for b in range(B)]
-    values = [dot(gt_ref[b], w_ref[b], NT) for b in range(B)]
+        for half in range(2):
+            at = (2 * h + half) * 16
+            piece = jnp.concatenate([side, queries[at : at + 16]], axis=0)
+            send_ref[half * PEERS + h] = piece.astype(BF16)
+    for store in stores:
+        store.wait()
+
+
+def grads_kernel(side_ref, four_ref, w_ref, q_ref, g_ref, keep_ref, give_ref, all_ref):
+    lanes = jnp.where(iota((T, HC), 0) == four_query((T, HC), 1), 1.0, 0.0).astype(BF16)
+    row_head = (iota((HC, HC), 0) * 171) >> 12
+    mask = (row_head & 3) == (iota((HC, HC), 1) & 3)
+
+    def select(source):
+        return jnp.where(mask, dot(source, lanes, TN), 0.0).astype(BF16)
+
+    def gather(left, fours):
+        quarter = HC // 4
+        return jnp.concatenate(
+            [dot(left[q * quarter : (q + 1) * quarter], fours[q], NT) for q in range(4)], axis=0
+        )
+
+    keys, values = [], []
+    for b in range(B):
+        keys.append(gather(select(q_ref[b]), [four_ref[b, q] for q in range(4)]) * SCALE)
+        parts = [w_ref[b, :, g * 128 : (g + 1) * 128].astype(F32) for g in range(G)]
+        values.append(gather(select(g_ref[b]), [four_heads(parts, q) for q in range(4)]))
     kv = jnp.concatenate(keys + values, axis=1)
     for h in range(H):
         for t in range(3):
-            part = kv[h * C : (h + 1) * C, t * 128 : (t + 1) * 128]
-            kv_ref[h, t * C : (t + 1) * C, :] = part.astype(BF16)
-
-
-def pair_kernel(groups, scaled_ref, along_ref, n_ref, wt_ref, out_ref, ones_ref, diag_ref):
-    first = (pl.program_id(0) == 0) & (pl.program_id(1) == 0)
+            all_ref[h, t * C : (t + 1) * C, :] = kv[h * C : (h + 1) * C, t * 128 : (t + 1) * 128]
+    y_lo = side_ref[0]
+    for z in range(DEPTH):
+        keep_ref[z] = all_ref[2 * z + y_lo].astype(BF16)
+        give_ref[z] = all_ref[2 * z + 1 - y_lo].astype(BF16)
+
+
+def pair_kernel(groups, scaled_ref, along_ref, n_ref, wt_ref, _, out_ref, ones_ref, diag_ref):
+    first = pl.program_id(0) == 0
 
     @pl.when(first)
     def _():
@@ -221,14 +265,26 @@
                 out_ref[0, g * I8 + 2 * p + k] = grad[g * T : (g + 1) * T, k * CP : (k + 1) * CP]
 
 
-def queries_out_kernel(got_ref, kv_ref, query_ref, send_ref):
-    total = jnp.sum(got_ref[:, 0:C, 0 : 2 * T].astype(F32), axis=0)
-    for b in range(B):
-        query_ref[b] = total[:, b * T : (b + 1) * T]
-    dwt = join_halves(got_ref[:, C : C + H, :]).astype(BF16)
-    send_ref[:, 0 : 3 * C, :] = kv_ref[...]
-    for h in range(H):
-        send_ref[h, 3 * C :, :] = dwt
+def bias_out_kernel(side_ref, got_ref, keep_ref, more_ref, _, send_ref, own_ref, other_ref):
+    side = jnp.sum(got_ref[:, 0:8, :].astype(F32), axis=0)
+    dwt = jnp.concatenate([side[:, :CP], side[:, CP:]], axis=0)
+    for z in range(DEPTH):
+        kv = keep_ref[z].astype(F32) + more_ref[z].astype(F32)
+        send_ref[z] = jnp.concatenate([kv, dwt], axis=0).astype(BF16)
+    parts = [
+        jnp.sum(got_ref[y * PEERS : (y + 1) * PEERS, 8:24, :].astype(F32), axis=0) for y in range(2)
+    ]
+    first = side_ref[0] == 0
+    own_ref[...] = jnp.where(first, parts[0], parts[1])
+    other_ref[...] = jnp.where(first, parts[1], parts[0])
+
+
+def queries_out_kernel(side_ref, own_ref, other_ref, query_ref):
+    first = side_ref[0] == 0
+    own, other = own_ref[0:12], other_ref[0:12]
+    both = jnp.concatenate([jnp.where(first, own, other), jnp.where(first, other, own)], axis=0)
+    for b in range(B):
+        query_ref[b] = both[:, b * T : (b + 1) * T]
 
 
 def keys_out_kernel(got_ref, key_ref, value_ref, dwt_ref):
@@ -268,7 +324,7 @@
 
 def expanded(query, grad):
     shape = bf16(B, HC, QH)
-    outs = [shape, shape, bf16(B * T, B * QH)]
+    outs = [shape, shape, bf16(256, B * HC), bf16(2 * H * 16, HC)]
     return call(expand_kernel, outs, 16, flops=400_000_000, moved=5_000_000)(query, grad)
 
 
@@ -300,50 +356,79 @@
 
 def scores(*args):
     low = far(B, T, QH)
+    four = far(B, 4, T, HC)
     cell = far(B, G, T, 128)
     whole = pl.BlockSpec(memory_space=pltpu.VMEM)
+    hbm = pl.BlockSpec(memory_space=pltpu.HBM)
     return call(
         scores_kernel,
-        [low, low, cell, cell, bf16(PEERS, C + H, 2 * CP)],
+        [four, low, cell, cell, bf16(PLANE, 24, 256)],
         24,
         flops=2_500_000_000,
         moved=8_000_000,
-        in_specs=[whole] * 7 + [pl.BlockSpec(memory_space=pltpu.HBM)],
-        out_specs=[whole] * 5,
-        scratch_shapes=[pltpu.VMEM((B, G, T, WIDE), BF16), pltpu.SemaphoreType.DMA],
+        in_specs=[whole] * 9,
+        out_specs=[hbm] * 4 + [whole],
+        scratch_shapes=[
+            pltpu.VMEM((B, T, QH), BF16),
+            pltpu.VMEM((B, 4, T, HC), BF16),
+            pltpu.VMEM((B, T, QH), BF16),
+            pltpu.VMEM((B, G, T, 128), BF16),
+            pltpu.VMEM((B, G, T, 128), BF16),
+            pltpu.SemaphoreType.DMA((4,)),
+        ],
     )(*args)
 
 
-def grads(*args):
-    wide = pltpu.VMEM((B, HC, QH), BF16)
+WHOLE = pl.BlockSpec(memory_space=pltpu.VMEM)
+SCALAR = pl.BlockSpec(memory_space=pltpu.SMEM)
+
+
+def grads(side, *args):
+    half = bf16(DEPTH, 3 * C, 128)
     return call(
         grads_kernel,
-        [bf16(PEERS, 3 * C, 128)],
+        [half, half],
         24,
         flops=2_500_000_000,
         moved=8_000_000,
-        scratch_shapes=[wide, wide],
-    )(*[in_hbm(x) for x in args])[0]
-
-
-def pair_grad(scaled, along, n, wt):
+        in_specs=[SCALAR] + [WHOLE] * 4,
+        scratch_shapes=[pltpu.VMEM((H, 3 * C, 128), F32)],
+    )(side, *[in_hbm(x) for x in args])
+
+
+def pair_grad(b, scaled, along, n, wt, done):
     groups = GROUPS
-    spec = lambda *tail: pl.BlockSpec((1, groups, T) + tail, lambda b, s: (b, s, 0, 0))
+    spec = lambda *tail: pl.BlockSpec((1, groups, T) + tail, lambda s: (b, s, 0, 0))
+    fresh = done is None
     return call(
-        lambda *refs: pair_kernel(groups, *refs),
-        [bf16(B, T, T, CP)],
+        lambda *refs: pair_kernel(groups, *(refs if not fresh else refs[:4] + (None,) + refs[4:])),
+        [far(B, T, T, CP)],
         24,
-        flops=4_000_000_000,
-        moved=10_000_000,
-        grid=(B, G // groups),
-        in_specs=[spec(128), spec(128), spec(WIDE), pl.BlockSpec((H, CP), lambda b, s: (0, 0))],
-        out_specs=[pl.BlockSpec((1, groups * I8, T, CP), lambda b, s: (b, s, 0, 0))],
+        flops=2_000_000_000,
+        moved=5_000_000,
+        grid=(G // groups,),
+        in_specs=[spec(128), spec(128), spec(WIDE), pl.BlockSpec((H, CP), lambda s: (0, 0))]
+        + ([] if fresh else [pl.BlockSpec(memory_space=pltpu.HBM)]),
+        out_specs=[pl.BlockSpec((1, groups * I8, T, CP), lambda s: (b, s, 0, 0))],
         scratch_shapes=[pltpu.VMEM((128, WIDE), BF16), pltpu.VMEM((128, WIDE), BF16)],
-    )(in_hbm(scaled), in_hbm(along), in_hbm(n), in_hbm(wt))[0]
-
-
-def queries_out(got, kv):
-    return call(queries_out_kernel, [f32(B, C, T), bf16(PEERS, 3 * C + H, 128)], 16)(got, kv)
+        **({} if fresh else dict(input_output_aliases={4: 0})),
+    )(in_hbm(scaled), in_hbm(along), in_hbm(n), in_hbm(wt), *([] if fresh else [done]))[0]
+
+
+def bias_out(side, got, keep, more, after):
+    half = f32(16, 256)
+    return call(
+        bias_out_kernel,
+        [bf16(DEPTH, 3 * C + H, 128), half, half],
+        16,
+        in_specs=[SCALAR] + [WHOLE] * 3 + [pl.BlockSpec(memory_space=pltpu.HBM)],
+    )(side, got, keep, more, in_hbm(after))
+
+
+def queries_out(side, own, other):
+    return call(queries_out_kernel, [f32(B, C, T)], 16, in_specs=[SCALAR] + [WHOLE] * 2)(
+        side, own, other
+    )[0]
 
 
 def keys_out(got):
@@ -379,8 +464,12 @@
     ]
 
 
-def spread_over(x, axis):
-    return lax.all_to_all(x, axis, 0, 0, tiled=True)
+def spread_over(x, axis, groups=None):
+    return lax.all_to_all(x, axis, 0, 0, tiled=True, axis_index_groups=groups)
+
+
+def swap_y(x):
+    return lax.ppermute(x, "row", [(r, r ^ 1) for r in range(PEERS)])
 
 
 def shards(query_in, key_in, value_in, pair, bias_weight, d_out):
@@ -388,16 +477,24 @@
     k = lax.ppermute(key_in, ("row", "col"), route)
     v = lax.ppermute(value_in, ("row", "col"), route)
     wt = bias_weight.T
-    qt, gt, pick = expanded(query_in, d_out)
+    side = (lax.axis_index("row") & 1).astype(jnp.int32).reshape(1)
+    qt, gt, pick, turn = expanded(query_in, d_out)
+    side, qt = lax.optimization_barrier((side, qt))
     n, bias, inv = norm(pair, wt)
     scaled_scores, dw, stats = logits(k, v, qt, gt, bias)
     stats = spread_over(stats, "col")
-    ds, w, scaled, along, send = scores(stats, scaled_scores, dw, bias, inv, k, pick, n)
-    got = spread_over(send, "col")
-    kv = grads(ds, w, query_in, d_out)
-    d_query, send = queries_out(got, kv)
-    got = spread_over(send, "row")
-    d_pair = pair_grad(scaled, along, n, wt)
+    ds, w, scaled, along, send = scores(
+        stats, scaled_scores, dw, bias, inv, k, pick, turn, n
+    )
+    planes = [list(range(z * PLANE, (z + 1) * PLANE)) for z in range(DEPTH)]
+    got = spread_over(send, ("row", "col"), planes)
+    keep, give = grads(side, ds, w, query_in, d_out)
+    d_pair = pair_grad(0, scaled, along, n, wt, None)
+    send, own, other = bias_out(side, got, keep, swap_y(give), d_pair)
+    lines = [list(range(y, PEERS, 2)) for y in range(2)]
+    got = spread_over(send, "row", lines)
+    d_query = queries_out(side, own, swap_y(other))
+    d_pair = pair_grad(1, scaled, along, n, wt, d_pair)
     d_key, d_value, dwt = keys_out(got)
     flip = lambda x: jnp.swapaxes(x, 1, 2)
     return flip(d_query), flip(d_key), flip(d_value), d_pair, dwt.T

time: 77.9 us -> 74.5 us (0.956)
  waiting for transfers between devices: 10.9 us -> 7.68 us
    all_to_all x2, waiting for transfers between devices: 10.8 us -> 4.78 us  [spread_over(): return lax.all_to_all(x, axis, 0, 0, tiled=True, axis_index_groups=groups)]
    ppermute x0 -> x2, waiting for transfers between devices: none -> 2.89 us  [swap_y(): return lax.ppermute(x, 'row', [(r, r ^ 1) for r in range(PEERS)])]
    ppermute x0 -> x2, starting transfers between devices: none -> 2.16 us  [swap_y(): return lax.ppermute(x, 'row', [(r, r ^ 1) for r in range(PEERS)])]
    all_to_all x2, starting transfers between devices: 13.1 us -> 11.6 us  [spread_over(): return lax.all_to_all(x, axis, 0, 0, tiled=True, axis_index_groups=groups)]
    pallas_call x4 -> x6, Pallas kernels: 16.8 us -> 16.5 us  [the longest x2 8.21 us: pair_grad(): call(lambda *refs: pair_kernel(groups, *(refs if not fresh else refs[:4]...]
  transfers between devices with their start and end apart: 4 -> 6, of which waited for: 2 -> 2; matrix products, arithmetic and copies ran while one was open for 0% -> 0% of each run, Pallas kernels for 27% -> 29%
where the time goes in v4:
time: 74.5 us; the launch traced here: 74 us
  Pallas kernels  27.9 us (37%)
  starting transfers between devices  24.8 us (33%)
  blocking collectives  12.9 us (17%)
  waiting for transfers between devices  7.68 us (10%)
    all_to_all x1, blocking collectives, spread_over(): return lax.all_to_all(x, axis, 0, 0, tiled=True, axis_index_groups=groups)  12.9 us
    all_to_all x2, starting transfers between devices, spread_over(): return lax.all_to_all(x, axis, 0, 0, tiled=True, axis_index_groups=groups)  11.6 us
    pallas_call x2, Pallas kernels, pair_grad(): call(lambda *refs: pair_kernel(groups, *(refs if not fresh else refs[:4]...  8.21 us
    pallas_call x1, Pallas kernels, norm(): call(lambda *refs: norm_kernel(groups, *refs), [far(B, G, T, WIDE), f32(B...  7.96 us
    ppermute x1, starting transfers between devices, shards(): k = lax.ppermute(key_in, ('row', 'col'), route)  6.72 us
    all_to_all x2, waiting for transfers between devices, spread_over(): return lax.all_to_all(x, axis, 0, 0, tiled=True, axis_index_groups=groups)  4.78 us
    ppermute x1, starting transfers between devices, shards(): v = lax.ppermute(value_in, ('row', 'col'), route)  4.38 us
    pallas_call x1, Pallas kernels, scores(): call(scores_kernel, [four, low, cell, cell, bf16(PLANE, 24, 256)], 24, fl...  4.24 us
  transfers between devices with their start and end apart: 6, of which 2 were waited for; matrix products, arithmetic and copies ran while one was open for 0% of the time, Pallas kernels for 29%

profile of v4, /device:TPU:16, one launch (start us, length us, event | category | flops | bytes accessed | tf_op | source)
XLA Modules:
  0.0 74.0 jit_solution(18292273252107093358)
XLA Ops:
  0.6 6.7 %collective-permute-start = (bf16[2,96,384]{2,1,0:T(8,128)(2,1)}, bf16[2,96,384]{2,1,0:T(8,128)(2,1)S(1)}, u32[]{:S(2)}, u32[]{:S(2)}) collective-permute-start(bf16[2,96,384]{2,1,0:T(8,128)(2,1)} %param.7), channel_id=1, source_target_pairs={{0,80},{1,128},{2,176},{3,144},{4,32},{5,160},{6,112},{7,48},{8,22... | collective-permute-start | bytes 442376 | tf_op jit(solution)/shard_map/ppermute | solution.py:477
  7.3 4.4 %collective-permute-start.1 = (bf16[2,96,384]{2,1,0:T(8,128)(2,1)}, bf16[2,96,384]{2,1,0:T(8,128)(2,1)S(1)}, u32[]{:S(2)}, u32[]{:S(2)}) collective-permute-start(bf16[2,96,384]{2,1,0:T(8,128)(2,1)} %param.8), channel_id=1, source_target_pairs={{0,80},{1,128},{2,176},{3,144},{4,32},{5,160},{6,112},{7,48},{8,22... | collective-permute-start | bytes 442376 | tf_op jit(solution)/shard_map/ppermute | solution.py:478
  11.7 0.0 copy-start.1
  11.7 0.0 copy-start.2
  11.7 8.0 %shard_map.102 = (bf16[2,12,96,1024]{3,2,1,0:T(8,128)(2,1)}, f32[2,12,96,128]{3,2,1,0:T(8,128)S(1)}, f32[2,12,96,128]{3,2,1,0:T(8,128)S(1)}) custom-call(bf16[2,96,96,128]{3,2,1,0:T(8,128)(2,1)} %refs_0_.1, bf16[16,128]{1,0:T(8,128)(2,1)} %bitcast.7), custom_call_target="tpu_custom_call" | custom-call | flops 4000000000 | bytes 12000000 | tf_op jit(solution)/shard_map/pallas_call | solution.py:334
  19.7 0.0 copy-done.1
  19.7 0.0 copy-done.2
  19.7 1.6 %shard_map.101 = (bf16[2,384,1536]{2,1,0:T(8,128)(2,1)S(1)}, bf16[2,384,1536]{2,1,0:T(8,128)(2,1)S(1)}, bf16[256,768]{1,0:T(8,128)(2,1)S(1)}, bf16[512,384]{1,0:T(8,128)(2,1)S(1)}) custom-call(bf16[2,96,384]{2,1,0:T(8,128)(2,1)S(1)} %copy-done.1, bf16[2,96,384]{2,1,0:T(8,128)(2,1)S(1)} %copy-done.2), custom_call_target="tpu_custom_call" | custom-call | flops 400000000 | bytes 5000000 | tf_op jit(solution)/shard_map/pallas_call | solution.py:328
  21.3 0.0 collective-permute-done.k_ref
  21.4 0.0 collective-permute-done.1.v_ref
  21.4 0.0 copy-start
  21.4 1.1 %shard_map.103 = (f32[2,12,96,128]{3,2,1,0:T(8,128)S(1)}, f32[2,12,96,128]{3,2,1,0:T(8,128)S(1)}, f32[16,48,128]{2,1,0:T(8,128)S(1)}) custom-call(bf16[2,96,384]{2,1,0:T(8,128)(2,1)S(1)} %collective-permute-done.k_ref, bf16[2,96,384]{2,1,0:T(8,128)(2,1)S(1)} %collective-permute-done.1.v_ref, bf16[2,384,1536]{2,1,0:T(8,128)(2,1)S(1)} %get-tuple-element.32.qt_ref, ...), custom_call_target="tpu_custom_call" | custom-call | flops 1000000000 | bytes 8000000 | tf_op jit(solution)/shard_map/pallas_call | solution.py:352
  22.5 12.9 %all_to_all.15.stats_ref = f32[16,48,128]{2,1,0:T(8,128)S(1)} all-to-all(f32[16,48,128]{2,1,0:T(8,128)S(1)} %get-tuple-element.35), channel_id=1, replica_groups=mesh['row'=16,'col'=16] {'col'}, dimensions={0} | all-to-all | bytes 786432 | tf_op jit(solution)/shard_map/all_to_all | solution.py:468
  35.3 0.0 copy-done
  35.3 4.2 %shard_map.104 = (bf16[2,4,96,384]{3,2,1,0:T(8,128)(2,1)}, bf16[2,96,1536]{2,1,0:T(8,128)(2,1)}, bf16[2,12,96,128]{3,2,1,0:T(8,128)(2,1)}, bf16[2,12,96,128]{3,2,1,0:T(8,128)(2,1)}, bf16[32,24,256]{2,1,0:T(8,128)(2,1)}) custom-call(f32[16,48,128]{2,1,0:T(8,128)S(1)} %all_to_all.15.stats_ref, f32[2,12,96,128]{3,2,1,0:T(8,128)S(1)} %get-tuple-element.36.logits_ref, ...), custom_call_target="tpu_custom_call" | custom-call | flops 2500000000 | bytes 8000000 | tf_op jit(solution)/shard_map/pallas_call | solution.py:363
  39.6 8.2 %all-to-all-start.1 = ((bf16[32,24,256]{2,1,0:T(8,128)(2,1)}), bf16[32,24,256]{2,1,0:T(8,128)(2,1)S(1)}, u32[]{:S(2)}, u32[]{:S(2)}) async-start(bf16[32,24,256]{2,1,0:T(8,128)(2,1)} %get-tuple-element.42), calls=%async_computation.1 | async-start | bytes 786432 | tf_op jit(solution)/shard_map/all_to_all | solution.py:468
  47.8 2.7 %shard_map.105 = (bf16[8,72,128]{2,1,0:T(8,128)(2,1)S(1)}, bf16[8,72,128]{2,1,0:T(8,128)(2,1)S(1)}) custom-call(s32[1]{0:T(128)} %bitcast.side_ref, bf16[2,4,96,384]{3,2,1,0:T(8,128)(2,1)} %get-tuple-element.43.four_ref, bf16[2,96,1536]{2,1,0:T(8,128)(2,1)} %get-tuple-element.44.w_ref, bf16[2,96,384]{2,1,0:T(8,128)(2,1)} %q_ref.3, bf16[2,96,384]{2,1,0:T(8,128)(2,1)} %g_ref.3), custom_call_target="tpu_custom_call" | custom-call | flops 2500000000 | bytes 8000000 | tf_op jit(solution)/shard_map/pallas_call | solution.py:388
  50.5 1.3 %collective-permute-start.2 = (bf16[8,72,128]{2,1,0:T(8,128)(2,1)S(1)}, bf16[8,72,128]{2,1,0:T(8,128)(2,1)S(1)}, u32[]{:S(2)}, u32[]{:S(2)}) collective-permute-start(bf16[8,72,128]{2,1,0:T(8,128)(2,1)S(1)} %get-tuple-element.46), channel_id=1, source_target_pairs={{0,16},{16,0},{32,48},{48,32},{64,80},{80,64},{96,112},{112,96},{1... | collective-permute-start | bytes 442376 | tf_op jit(solution)/shard_map/ppermute | solution.py:472
  51.7 4.1 %shard_map.106._.refs_4_ = bf16[2,96,96,128]{3,2,1,0:T(8,128)(2,1)} custom-call(bf16[2,12,96,128]{3,2,1,0:T(8,128)(2,1)} %get-tuple-element.47.refs_0_, bf16[2,12,96,128]{3,2,1,0:T(8,128)(2,1)} %get-tuple-element.48.refs_1_, bf16[2,12,96,1024]{3,2,1,0:T(8,128)(2,1)} %get-tuple-element.41.n_ref.refs_2_, bf16[16,128]{1,0:T(8,128)(2,1)} %bitcast.8), custom_call_target="tpu_custom_call" | custom-call | flops 2000000000 | bytes 5000000 | tf_op jit(solution)/shard_map/pallas_call | solution.py:403
  55.8 2.9 %collective-permute-done.2.more_ref = bf16[8,72,128]{2,1,0:T(8,128)(2,1)S(1)} collective-permute-done((bf16[8,72,128]{2,1,0:T(8,128)(2,1)S(1)}, bf16[8,72,128]{2,1,0:T(8,128)(2,1)S(1)}, u32[]{:S(2)}, u32[]{:S(2)}) %collective-permute-start.2) | collective-permute-done | bytes 147488 | tf_op jit(solution)/shard_map/ppermute | solution.py:472
  58.7 0.0 all-to-all-done.1.got_ref
  58.7 0.7 shard_map.107
  59.4 3.4 %all-to-all-start.2 = ((bf16[8,88,128]{2,1,0:T(8,128)(2,1)}), bf16[8,88,128]{2,1,0:T(8,128)(2,1)S(1)}, u32[]{:S(2)}, u32[]{:S(2)}) async-start(bf16[8,88,128]{2,1,0:T(8,128)(2,1)} %get-tuple-element.51), calls=%async_computation.2 | async-start | bytes 360448 | tf_op jit(solution)/shard_map/all_to_all | solution.py:468
  62.8 0.9 %collective-permute-start.3 = (f32[16,256]{1,0:T(8,128)S(1)}, f32[16,256]{1,0:T(8,128)S(1)}, u32[]{:S(2)}, u32[]{:S(2)}) collective-permute-start(f32[16,256]{1,0:T(8,128)S(1)} %get-tuple-element.50), channel_id=1, source_target_pairs={{0,16},{16,0},{32,48},{48,32},{64,80},{80,64},{96,112},{112,96},{1... | collective-permute-start | bytes 49160 | tf_op jit(solution)/shard_map/ppermute | solution.py:472
  63.7 4.1 %shard_map.110 = bf16[2,96,96,128]{3,2,1,0:T(8,128)(2,1)} custom-call(bf16[2,12,96,128]{3,2,1,0:T(8,128)(2,1)} %get-tuple-element.47.refs_0_, bf16[2,12,96,128]{3,2,1,0:T(8,128)(2,1)} %get-tuple-element.48.refs_1_, bf16[2,12,96,1024]{3,2,1,0:T(8,128)(2,1)} %get-tuple-element.41.n_ref.refs_2_, ...), custom_call_target="tpu_custom_call", output_to_operand_aliasing={{}: (4, {})} | custom-call | flops 2000000000 | bytes 5000000 | tf_op jit(solution)/shard_map/pallas_call | solution.py:403
  67.8 0.0 collective-permute-done.3.other_ref
  67.8 0.7 shard_map.108
  68.5 4.8 %all-to-all-done.2.got_ref = bf16[8,88,128]{2,1,0:T(8,128)(2,1)S(1)} async-done(((bf16[8,88,128]{2,1,0:T(8,128)(2,1)}), bf16[8,88,128]{2,1,0:T(8,128)(2,1)S(1)}, u32[]{:S(2)}, u32[]{:S(2)}) %all-to-all-start.2) | async-done | bytes 180256 | tf_op jit(solution)/shard_map/all_to_all | solution.py:468
  73.3 0.7 shard_map.109
Async XLA Ops:
  0.6 20.7 %collective-permute-start = (bf16[2,96,384]{2,1,0:T(8,128)(2,1)}, bf16[2,96,384]{2,1,0:T(8,128)(2,1)S(1)}, u32[]{:S(2)}, u32[]{:S(2)}) collective-permute-start(bf16[2,96,384]{2,1,0:T(8,128)(2,1)} %param.7), channel_id=1, source_target_pairs={{0,80},{1,128},{2,176},{3,144},{4,32},{5,160},{6,112},{7,48},{8,22... | collective-permute-start | bytes 442376 | tf_op jit(solution)/shard_map/ppermute | solution.py:477
  7.3 14.0 %collective-permute-start.1 = (bf16[2,96,384]{2,1,0:T(8,128)(2,1)}, bf16[2,96,384]{2,1,0:T(8,128)(2,1)S(1)}, u32[]{:S(2)}, u32[]{:S(2)}) collective-permute-start(bf16[2,96,384]{2,1,0:T(8,128)(2,1)} %param.8), channel_id=1, source_target_pairs={{0,80},{1,128},{2,176},{3,144},{4,32},{5,160},{6,112},{7,48},{8,22... | collective-permute-start | bytes 442376 | tf_op jit(solution)/shard_map/ppermute | solution.py:478
  11.7 8.0 %copy-start.1 = (bf16[2,96,384]{2,1,0:T(8,128)(2,1)S(1)}, bf16[2,96,384]{2,1,0:T(8,128)(2,1)}, u32[]{:S(2)}) copy-start(bf16[2,96,384]{2,1,0:T(8,128)(2,1)} %q_ref.3) | copy-start | bytes 442372
  11.7 8.0 %copy-start.2 = (bf16[2,96,384]{2,1,0:T(8,128)(2,1)S(1)}, bf16[2,96,384]{2,1,0:T(8,128)(2,1)}, u32[]{:S(2)}) copy-start(bf16[2,96,384]{2,1,0:T(8,128)(2,1)} %g_ref.3) | copy-start | bytes 442372
  21.4 14.0 %copy-start = (bf16[2,12,96,1024]{3,2,1,0:T(8,128)(2,1)S(1)}, bf16[2,12,96,1024]{3,2,1,0:T(8,128)(2,1)}, u32[]{:S(2)}) copy-start(bf16[2,12,96,1024]{3,2,1,0:T(8,128)(2,1)} %get-tuple-element.41.n_ref.refs_2_) | copy-start | bytes 14155780
  39.6 19.1 %all-to-all-start.1 = ((bf16[32,24,256]{2,1,0:T(8,128)(2,1)}), bf16[32,24,256]{2,1,0:T(8,128)(2,1)S(1)}, u32[]{:S(2)}, u32[]{:S(2)}) async-start(bf16[32,24,256]{2,1,0:T(8,128)(2,1)} %get-tuple-element.42), calls=%async_computation.1 | async-start | bytes 786432 | tf_op jit(solution)/shard_map/all_to_all | solution.py:468
  50.5 8.3 %collective-permute-start.2 = (bf16[8,72,128]{2,1,0:T(8,128)(2,1)S(1)}, bf16[8,72,128]{2,1,0:T(8,128)(2,1)S(1)}, u32[]{:S(2)}, u32[]{:S(2)}) collective-permute-start(bf16[8,72,128]{2,1,0:T(8,128)(2,1)S(1)} %get-tuple-element.46), channel_id=1, source_target_pairs={{0,16},{16,0},{32,48},{48,32},{64,80},{80,64},{96,112},{112,96},{1... | collective-permute-start | bytes 442376 | tf_op jit(solution)/shard_map/ppermute | solution.py:472
  59.4 13.9 %all-to-all-start.2 = ((bf16[8,88,128]{2,1,0:T(8,128)(2,1)}), bf16[8,88,128]{2,1,0:T(8,128)(2,1)S(1)}, u32[]{:S(2)}, u32[]{:S(2)}) async-start(bf16[8,88,128]{2,1,0:T(8,128)(2,1)} %get-tuple-element.51), calls=%async_computation.2 | async-start | bytes 360448 | tf_op jit(solution)/shard_map/all_to_all | solution.py:468
  62.8 5.0 %collective-permute-start.3 = (f32[16,256]{1,0:T(8,128)S(1)}, f32[16,256]{1,0:T(8,128)S(1)}, u32[]{:S(2)}, u32[]{:S(2)}) collective-permute-start(f32[16,256]{1,0:T(8,128)S(1)} %get-tuple-element.50), channel_id=1, source_target_pairs={{0,16},{16,0},{32,48},{48,32},{64,80},{80,64},{96,112},{112,96},{1... | collective-permute-start | bytes 49160 | tf_op jit(solution)/shard_map/ppermute | solution.py:472

commit v5 on v4

--- a/solution.py
+++ b/solution.py
@@ -79,7 +79,9 @@
     turn_ref[...] = jnp.where(used, 1.0, 0.0).astype(BF16)
 
 
-def norm_kernel(groups, pair_ref, wt_ref, n_ref, bias_ref, inv_ref, ones_ref, diag_ref):
+def norm_kernel(
+    groups, pair_ref, wt_ref, n_ref, bias_ref, low_bias_ref, inv_ref, ones_ref, diag_ref
+):
     first = (pl.program_id(0) == 0) & (pl.program_id(1) == 0)
 
     @pl.when(first)
@@ -112,8 +114,10 @@
                 lane_query == 2 * p + k, inverse[:, k * CP : (k + 1) * CP], compact
             )
         bias = bias + dot(normed, diag_ref[:, p * 256 : (p + 1) * 256], NT)
-    inv_ref[0] = compact.reshape(groups, T, 128)
-    bias_ref[0] = bias.reshape(groups, T, 128)
+    inv_ref[0] = compact.reshape(groups, T, 128).astype(BF16)
+    bias = bias.reshape(groups, T, 128)
+    bias_ref[0] = bias
+    low_bias_ref[0] = (bias * (1.0 / CP)).astype(BF16)
 
 
 def logits_kernel(k_ref, v_ref, qt_ref, gt_ref, bias_ref, logits_ref, dw_ref, stats_ref):
@@ -155,12 +159,13 @@
 
 
 def scores_kernel(
-    stats_ref, logits_ref, dw_ref, bias_ref, inv_ref, k_ref, pick_ref, turn_ref, n_ref,
-    four_out, w_out, scaled_out, along_out, send_ref,
-    ds_ref, four_ref, w_ref, scaled_ref, along_ref, sems,
+    stats_ref, logits_ref, dw_ref, k_ref, pick_ref, turn_ref, n_ref,
+    four_out, w_out, ds_out, send_ref,
+    ds_ref, four_ref, w_ref, sems,
 ):
     keep = iota((128, HC), 0) >> 5 == (iota((128, HC), 1) & 3)
-    chosen = []
+    pairs = ((four_ref, four_out), (w_ref, w_out), (ds_ref, ds_out))
+    stores = []
     for b in range(B):
         levels = stats_ref[:, b * 2 * G : b * 2 * G + G, :]
         balances = stats_ref[:, b * 2 * G + G : (b + 1) * 2 * G, :]
@@ -172,34 +177,30 @@
         lows = []
         for g in range(G):
             weights = jnp.exp(logits_ref[b, g] - level[g : g + 1])
-            ds = weights * (dw_ref[b, g] - balance[g : g + 1])
-            low = ds.astype(BF16)
-            at = slice(g * 128, (g + 1) * 128)
-            ds_ref[b, :, at] = low
-            w_ref[b, :, at] = weights.astype(BF16)
-            low = low.astype(F32)
-            lows.append(low)
-            scaled = low * inv_ref[b, g]
-            scaled_ref[b, g] = scaled.astype(BF16)
-            along_ref[b, g] = (scaled * bias_ref[b, g] * (1.0 / CP)).astype(BF16)
+            low = (weights * (dw_ref[b, g] - balance[g : g + 1])).astype(BF16)
+            ds_ref[b, g] = low
+            w_ref[b, g] = weights.astype(BF16)
+            lows.append(low.astype(F32))
+        for q in range(4):
+            four_ref[b, q] = four_heads(lows, q)
+        for i, (x, y) in enumerate(pairs):
+            store = pltpu.make_async_copy(x.at[b], y.at[b], sems.at[b * 3 + i])
+            store.start()
+            stores.append(store)
+
+    chosen = []
+    for b in range(B):
         k_turned = dot(turn_ref[...], k_ref[b], NT).astype(BF16)
         quarters = []
         for q in range(4):
-            four = four_heads(lows, q)
-            four_ref[b, q] = four
-            spread = dot(k_turned[q * 128 : (q + 1) * 128], four)
+            spread = dot(k_turned[q * 128 : (q + 1) * 128], four_ref[b, q])
             quarters.append(jnp.where(keep, spread, 0.0).astype(BF16))
         chosen.append(jnp.concatenate(quarters, axis=0))
-    pairs = ((four_ref, four_out), (w_ref, w_out), (scaled_ref, scaled_out), (along_ref, along_out))
-    stores = [pltpu.make_async_copy(x, y, sems.at[i]) for i, (x, y) in enumerate(pairs)]
-    for store in stores:
-        store.start()
     queries = dot(jnp.concatenate(chosen, axis=1), pick_ref[...], NT) * SCALE
 
     total = jnp.zeros((128, WIDE), F32)
     for b in range(B):
-        left = jnp.concatenate([ds_ref[b, :, g * 128 : (g + 1) * 128] for g in range(G)], axis=0)
-        total = total + dot(left, n_ref[b].reshape(G * T, WIDE), TN)
+        total = total + dot(ds_ref[b].reshape(G * T, 128), n_ref[b].reshape(G * T, WIDE), TN)
     dwt = jnp.zeros((H, CP), F32)
     for i in range(I8):
         dwt = dwt + total[i * H : (i + 1) * H, i * CP : (i + 1) * CP]
@@ -230,7 +231,7 @@
     keys, values = [], []
     for b in range(B):
         keys.append(gather(select(q_ref[b]), [four_ref[b, q] for q in range(4)]) * SCALE)
-        parts = [w_ref[b, :, g * 128 : (g + 1) * 128].astype(F32) for g in range(G)]
+        parts = [w_ref[b, g].astype(F32) for g in range(G)]
         values.append(gather(select(g_ref[b]), [four_heads(parts, q) for q in range(4)]))
     kv = jnp.concatenate(keys + values, axis=1)
     for h in range(H):
@@ -242,7 +243,9 @@
         give_ref[z] = all_ref[2 * z + 1 - y_lo].astype(BF16)
 
 
-def pair_kernel(groups, scaled_ref, along_ref, n_ref, wt_ref, _, out_ref, ones_ref, diag_ref):
+def pair_kernel(
+    groups, ds_ref, inv_ref, bias_ref, n_ref, wt_ref, _, out_ref, ones_ref, diag_ref
+):
     first = pl.program_id(0) == 0
 
     @pl.when(first)
@@ -253,8 +256,9 @@
         diag_ref[...] = block_diagonal(jnp.concatenate([wt] * I8, axis=0), H).astype(BF16)
 
     rows = groups * T
-    scaled = scaled_ref[0].reshape(rows, 128)
-    along = along_ref[0].reshape(rows, 128)
+    scaled = ds_ref[0].astype(F32) * inv_ref[0].astype(F32)
+    along = (scaled * bias_ref[0].astype(F32)).astype(BF16).reshape(rows, 128)
+    scaled = scaled.astype(BF16).reshape(rows, 128)
     for p in range(I8 // 2):
         at = slice(p * 256, (p + 1) * 256)
         back = dot(scaled, diag_ref[:, at])
@@ -322,6 +326,10 @@
     return pltpu.with_memory_space_constraint(x, pltpu.HBM)
 
 
+WHOLE = pl.BlockSpec(memory_space=pltpu.VMEM)
+SCALAR = pl.BlockSpec(memory_space=pltpu.SMEM)
+
+
 def expanded(query, grad):
     shape = bf16(B, HC, QH)
     outs = [shape, shape, bf16(256, B * HC), bf16(2 * H * 16, HC)]
@@ -333,7 +341,7 @@
     spec = lambda *tail: pl.BlockSpec((1, groups, T) + tail, lambda b, s: (b, s, 0, 0))
     return call(
         lambda *refs: norm_kernel(groups, *refs),
-        [far(B, G, T, WIDE), f32(B, G, T, 128), f32(B, G, T, 128)],
+        [far(B, G, T, WIDE), f32(B, G, T, 128), far(B, G, T, 128), far(B, G, T, 128)],
         24,
         flops=4_000_000_000,
         moved=12_000_000,
@@ -342,7 +350,7 @@
             pl.BlockSpec((1, groups * I8, T, CP), lambda b, s: (b, s, 0, 0)),
             pl.BlockSpec((H, CP), lambda b, s: (0, 0)),
         ],
-        out_specs=[spec(WIDE), spec(128), spec(128)],
+        out_specs=[spec(WIDE), spec(128), spec(128), spec(128)],
         scratch_shapes=[pltpu.VMEM((256, 256), BF16), pltpu.VMEM((128, WIDE), BF16)],
     )(in_hbm(pair), in_hbm(wt))
 
@@ -355,32 +363,23 @@
 
 
 def scores(*args):
-    low = far(B, T, QH)
-    four = far(B, 4, T, HC)
     cell = far(B, G, T, 128)
-    whole = pl.BlockSpec(memory_space=pltpu.VMEM)
     hbm = pl.BlockSpec(memory_space=pltpu.HBM)
     return call(
         scores_kernel,
-        [four, low, cell, cell, bf16(PLANE, 24, 256)],
+        [far(B, 4, T, HC), cell, cell, bf16(PLANE, 24, 256)],
         24,
         flops=2_500_000_000,
         moved=8_000_000,
-        in_specs=[whole] * 9,
-        out_specs=[hbm] * 4 + [whole],
+        in_specs=[WHOLE] * 7,
+        out_specs=[hbm] * 3 + [WHOLE],
         scratch_shapes=[
-            pltpu.VMEM((B, T, QH), BF16),
+            pltpu.VMEM((B, G, T, 128), BF16),
             pltpu.VMEM((B, 4, T, HC), BF16),
-            pltpu.VMEM((B, T, QH), BF16),
             pltpu.VMEM((B, G, T, 128), BF16),
-            pltpu.VMEM((B, G, T, 128), BF16),
-            pltpu.SemaphoreType.DMA((4,)),
+            pltpu.SemaphoreType.DMA((3 * B,)),
         ],
     )(*args)
-
-
-WHOLE = pl.BlockSpec(memory_space=pltpu.VMEM)
-SCALAR = pl.BlockSpec(memory_space=pltpu.SMEM)
 
 
 def grads(side, *args):
@@ -396,23 +395,23 @@
     )(side, *[in_hbm(x) for x in args])
 
 
-def pair_grad(b, scaled, along, n, wt, done):
+def pair_grad(b, ds, inv, bias, n, wt, done):
     groups = GROUPS
     spec = lambda *tail: pl.BlockSpec((1, groups, T) + tail, lambda s: (b, s, 0, 0))
     fresh = done is None
     return call(
-        lambda *refs: pair_kernel(groups, *(refs if not fresh else refs[:4] + (None,) + refs[4:])),
+        lambda *refs: pair_kernel(groups, *(refs if not fresh else refs[:5] + (None,) + refs[5:])),
         [far(B, T, T, CP)],
         24,
         flops=2_000_000_000,
         moved=5_000_000,
         grid=(G // groups,),
-        in_specs=[spec(128), spec(128), spec(WIDE), pl.BlockSpec((H, CP), lambda s: (0, 0))]
+        in_specs=[spec(128)] * 3 + [spec(WIDE), pl.BlockSpec((H, CP), lambda s: (0, 0))]
         + ([] if fresh else [pl.BlockSpec(memory_space=pltpu.HBM)]),
         out_specs=[pl.BlockSpec((1, groups * I8, T, CP), lambda s: (b, s, 0, 0))],
         scratch_shapes=[pltpu.VMEM((128, WIDE), BF16), pltpu.VMEM((128, WIDE), BF16)],
-        **({} if fresh else dict(input_output_aliases={4: 0})),
-    )(in_hbm(scaled), in_hbm(along), in_hbm(n), in_hbm(wt), *([] if fresh else [done]))[0]
+        **({} if fresh else dict(input_output_aliases={5: 0})),
+    )(*[in_hbm(x) for x in (ds, inv, bias, n, wt)], *([] if fresh else [done]))[0]
 
 
 def bias_out(side, got, keep, more, after):
@@ -480,21 +479,19 @@
     side = (lax.axis_index("row") & 1).astype(jnp.int32).reshape(1)
     qt, gt, pick, turn = expanded(query_in, d_out)
     side, qt = lax.optimization_barrier((side, qt))
-    n, bias, inv = norm(pair, wt)
+    n, bias, low_bias, inv = norm(pair, wt)
     scaled_scores, dw, stats = logits(k, v, qt, gt, bias)
     stats = spread_over(stats, "col")
-    ds, w, scaled, along, send = scores(
-        stats, scaled_scores, dw, bias, inv, k, pick, turn, n
-    )
+    four, w, ds, send = scores(stats, scaled_scores, dw, k, pick, turn, n)
     planes = [list(range(z * PLANE, (z + 1) * PLANE)) for z in range(DEPTH)]
     got = spread_over(send, ("row", "col"), planes)
-    keep, give = grads(side, ds, w, query_in, d_out)
-    d_pair = pair_grad(0, scaled, along, n, wt, None)
+    keep, give = grads(side, four, w, query_in, d_out)
+    d_pair = pair_grad(0, ds, inv, low_bias, n, wt, None)
     send, own, other = bias_out(side, got, keep, swap_y(give), d_pair)
     lines = [list(range(y, PEERS, 2)) for y in range(2)]
     got = spread_over(send, "row", lines)
     d_query = queries_out(side, own, swap_y(other))
-    d_pair = pair_grad(1, scaled, along, n, wt, d_pair)
+    d_pair = pair_grad(1, ds, inv, low_bias, n, wt, d_pair)
     d_key, d_value, dwt = keys_out(got)
     flip = lambda x: jnp.swapaxes(x, 1, 2)
     return flip(d_query), flip(d_key), flip(d_value), d_pair, dwt.T

time: 74.5 us -> 73.3 us (0.984)
  Pallas kernels: 27.9 us -> 26.9 us
    pallas_call x3, Pallas kernels: 12.5 us -> 11.2 us  [the longest x2 8.39 us: pair_grad(): call(lambda *refs: pair_kernel(groups, *(refs if not fresh else refs[:5]...]
  transfers between devices with their start and end apart: 6 -> 6, of which waited for: 2 -> 2; matrix products, arithmetic and copies ran while one was open for 0% -> 0% of each run, Pallas kernels for 29% -> 30%
where the time goes in v5:
time: 73.3 us; the launch traced here: 72.9 us
  Pallas kernels  26.9 us (37%)
  starting transfers between devices  24.9 us (34%)
  blocking collectives  12.9 us (18%)
  waiting for transfers between devices  7.5 us (10%)
    all_to_all x1, blocking collectives, spread_over(): return lax.all_to_all(x, axis, 0, 0, tiled=True, axis_index_groups=groups)  12.9 us
    all_to_all x2, starting transfers between devices, spread_over(): return lax.all_to_all(x, axis, 0, 0, tiled=True, axis_index_groups=groups)  11.6 us
    pallas_call x2, Pallas kernels, pair_grad(): call(lambda *refs: pair_kernel(groups, *(refs if not fresh else refs[:5]...  8.39 us
    pallas_call x1, Pallas kernels, norm(): call(lambda *refs: norm_kernel(groups, *refs), [far(B, G, T, WIDE), f32(B...  8.18 us
    ppermute x1, starting transfers between devices, shards(): k = lax.ppermute(key_in, ('row', 'col'), route)  6.72 us
    all_to_all x2, waiting for transfers between devices, spread_over(): return lax.all_to_all(x, axis, 0, 0, tiled=True, axis_index_groups=groups)  4.68 us
    ppermute x1, starting transfers between devices, shards(): v = lax.ppermute(value_in, ('row', 'col'), route)  4.38 us
    pallas_call x1, Pallas kernels, scores(): call(scores_kernel, [far(B, 4, T, HC), cell, cell, bf16(PLANE, 24, 256)],...  2.85 us
  transfers between devices with their start and end apart: 6, of which 2 were waited for; matrix products, arithmetic and copies ran while one was open for 0% of the time, Pallas kernels for 30%

profile of v5, /device:TPU:16, one launch (start us, length us, event | category | flops | bytes accessed | tf_op | source)
XLA Modules:
  0.0 72.9 jit_solution(8417601825119447682)
XLA Ops:
  0.6 6.7 %collective-permute-start = (bf16[2,96,384]{2,1,0:T(8,128)(2,1)}, bf16[2,96,384]{2,1,0:T(8,128)(2,1)S(1)}, u32[]{:S(2)}, u32[]{:S(2)}) collective-permute-start(bf16[2,96,384]{2,1,0:T(8,128)(2,1)} %param.7), channel_id=1, source_target_pairs={{0,80},{1,128},{2,176},{3,144},{4,32},{5,160},{6,112},{7,48},{8,22... | collective-permute-start | bytes 442376 | tf_op jit(solution)/shard_map/ppermute | solution.py:476
  7.3 4.4 %collective-permute-start.1 = (bf16[2,96,384]{2,1,0:T(8,128)(2,1)}, bf16[2,96,384]{2,1,0:T(8,128)(2,1)S(1)}, u32[]{:S(2)}, u32[]{:S(2)}) collective-permute-start(bf16[2,96,384]{2,1,0:T(8,128)(2,1)} %param.8), channel_id=1, source_target_pairs={{0,80},{1,128},{2,176},{3,144},{4,32},{5,160},{6,112},{7,48},{8,22... | collective-permute-start | bytes 442376 | tf_op jit(solution)/shard_map/ppermute | solution.py:477
  11.7 0.0 copy-start.1
  11.7 0.0 copy-start.2
  11.7 8.2 %shard_map.102 = (bf16[2,12,96,1024]{3,2,1,0:T(8,128)(2,1)}, f32[2,12,96,128]{3,2,1,0:T(8,128)S(1)}, bf16[2,12,96,128]{3,2,1,0:T(8,128)(2,1)}, bf16[2,12,96,128]{3,2,1,0:T(8,128)(2,1)}) custom-call(bf16[2,96,96,128]{3,2,1,0:T(8,128)(2,1)} %refs_0_.1, bf16[16,128]{1,0:T(8,128)(2,1)} %bitcast.7), custom_call_target="tpu_custom_call" | custom-call | flops 4000000000 | bytes 12000000 | tf_op jit(solution)/shard_map/pallas_call | solution.py:342
  19.9 0.0 copy-done.1
  19.9 0.0 copy-done.2
  19.9 1.6 %shard_map.101 = (bf16[2,384,1536]{2,1,0:T(8,128)(2,1)S(1)}, bf16[2,384,1536]{2,1,0:T(8,128)(2,1)S(1)}, bf16[256,768]{1,0:T(8,128)(2,1)S(1)}, bf16[512,384]{1,0:T(8,128)(2,1)S(1)}) custom-call(bf16[2,96,384]{2,1,0:T(8,128)(2,1)S(1)} %copy-done.1, bf16[2,96,384]{2,1,0:T(8,128)(2,1)S(1)} %copy-done.2), custom_call_target="tpu_custom_call" | custom-call | flops 400000000 | bytes 5000000 | tf_op jit(solution)/shard_map/pallas_call | solution.py:336
  21.6 0.0 collective-permute-done.k_ref
  21.6 0.0 collective-permute-done.1.v_ref
  21.6 0.0 copy-start
  21.6 1.1 %shard_map.103 = (f32[2,12,96,128]{3,2,1,0:T(8,128)S(1)}, f32[2,12,96,128]{3,2,1,0:T(8,128)S(1)}, f32[16,48,128]{2,1,0:T(8,128)S(1)}) custom-call(bf16[2,96,384]{2,1,0:T(8,128)(2,1)S(1)} %collective-permute-done.k_ref, bf16[2,96,384]{2,1,0:T(8,128)(2,1)S(1)} %collective-permute-done.1.v_ref, bf16[2,384,1536]{2,1,0:T(8,128)(2,1)S(1)} %get-tuple-element.32.qt_ref, ...), custom_call_target="tpu_custom_call" | custom-call | flops 1000000000 | bytes 8000000 | tf_op jit(solution)/shard_map/pallas_call | solution.py:360
  22.7 12.9 %all_to_all.15.stats_ref = f32[16,48,128]{2,1,0:T(8,128)S(1)} all-to-all(f32[16,48,128]{2,1,0:T(8,128)S(1)} %get-tuple-element.35), channel_id=1, replica_groups=mesh['row'=16,'col'=16] {'col'}, dimensions={0} | all-to-all | bytes 786432 | tf_op jit(solution)/shard_map/all_to_all | solution.py:467
  35.6 0.0 copy-done
  35.6 2.9 %shard_map.104 = (bf16[2,4,96,384]{3,2,1,0:T(8,128)(2,1)}, bf16[2,12,96,128]{3,2,1,0:T(8,128)(2,1)}, bf16[2,12,96,128]{3,2,1,0:T(8,128)(2,1)}, bf16[32,24,256]{2,1,0:T(8,128)(2,1)}) custom-call(f32[16,48,128]{2,1,0:T(8,128)S(1)} %all_to_all.15.stats_ref, f32[2,12,96,128]{3,2,1,0:T(8,128)S(1)} %get-tuple-element.36.logits_ref, ...), custom_call_target="tpu_custom_call" | custom-call | flops 2500000000 | bytes 8000000 | tf_op jit(solution)/shard_map/pallas_call | solution.py:368
  38.4 8.2 %all-to-all-start.1 = ((bf16[32,24,256]{2,1,0:T(8,128)(2,1)}), bf16[32,24,256]{2,1,0:T(8,128)(2,1)S(1)}, u32[]{:S(2)}, u32[]{:S(2)}) async-start(bf16[32,24,256]{2,1,0:T(8,128)(2,1)} %get-tuple-element.41), calls=%async_computation.1 | async-start | bytes 786432 | tf_op jit(solution)/shard_map/all_to_all | solution.py:467
  46.6 2.7 %shard_map.105 = (bf16[8,72,128]{2,1,0:T(8,128)(2,1)S(1)}, bf16[8,72,128]{2,1,0:T(8,128)(2,1)S(1)}) custom-call(s32[1]{0:T(128)} %bitcast.side_ref, bf16[2,4,96,384]{3,2,1,0:T(8,128)(2,1)} %get-tuple-element.42.four_ref, bf16[2,12,96,128]{3,2,1,0:T(8,128)(2,1)} %get-tuple-element.43.w_ref, bf16[2,96,384]{2,1,0:T(8,128)(2,1)} %q_ref.3, bf16[2,96,384]{2,1,0:T(8,128)(2,1)} %g_ref.3), custom_call_target="tpu_custom_call" | custom-call | flops 2500000000 | bytes 8000000 | tf_op jit(solution)/shard_map/pallas_call | solution.py:387
  49.3 1.3 %collective-permute-start.2 = (bf16[8,72,128]{2,1,0:T(8,128)(2,1)S(1)}, bf16[8,72,128]{2,1,0:T(8,128)(2,1)S(1)}, u32[]{:S(2)}, u32[]{:S(2)}) collective-permute-start(bf16[8,72,128]{2,1,0:T(8,128)(2,1)S(1)} %get-tuple-element.45), channel_id=1, source_target_pairs={{0,16},{16,0},{32,48},{48,32},{64,80},{80,64},{96,112},{112,96},{1... | collective-permute-start | bytes 442376 | tf_op jit(solution)/shard_map/ppermute | solution.py:471
  50.6 4.2 %shard_map.106._.refs_5_ = bf16[2,96,96,128]{3,2,1,0:T(8,128)(2,1)} custom-call(bf16[2,12,96,128]{3,2,1,0:T(8,128)(2,1)} %get-tuple-element.46.refs_0_, bf16[2,12,96,128]{3,2,1,0:T(8,128)(2,1)} %get-tuple-element.47.refs_1_, bf16[2,12,96,128]{3,2,1,0:T(8,128)(2,1)} %get-tuple-element.48.refs_2_, bf16[2,12,96,1024]{3,2,1,0:T(8,128)(2,1)} %get-tuple-element.40.n_ref.refs_3_, ...), custom_call_target="tpu_custom_call" | custom-call | flops 2000000000 | bytes 5000000 | tf_op jit(solution)/shard_map/pallas_call | solution.py:402
  54.8 2.8 %collective-permute-done.2.more_ref = bf16[8,72,128]{2,1,0:T(8,128)(2,1)S(1)} collective-permute-done((bf16[8,72,128]{2,1,0:T(8,128)(2,1)S(1)}, bf16[8,72,128]{2,1,0:T(8,128)(2,1)S(1)}, u32[]{:S(2)}, u32[]{:S(2)}) %collective-permute-start.2) | collective-permute-done | bytes 147488 | tf_op jit(solution)/shard_map/ppermute | solution.py:471
  57.6 0.0 all-to-all-done.1.got_ref
  57.6 0.7 shard_map.107
  58.3 3.4 %all-to-all-start.2 = ((bf16[8,88,128]{2,1,0:T(8,128)(2,1)}), bf16[8,88,128]{2,1,0:T(8,128)(2,1)S(1)}, u32[]{:S(2)}, u32[]{:S(2)}) async-start(bf16[8,88,128]{2,1,0:T(8,128)(2,1)} %get-tuple-element.51), calls=%async_computation.2 | async-start | bytes 360448 | tf_op jit(solution)/shard_map/all_to_all | solution.py:467
  61.7 0.9 %collective-permute-start.3 = (f32[16,256]{1,0:T(8,128)S(1)}, f32[16,256]{1,0:T(8,128)S(1)}, u32[]{:S(2)}, u32[]{:S(2)}) collective-permute-start(f32[16,256]{1,0:T(8,128)S(1)} %get-tuple-element.50), channel_id=1, source_target_pairs={{0,16},{16,0},{32,48},{48,32},{64,80},{80,64},{96,112},{112,96},{1... | collective-permute-start | bytes 49160 | tf_op jit(solution)/shard_map/ppermute | solution.py:471
  62.6 4.2 %shard_map.110 = bf16[2,96,96,128]{3,2,1,0:T(8,128)(2,1)} custom-call(bf16[2,12,96,128]{3,2,1,0:T(8,128)(2,1)} %get-tuple-element.46.refs_0_, bf16[2,12,96,128]{3,2,1,0:T(8,128)(2,1)} %get-tuple-element.47.refs_1_, bf16[2,12,96,128]{3,2,1,0:T(8,128)(2,1)} %get-tuple-element.48.refs_2_, ...), custom_call_target="tpu_custom_call", output_to_operand_aliasing={{}: (5, {})} | custom-call | flops 2000000000 | bytes 5000000 | tf_op jit(solution)/shard_map/pallas_call | solution.py:402
  66.8 0.0 collective-permute-done.3.other_ref
  66.8 0.7 shard_map.108
  67.5 4.7 %all-to-all-done.2.got_ref = bf16[8,88,128]{2,1,0:T(8,128)(2,1)S(1)} async-done(((bf16[8,88,128]{2,1,0:T(8,128)(2,1)}), bf16[8,88,128]{2,1,0:T(8,128)(2,1)S(1)}, u32[]{:S(2)}, u32[]{:S(2)}) %all-to-all-start.2) | async-done | bytes 180256 | tf_op jit(solution)/shard_map/all_to_all | solution.py:467
  72.1 0.7 shard_map.109
Async XLA Ops:
  0.6 20.9 %collective-permute-start = (bf16[2,96,384]{2,1,0:T(8,128)(2,1)}, bf16[2,96,384]{2,1,0:T(8,128)(2,1)S(1)}, u32[]{:S(2)}, u32[]{:S(2)}) collective-permute-start(bf16[2,96,384]{2,1,0:T(8,128)(2,1)} %param.7), channel_id=1, source_target_pairs={{0,80},{1,128},{2,176},{3,144},{4,32},{5,160},{6,112},{7,48},{8,22... | collective-permute-start | bytes 442376 | tf_op jit(solution)/shard_map/ppermute | solution.py:476
  7.3 14.2 %collective-permute-start.1 = (bf16[2,96,384]{2,1,0:T(8,128)(2,1)}, bf16[2,96,384]{2,1,0:T(8,128)(2,1)S(1)}, u32[]{:S(2)}, u32[]{:S(2)}) collective-permute-start(bf16[2,96,384]{2,1,0:T(8,128)(2,1)} %param.8), channel_id=1, source_target_pairs={{0,80},{1,128},{2,176},{3,144},{4,32},{5,160},{6,112},{7,48},{8,22... | collective-permute-start | bytes 442376 | tf_op jit(solution)/shard_map/ppermute | solution.py:477
  11.7 8.2 %copy-start.1 = (bf16[2,96,384]{2,1,0:T(8,128)(2,1)S(1)}, bf16[2,96,384]{2,1,0:T(8,128)(2,1)}, u32[]{:S(2)}) copy-start(bf16[2,96,384]{2,1,0:T(8,128)(2,1)} %q_ref.3) | copy-start | bytes 442372
  11.7 8.2 %copy-start.2 = (bf16[2,96,384]{2,1,0:T(8,128)(2,1)S(1)}, bf16[2,96,384]{2,1,0:T(8,128)(2,1)}, u32[]{:S(2)}) copy-start(bf16[2,96,384]{2,1,0:T(8,128)(2,1)} %g_ref.3) | copy-start | bytes 442372
  21.6 14.0 %copy-start = (bf16[2,12,96,1024]{3,2,1,0:T(8,128)(2,1)S(1)}, bf16[2,12,96,1024]{3,2,1,0:T(8,128)(2,1)}, u32[]{:S(2)}) copy-start(bf16[2,12,96,1024]{3,2,1,0:T(8,128)(2,1)} %get-tuple-element.40.n_ref.refs_3_) | copy-start | bytes 14155780
  38.4 19.1 %all-to-all-start.1 = ((bf16[32,24,256]{2,1,0:T(8,128)(2,1)}), bf16[32,24,256]{2,1,0:T(8,128)(2,1)S(1)}, u32[]{:S(2)}, u32[]{:S(2)}) async-start(bf16[32,24,256]{2,1,0:T(8,128)(2,1)} %get-tuple-element.41), calls=%async_computation.1 | async-start | bytes 786432 | tf_op jit(solution)/shard_map/all_to_all | solution.py:467
  49.3 8.3 %collective-permute-start.2 = (bf16[8,72,128]{2,1,0:T(8,128)(2,1)S(1)}, bf16[8,72,128]{2,1,0:T(8,128)(2,1)S(1)}, u32[]{:S(2)}, u32[]{:S(2)}) collective-permute-start(bf16[8,72,128]{2,1,0:T(8,128)(2,1)S(1)} %get-tuple-element.45), channel_id=1, source_target_pairs={{0,16},{16,0},{32,48},{48,32},{64,80},{80,64},{96,112},{112,96},{1... | collective-permute-start | bytes 442376 | tf_op jit(solution)/shard_map/ppermute | solution.py:471
  58.3 13.8 %all-to-all-start.2 = ((bf16[8,88,128]{2,1,0:T(8,128)(2,1)}), bf16[8,88,128]{2,1,0:T(8,128)(2,1)S(1)}, u32[]{:S(2)}, u32[]{:S(2)}) async-start(bf16[8,88,128]{2,1,0:T(8,128)(2,1)} %get-tuple-element.51), calls=%async_computation.2 | async-start | bytes 360448 | tf_op jit(solution)/shard_map/all_to_all | solution.py:467
  61.7 5.1 %collective-permute-start.3 = (f32[16,256]{1,0:T(8,128)S(1)}, f32[16,256]{1,0:T(8,128)S(1)}, u32[]{:S(2)}, u32[]{:S(2)}) collective-permute-start(f32[16,256]{1,0:T(8,128)S(1)} %get-tuple-element.50), channel_id=1, source_target_pairs={{0,16},{16,0},{32,48},{48,32},{64,80},{80,64},{96,112},{112,96},{1... | collective-permute-start | bytes 49160 | tf_op jit(solution)/shard_map/ppermute | solution.py:471

commit v6 on v5

--- a/solution.py
+++ b/solution.py
@@ -72,11 +72,8 @@
     batch = jnp.where(lane >= HC, 1, 0)
     within = lane - batch * HC
     query = (within >> 7) * 32 + (within >> 2 & 3) * I8 + (within >> 4 & 7)
-    pick_ref[...] = jnp.where(iota((256, B * HC), 0) == batch * T + query, 1.0, 0.0).astype(BF16)
-    row = iota((2 * H * 16, HC), 0)
-    feature = (row >> 5) * C + (row >> 4 & 1) * 12 + (row & 15)
-    used = ((row & 15) < 12) & (iota((2 * H * 16, HC), 1) == feature)
-    turn_ref[...] = jnp.where(used, 1.0, 0.0).astype(BF16)
+    pick_ref[...] = jnp.where(iota((256, B * HC), 0) == batch * 128 + query, 1.0, 0.0).astype(BF16)
+    turn_ref[...] = jnp.where(iota((HC, HC), 0) == iota((HC, HC), 1), 1.0, 0.0).astype(BF16)
 
 
 def norm_kernel(
@@ -104,7 +101,11 @@
             ],
             axis=0,
         )
-        centred = x.astype(F32) - dot(x, ones)
+        wide = x.astype(F32)
+        means = [
+            jnp.mean(wide[:, k * CP : (k + 1) * CP], axis=1, keepdims=True) for k in range(2)
+        ]
+        centred = wide - jnp.concatenate([jnp.broadcast_to(m, (rows, CP)) for m in means], axis=1)
         spread = dot((centred * centred).astype(BF16), ones)
         inverse = lax.rsqrt(spread + EPS)
         normed = (centred * inverse).astype(BF16)
@@ -163,7 +164,7 @@
     four_out, w_out, ds_out, send_ref,
     ds_ref, four_ref, w_ref, sems,
 ):
-    keep = iota((128, HC), 0) >> 5 == (iota((128, HC), 1) & 3)
+    keep = (iota((HC // 4, HC), 0) * 171) >> 12 == (iota((HC // 4, HC), 1) & 3)
     pairs = ((four_ref, four_out), (w_ref, w_out), (ds_ref, ds_out))
     stores = []
     for b in range(B):
@@ -193,7 +194,7 @@
         k_turned = dot(turn_ref[...], k_ref[b], NT).astype(BF16)
         quarters = []
         for q in range(4):
-            spread = dot(k_turned[q * 128 : (q + 1) * 128], four_ref[b, q])
+            spread = dot(k_turned[q * HC // 4 : (q + 1) * HC // 4], four_ref[b, q])
             quarters.append(jnp.where(keep, spread, 0.0).astype(BF16))
         chosen.append(jnp.concatenate(quarters, axis=0))
     queries = dot(jnp.concatenate(chosen, axis=1), pick_ref[...], NT) * SCALE
@@ -204,12 +205,10 @@
     dwt = jnp.zeros((H, CP), F32)
     for i in range(I8):
         dwt = dwt + total[i * H : (i + 1) * H, i * CP : (i + 1) * CP]
-    side = jnp.concatenate([dwt[0:8], dwt[8:16]], axis=1)
-    for h in range(H):
-        for half in range(2):
-            at = (2 * h + half) * 16
-            piece = jnp.concatenate([side, queries[at : at + 16]], axis=0)
-            send_ref[half * PEERS + h] = piece.astype(BF16)
+    for half in range(B):
+        for h in range(H):
+            own = queries[h * C : (h + 1) * C, half * 128 : (half + 1) * 128]
+            send_ref[half * PEERS + h] = jnp.concatenate([own, dwt], axis=0).astype(BF16)
     for store in stores:
         store.wait()
 
@@ -270,13 +269,12 @@
 
 
 def bias_out_kernel(side_ref, got_ref, keep_ref, more_ref, _, send_ref, own_ref, other_ref):
-    side = jnp.sum(got_ref[:, 0:8, :].astype(F32), axis=0)
-    dwt = jnp.concatenate([side[:, :CP], side[:, CP:]], axis=0)
+    dwt = jnp.sum(got_ref[:, C : C + H, :].astype(F32), axis=0)
     for z in range(DEPTH):
         kv = keep_ref[z].astype(F32) + more_ref[z].astype(F32)
         send_ref[z] = jnp.concatenate([kv, dwt], axis=0).astype(BF16)
     parts = [
-        jnp.sum(got_ref[y * PEERS : (y + 1) * PEERS, 8:24, :].astype(F32), axis=0) for y in range(2)
+        jnp.sum(got_ref[y * PEERS : (y + 1) * PEERS, 0:C, :].astype(F32), axis=0) for y in range(2)
     ]
     first = side_ref[0] == 0
     own_ref[...] = jnp.where(first, parts[0], parts[1])
@@ -285,10 +283,9 @@
 
 def queries_out_kernel(side_ref, own_ref, other_ref, query_ref):
     first = side_ref[0] == 0
-    own, other = own_ref[0:12], other_ref[0:12]
-    both = jnp.concatenate([jnp.where(first, own, other), jnp.where(first, other, own)], axis=0)
-    for b in range(B):
-        query_ref[b] = both[:, b * T : (b + 1) * T]
+    own, other = own_ref[:, 0:T], other_ref[:, 0:T]
+    query_ref[0] = jnp.where(first, own, other)
+    query_ref[1] = jnp.where(first, other, own)
 
 
 def keys_out_kernel(got_ref, key_ref, value_ref, dwt_ref):
@@ -332,7 +329,7 @@
 
 def expanded(query, grad):
     shape = bf16(B, HC, QH)
-    outs = [shape, shape, bf16(256, B * HC), bf16(2 * H * 16, HC)]
+    outs = [shape, shape, bf16(256, B * HC), bf16(HC, HC)]
     return call(expand_kernel, outs, 16, flops=400_000_000, moved=5_000_000)(query, grad)
 
 
@@ -367,7 +364,7 @@
     hbm = pl.BlockSpec(memory_space=pltpu.HBM)
     return call(
         scores_kernel,
-        [far(B, 4, T, HC), cell, cell, bf16(PLANE, 24, 256)],
+        [far(B, 4, T, HC), cell, cell, bf16(PLANE, C + H, 128)],
         24,
         flops=2_500_000_000,
         moved=8_000_000,
@@ -415,7 +412,7 @@
 
 
 def bias_out(side, got, keep, more, after):
-    half = f32(16, 256)
+    half = f32(C, 128)
     return call(
         bias_out_kernel,
         [bf16(DEPTH, 3 * C + H, 128), half, half],

time: 73.3 us -> 72 us (0.982)
  waiting for transfers between devices: 7.5 us -> 6.56 us
  transfers between devices with their start and end apart: 6 -> 6, of which waited for: 2 -> 2; matrix products, arithmetic and copies ran while one was open for 0% -> 0% of each run, Pallas kernels for 30% -> 29%
where the time goes in v6:
time: 72 us; the launch traced here: 71.6 us
  Pallas kernels  26.3 us (37%)
  starting transfers between devices  25.2 us (35%)
  blocking collectives  12.9 us (18%)
  waiting for transfers between devices  6.56 us (9%)
    all_to_all x1, blocking collectives, spread_over(): return lax.all_to_all(x, axis, 0, 0, tiled=True, axis_index_groups=groups)  12.9 us
    all_to_all x2, starting transfers between devices, spread_over(): return lax.all_to_all(x, axis, 0, 0, tiled=True, axis_index_groups=groups)  11.9 us
    pallas_call x2, Pallas kernels, pair_grad(): call(lambda *refs: pair_kernel(groups, *(refs if not fresh else refs[:5]...  8.38 us
    pallas_call x1, Pallas kernels, norm(): call(lambda *refs: norm_kernel(groups, *refs), [far(B, G, T, WIDE), f32(B...  7.69 us
    ppermute x1, starting transfers between devices, shards(): k = lax.ppermute(key_in, ('row', 'col'), route)  6.72 us
    all_to_all x2, waiting for transfers between devices, spread_over(): return lax.all_to_all(x, axis, 0, 0, tiled=True, axis_index_groups=groups)  4.38 us
    ppermute x1, starting transfers between devices, shards(): v = lax.ppermute(value_in, ('row', 'col'), route)  4.38 us
    pallas_call x1, Pallas kernels, scores(): call(scores_kernel, [far(B, 4, T, HC), cell, cell, bf16(PLANE, C + H, 128...  2.85 us
  transfers between devices with their start and end apart: 6, of which 2 were waited for; matrix products, arithmetic and copies ran while one was open for 0% of the time, Pallas kernels for 29%

profile of v6, /device:TPU:16, one launch (start us, length us, event | category | flops | bytes accessed | tf_op | source)
XLA Modules:
  0.0 71.6 jit_solution(1665559302858024927)
XLA Ops:
  0.6 6.7 %collective-permute-start = (bf16[2,96,384]{2,1,0:T(8,128)(2,1)}, bf16[2,96,384]{2,1,0:T(8,128)(2,1)S(1)}, u32[]{:S(2)}, u32[]{:S(2)}) collective-permute-start(bf16[2,96,384]{2,1,0:T(8,128)(2,1)} %param.7), channel_id=1, source_target_pairs={{0,80},{1,128},{2,176},{3,144},{4,32},{5,160},{6,112},{7,48},{8,22... | collective-permute-start | bytes 442376 | tf_op jit(solution)/shard_map/ppermute | solution.py:473
  7.3 4.4 %collective-permute-start.1 = (bf16[2,96,384]{2,1,0:T(8,128)(2,1)}, bf16[2,96,384]{2,1,0:T(8,128)(2,1)S(1)}, u32[]{:S(2)}, u32[]{:S(2)}) collective-permute-start(bf16[2,96,384]{2,1,0:T(8,128)(2,1)} %param.8), channel_id=1, source_target_pairs={{0,80},{1,128},{2,176},{3,144},{4,32},{5,160},{6,112},{7,48},{8,22... | collective-permute-start | bytes 442376 | tf_op jit(solution)/shard_map/ppermute | solution.py:474
  11.7 0.0 copy-start.1
  11.7 0.0 copy-start.2
  11.7 7.7 %shard_map.102 = (bf16[2,12,96,1024]{3,2,1,0:T(8,128)(2,1)}, f32[2,12,96,128]{3,2,1,0:T(8,128)S(1)}, bf16[2,12,96,128]{3,2,1,0:T(8,128)(2,1)}, bf16[2,12,96,128]{3,2,1,0:T(8,128)(2,1)}) custom-call(bf16[2,96,96,128]{3,2,1,0:T(8,128)(2,1)} %refs_0_.1, bf16[16,128]{1,0:T(8,128)(2,1)} %bitcast.7), custom_call_target="tpu_custom_call" | custom-call | flops 4000000000 | bytes 12000000 | tf_op jit(solution)/shard_map/pallas_call | solution.py:339
  19.4 0.0 copy-done.1
  19.4 0.0 copy-done.2
  19.4 1.5 %shard_map.101 = (bf16[2,384,1536]{2,1,0:T(8,128)(2,1)S(1)}, bf16[2,384,1536]{2,1,0:T(8,128)(2,1)S(1)}, bf16[256,768]{1,0:T(8,128)(2,1)S(1)}, bf16[384,384]{1,0:T(8,128)(2,1)S(1)}) custom-call(bf16[2,96,384]{2,1,0:T(8,128)(2,1)S(1)} %copy-done.1, bf16[2,96,384]{2,1,0:T(8,128)(2,1)S(1)} %copy-done.2), custom_call_target="tpu_custom_call" | custom-call | flops 400000000 | bytes 5000000 | tf_op jit(solution)/shard_map/pallas_call | solution.py:333
  21.0 0.0 collective-permute-done.k_ref
  21.0 0.0 collective-permute-done.1.v_ref
  21.0 0.0 copy-start
  21.0 1.1 %shard_map.103 = (f32[2,12,96,128]{3,2,1,0:T(8,128)S(1)}, f32[2,12,96,128]{3,2,1,0:T(8,128)S(1)}, f32[16,48,128]{2,1,0:T(8,128)S(1)}) custom-call(bf16[2,96,384]{2,1,0:T(8,128)(2,1)S(1)} %collective-permute-done.k_ref, bf16[2,96,384]{2,1,0:T(8,128)(2,1)S(1)} %collective-permute-done.1.v_ref, bf16[2,384,1536]{2,1,0:T(8,128)(2,1)S(1)} %get-tuple-element.32.qt_ref, ...), custom_call_target="tpu_custom_call" | custom-call | flops 1000000000 | bytes 8000000 | tf_op jit(solution)/shard_map/pallas_call | solution.py:357
  22.1 12.9 %all_to_all.15.stats_ref = f32[16,48,128]{2,1,0:T(8,128)S(1)} all-to-all(f32[16,48,128]{2,1,0:T(8,128)S(1)} %get-tuple-element.35), channel_id=1, replica_groups=mesh['row'=16,'col'=16] {'col'}, dimensions={0} | all-to-all | bytes 786432 | tf_op jit(solution)/shard_map/all_to_all | solution.py:464
  35.0 0.0 copy-done
  35.0 2.9 %shard_map.104 = (bf16[2,4,96,384]{3,2,1,0:T(8,128)(2,1)}, bf16[2,12,96,128]{3,2,1,0:T(8,128)(2,1)}, bf16[2,12,96,128]{3,2,1,0:T(8,128)(2,1)}, bf16[32,40,128]{2,1,0:T(8,128)(2,1)}) custom-call(f32[16,48,128]{2,1,0:T(8,128)S(1)} %all_to_all.15.stats_ref, f32[2,12,96,128]{3,2,1,0:T(8,128)S(1)} %get-tuple-element.36.logits_ref, ...), custom_call_target="tpu_custom_call" | custom-call | flops 2500000000 | bytes 8000000 | tf_op jit(solution)/shard_map/pallas_call | solution.py:365
  37.8 8.2 %all-to-all-start.1 = ((bf16[32,40,128]{2,1,0:T(8,128)(2,1)}), bf16[32,40,128]{2,1,0:T(8,128)(2,1)S(1)}, u32[]{:S(2)}, u32[]{:S(2)}) async-start(bf16[32,40,128]{2,1,0:T(8,128)(2,1)} %get-tuple-element.41), calls=%async_computation.1 | async-start | bytes 655360 | tf_op jit(solution)/shard_map/all_to_all | solution.py:464
  46.1 2.7 %shard_map.105 = (bf16[8,72,128]{2,1,0:T(8,128)(2,1)S(1)}, bf16[8,72,128]{2,1,0:T(8,128)(2,1)S(1)}) custom-call(s32[1]{0:T(128)} %bitcast.side_ref, bf16[2,4,96,384]{3,2,1,0:T(8,128)(2,1)} %get-tuple-element.42.four_ref, bf16[2,12,96,128]{3,2,1,0:T(8,128)(2,1)} %get-tuple-element.43.w_ref, bf16[2,96,384]{2,1,0:T(8,128)(2,1)} %q_ref.3, bf16[2,96,384]{2,1,0:T(8,128)(2,1)} %g_ref.3), custom_call_target="tpu_custom_call" | custom-call | flops 2500000000 | bytes 8000000 | tf_op jit(solution)/shard_map/pallas_call | solution.py:384
  48.7 1.3 %collective-permute-start.2 = (bf16[8,72,128]{2,1,0:T(8,128)(2,1)S(1)}, bf16[8,72,128]{2,1,0:T(8,128)(2,1)S(1)}, u32[]{:S(2)}, u32[]{:S(2)}) collective-permute-start(bf16[8,72,128]{2,1,0:T(8,128)(2,1)S(1)} %get-tuple-element.45), channel_id=1, source_target_pairs={{0,16},{16,0},{32,48},{48,32},{64,80},{80,64},{96,112},{112,96},{1... | collective-permute-start | bytes 442376 | tf_op jit(solution)/shard_map/ppermute | solution.py:468
  50.0 4.2 %shard_map.106._.refs_5_ = bf16[2,96,96,128]{3,2,1,0:T(8,128)(2,1)} custom-call(bf16[2,12,96,128]{3,2,1,0:T(8,128)(2,1)} %get-tuple-element.46.refs_0_, bf16[2,12,96,128]{3,2,1,0:T(8,128)(2,1)} %get-tuple-element.47.refs_1_, bf16[2,12,96,128]{3,2,1,0:T(8,128)(2,1)} %get-tuple-element.48.refs_2_, bf16[2,12,96,1024]{3,2,1,0:T(8,128)(2,1)} %get-tuple-element.40.n_ref.refs_3_, ...), custom_call_target="tpu_custom_call" | custom-call | flops 2000000000 | bytes 5000000 | tf_op jit(solution)/shard_map/pallas_call | solution.py:399
  54.2 2.2 %collective-permute-done.2.more_ref = bf16[8,72,128]{2,1,0:T(8,128)(2,1)S(1)} collective-permute-done((bf16[8,72,128]{2,1,0:T(8,128)(2,1)S(1)}, bf16[8,72,128]{2,1,0:T(8,128)(2,1)S(1)}, u32[]{:S(2)}, u32[]{:S(2)}) %collective-permute-start.2) | collective-permute-done | bytes 147488 | tf_op jit(solution)/shard_map/ppermute | solution.py:468
  56.4 0.0 all-to-all-done.1.got_ref
  56.4 0.7 %shard_map.107 = (bf16[8,88,128]{2,1,0:T(8,128)(2,1)}, f32[24,128]{1,0:T(8,128)S(1)}, f32[24,128]{1,0:T(8,128)S(1)}) custom-call(s32[1]{0:T(128)} %bitcast.side_ref, bf16[32,40,128]{2,1,0:T(8,128)(2,1)S(1)} %all-to-all-done.1.got_ref, bf16[8,72,128]{2,1,0:T(8,128)(2,1)S(1)} %get-tuple-element.44.keep_ref, ...), custom_call_target="tpu_custom_call" | custom-call | tf_op jit(solution)/shard_map/pallas_call | solution.py:416
  57.1 3.7 %all-to-all-start.2 = ((bf16[8,88,128]{2,1,0:T(8,128)(2,1)}), bf16[8,88,128]{2,1,0:T(8,128)(2,1)S(1)}, u32[]{:S(2)}, u32[]{:S(2)}) async-start(bf16[8,88,128]{2,1,0:T(8,128)(2,1)} %get-tuple-element.51), calls=%async_computation.2 | async-start | bytes 360448 | tf_op jit(solution)/shard_map/all_to_all | solution.py:464
  60.8 0.9 %collective-permute-start.3 = (f32[24,128]{1,0:T(8,128)S(1)}, f32[24,128]{1,0:T(8,128)S(1)}, u32[]{:S(2)}, u32[]{:S(2)}) collective-permute-start(f32[24,128]{1,0:T(8,128)S(1)} %get-tuple-element.50), channel_id=1, source_target_pairs={{0,16},{16,0},{32,48},{48,32},{64,80},{80,64},{96,112},{112,96},{1... | collective-permute-start | bytes 36872 | tf_op jit(solution)/shard_map/ppermute | solution.py:468
  61.7 4.2 %shard_map.110 = bf16[2,96,96,128]{3,2,1,0:T(8,128)(2,1)} custom-call(bf16[2,12,96,128]{3,2,1,0:T(8,128)(2,1)} %get-tuple-element.46.refs_0_, bf16[2,12,96,128]{3,2,1,0:T(8,128)(2,1)} %get-tuple-element.47.refs_1_, bf16[2,12,96,128]{3,2,1,0:T(8,128)(2,1)} %get-tuple-element.48.refs_2_, ...), custom_call_target="tpu_custom_call", output_to_operand_aliasing={{}: (5, {})} | custom-call | flops 2000000000 | bytes 5000000 | tf_op jit(solution)/shard_map/pallas_call | solution.py:399
  65.9 0.0 collective-permute-done.3.other_ref
  65.9 0.6 shard_map.108
  66.5 4.4 %all-to-all-done.2.got_ref = bf16[8,88,128]{2,1,0:T(8,128)(2,1)S(1)} async-done(((bf16[8,88,128]{2,1,0:T(8,128)(2,1)}), bf16[8,88,128]{2,1,0:T(8,128)(2,1)S(1)}, u32[]{:S(2)}, u32[]{:S(2)}) %all-to-all-start.2) | async-done | bytes 180256 | tf_op jit(solution)/shard_map/all_to_all | solution.py:464
  70.9 0.7 shard_map.109
Async XLA Ops:
  0.6 20.4 %collective-permute-start = (bf16[2,96,384]{2,1,0:T(8,128)(2,1)}, bf16[2,96,384]{2,1,0:T(8,128)(2,1)S(1)}, u32[]{:S(2)}, u32[]{:S(2)}) collective-permute-start(bf16[2,96,384]{2,1,0:T(8,128)(2,1)} %param.7), channel_id=1, source_target_pairs={{0,80},{1,128},{2,176},{3,144},{4,32},{5,160},{6,112},{7,48},{8,22... | collective-permute-start | bytes 442376 | tf_op jit(solution)/shard_map/ppermute | solution.py:473
  7.3 13.7 %collective-permute-start.1 = (bf16[2,96,384]{2,1,0:T(8,128)(2,1)}, bf16[2,96,384]{2,1,0:T(8,128)(2,1)S(1)}, u32[]{:S(2)}, u32[]{:S(2)}) collective-permute-start(bf16[2,96,384]{2,1,0:T(8,128)(2,1)} %param.8), channel_id=1, source_target_pairs={{0,80},{1,128},{2,176},{3,144},{4,32},{5,160},{6,112},{7,48},{8,22... | collective-permute-start | bytes 442376 | tf_op jit(solution)/shard_map/ppermute | solution.py:474
  11.7 7.7 %copy-start.1 = (bf16[2,96,384]{2,1,0:T(8,128)(2,1)S(1)}, bf16[2,96,384]{2,1,0:T(8,128)(2,1)}, u32[]{:S(2)}) copy-start(bf16[2,96,384]{2,1,0:T(8,128)(2,1)} %q_ref.3) | copy-start | bytes 442372
  11.7 7.7 %copy-start.2 = (bf16[2,96,384]{2,1,0:T(8,128)(2,1)S(1)}, bf16[2,96,384]{2,1,0:T(8,128)(2,1)}, u32[]{:S(2)}) copy-start(bf16[2,96,384]{2,1,0:T(8,128)(2,1)} %g_ref.3) | copy-start | bytes 442372
  21.0 14.0 %copy-start = (bf16[2,12,96,1024]{3,2,1,0:T(8,128)(2,1)S(1)}, bf16[2,12,96,1024]{3,2,1,0:T(8,128)(2,1)}, u32[]{:S(2)}) copy-start(bf16[2,12,96,1024]{3,2,1,0:T(8,128)(2,1)} %get-tuple-element.40.n_ref.refs_3_) | copy-start | bytes 14155780
  37.8 18.5 %all-to-all-start.1 = ((bf16[32,40,128]{2,1,0:T(8,128)(2,1)}), bf16[32,40,128]{2,1,0:T(8,128)(2,1)S(1)}, u32[]{:S(2)}, u32[]{:S(2)}) async-start(bf16[32,40,128]{2,1,0:T(8,128)(2,1)} %get-tuple-element.41), calls=%async_computation.1 | async-start | bytes 655360 | tf_op jit(solution)/shard_map/all_to_all | solution.py:464
  48.7 7.6 %collective-permute-start.2 = (bf16[8,72,128]{2,1,0:T(8,128)(2,1)S(1)}, bf16[8,72,128]{2,1,0:T(8,128)(2,1)S(1)}, u32[]{:S(2)}, u32[]{:S(2)}) collective-permute-start(bf16[8,72,128]{2,1,0:T(8,128)(2,1)S(1)} %get-tuple-element.45), channel_id=1, source_target_pairs={{0,16},{16,0},{32,48},{48,32},{64,80},{80,64},{96,112},{112,96},{1... | collective-permute-start | bytes 442376 | tf_op jit(solution)/shard_map/ppermute | solution.py:468
  57.1 13.8 %all-to-all-start.2 = ((bf16[8,88,128]{2,1,0:T(8,128)(2,1)}), bf16[8,88,128]{2,1,0:T(8,128)(2,1)S(1)}, u32[]{:S(2)}, u32[]{:S(2)}) async-start(bf16[8,88,128]{2,1,0:T(8,128)(2,1)} %get-tuple-element.51), calls=%async_computation.2 | async-start | bytes 360448 | tf_op jit(solution)/shard_map/all_to_all | solution.py:464
  60.8 5.1 %collective-permute-start.3 = (f32[24,128]{1,0:T(8,128)S(1)}, f32[24,128]{1,0:T(8,128)S(1)}, u32[]{:S(2)}, u32[]{:S(2)}) collective-permute-start(f32[24,128]{1,0:T(8,128)S(1)} %get-tuple-element.50), channel_id=1, source_target_pairs={{0,16},{16,0},{32,48},{48,32},{64,80},{80,64},{96,112},{112,96},{1... | collective-permute-start | bytes 36872 | tf_op jit(solution)/shard_map/ppermute | solution.py:468

commit v7 on v6

--- a/solution.py
+++ b/solution.py
@@ -76,6 +76,13 @@
     turn_ref[...] = jnp.where(iota((HC, HC), 0) == iota((HC, HC), 1), 1.0, 0.0).astype(BF16)
 
 
+def lane_means(wide):
+    means = [
+        jnp.mean(wide[:, k * CP : (k + 1) * CP], axis=1, keepdims=True) for k in range(2)
+    ]
+    return jnp.concatenate([jnp.broadcast_to(m, (wide.shape[0], CP)) for m in means], axis=1)
+
+
 def norm_kernel(
     groups, pair_ref, wt_ref, n_ref, bias_ref, low_bias_ref, inv_ref, ones_ref, diag_ref
 ):
@@ -102,11 +109,12 @@
             axis=0,
         )
         wide = x.astype(F32)
-        means = [
-            jnp.mean(wide[:, k * CP : (k + 1) * CP], axis=1, keepdims=True) for k in range(2)
-        ]
-        centred = wide - jnp.concatenate([jnp.broadcast_to(m, (rows, CP)) for m in means], axis=1)
-        spread = dot((centred * centred).astype(BF16), ones)
+        if p < I8 // 4:
+            centred = wide - lane_means(wide)
+            spread = dot((centred * centred).astype(BF16), ones)
+        else:
+            centred = wide - dot(x, ones)
+            spread = lane_means(centred * centred)
         inverse = lax.rsqrt(spread + EPS)
         normed = (centred * inverse).astype(BF16)
         n_ref[0, :, :, p * 256 : (p + 1) * 256] = normed.reshape(groups, T, 256)

time: 72 us -> 72 us (level)
  no operation moved by 1% of the time
where the time goes in v7:
time: 72 us; the launch traced here: 71.6 us
  Pallas kernels  26 us (36%)
  starting transfers between devices  25.4 us (35%)
  blocking collectives  12.9 us (18%)
  waiting for transfers between devices  6.56 us (9%)
    all_to_all x1, blocking collectives, spread_over(): return lax.all_to_all(x, axis, 0, 0, tiled=True, axis_index_groups=groups)  12.9 us
    all_to_all x2, starting transfers between devices, spread_over(): return lax.all_to_all(x, axis, 0, 0, tiled=True, axis_index_groups=groups)  12.1 us
    pallas_call x2, Pallas kernels, pair_grad(): call(lambda *refs: pair_kernel(groups, *(refs if not fresh else refs[:5]...  8.38 us
    pallas_call x1, Pallas kernels, norm(): call(lambda *refs: norm_kernel(groups, *refs), [far(B, G, T, WIDE), f32(B...  7.47 us
    ppermute x1, starting transfers between devices, shards(): k = lax.ppermute(key_in, ('row', 'col'), route)  6.72 us
    all_to_all x2, waiting for transfers between devices, spread_over(): return lax.all_to_all(x, axis, 0, 0, tiled=True, axis_index_groups=groups)  4.38 us
    ppermute x1, starting transfers between devices, shards(): v = lax.ppermute(value_in, ('row', 'col'), route)  4.38 us
    pallas_call x1, Pallas kernels, scores(): call(scores_kernel, [far(B, 4, T, HC), cell, cell, bf16(PLANE, C + H, 128...  2.85 us
  transfers between devices with their start and end apart: 6, of which 2 were waited for; matrix products, arithmetic and copies ran while one was open for 0% of the time, Pallas kernels for 29%

profile of v7, /device:TPU:16, one launch (start us, length us, event | category | flops | bytes accessed | tf_op | source)
XLA Modules:
  0.0 71.6 jit_solution(1863350461441030410)
XLA Ops:
  0.6 6.7 %collective-permute-start = (bf16[2,96,384]{2,1,0:T(8,128)(2,1)}, bf16[2,96,384]{2,1,0:T(8,128)(2,1)S(1)}, u32[]{:S(2)}, u32[]{:S(2)}) collective-permute-start(bf16[2,96,384]{2,1,0:T(8,128)(2,1)} %param.7), channel_id=1, source_target_pairs={{0,80},{1,128},{2,176},{3,144},{4,32},{5,160},{6,112},{7,48},{8,22... | collective-permute-start | bytes 442376 | tf_op jit(solution)/shard_map/ppermute | solution.py:481
  7.3 4.4 %collective-permute-start.1 = (bf16[2,96,384]{2,1,0:T(8,128)(2,1)}, bf16[2,96,384]{2,1,0:T(8,128)(2,1)S(1)}, u32[]{:S(2)}, u32[]{:S(2)}) collective-permute-start(bf16[2,96,384]{2,1,0:T(8,128)(2,1)} %param.8), channel_id=1, source_target_pairs={{0,80},{1,128},{2,176},{3,144},{4,32},{5,160},{6,112},{7,48},{8,22... | collective-permute-start | bytes 442376 | tf_op jit(solution)/shard_map/ppermute | solution.py:482
  11.7 0.0 copy-start.1
  11.7 0.0 copy-start.2
  11.7 7.5 %shard_map.102 = (bf16[2,12,96,1024]{3,2,1,0:T(8,128)(2,1)}, f32[2,12,96,128]{3,2,1,0:T(8,128)S(1)}, bf16[2,12,96,128]{3,2,1,0:T(8,128)(2,1)}, bf16[2,12,96,128]{3,2,1,0:T(8,128)(2,1)}) custom-call(bf16[2,96,96,128]{3,2,1,0:T(8,128)(2,1)} %refs_0_.1, bf16[16,128]{1,0:T(8,128)(2,1)} %bitcast.7), custom_call_target="tpu_custom_call" | custom-call | flops 4000000000 | bytes 12000000 | tf_op jit(solution)/shard_map/pallas_call | solution.py:347
  19.2 0.0 copy-done.1
  19.2 0.0 copy-done.2
  19.2 1.5 %shard_map.101 = (bf16[2,384,1536]{2,1,0:T(8,128)(2,1)S(1)}, bf16[2,384,1536]{2,1,0:T(8,128)(2,1)S(1)}, bf16[256,768]{1,0:T(8,128)(2,1)S(1)}, bf16[384,384]{1,0:T(8,128)(2,1)S(1)}) custom-call(bf16[2,96,384]{2,1,0:T(8,128)(2,1)S(1)} %copy-done.1, bf16[2,96,384]{2,1,0:T(8,128)(2,1)S(1)} %copy-done.2), custom_call_target="tpu_custom_call" | custom-call | flops 400000000 | bytes 5000000 | tf_op jit(solution)/shard_map/pallas_call | solution.py:341
  20.8 0.0 collective-permute-done.k_ref
  20.8 0.0 collective-permute-done.1.v_ref
  20.8 0.0 copy-start
  20.8 1.1 %shard_map.103 = (f32[2,12,96,128]{3,2,1,0:T(8,128)S(1)}, f32[2,12,96,128]{3,2,1,0:T(8,128)S(1)}, f32[16,48,128]{2,1,0:T(8,128)S(1)}) custom-call(bf16[2,96,384]{2,1,0:T(8,128)(2,1)S(1)} %collective-permute-done.k_ref, bf16[2,96,384]{2,1,0:T(8,128)(2,1)S(1)} %collective-permute-done.1.v_ref, bf16[2,384,1536]{2,1,0:T(8,128)(2,1)S(1)} %get-tuple-element.32.qt_ref, ...), custom_call_target="tpu_custom_call" | custom-call | flops 1000000000 | bytes 8000000 | tf_op jit(solution)/shard_map/pallas_call | solution.py:365
  21.9 12.9 %all_to_all.15.stats_ref = f32[16,48,128]{2,1,0:T(8,128)S(1)} all-to-all(f32[16,48,128]{2,1,0:T(8,128)S(1)} %get-tuple-element.35), channel_id=1, replica_groups=mesh['row'=16,'col'=16] {'col'}, dimensions={0} | all-to-all | bytes 786432 | tf_op jit(solution)/shard_map/all_to_all | solution.py:472
  34.8 0.0 copy-done
  34.8 2.9 %shard_map.104 = (bf16[2,4,96,384]{3,2,1,0:T(8,128)(2,1)}, bf16[2,12,96,128]{3,2,1,0:T(8,128)(2,1)}, bf16[2,12,96,128]{3,2,1,0:T(8,128)(2,1)}, bf16[32,40,128]{2,1,0:T(8,128)(2,1)}) custom-call(f32[16,48,128]{2,1,0:T(8,128)S(1)} %all_to_all.15.stats_ref, f32[2,12,96,128]{3,2,1,0:T(8,128)S(1)} %get-tuple-element.36.logits_ref, ...), custom_call_target="tpu_custom_call" | custom-call | flops 2500000000 | bytes 8000000 | tf_op jit(solution)/shard_map/pallas_call | solution.py:373
  37.6 8.2 %all-to-all-start.1 = ((bf16[32,40,128]{2,1,0:T(8,128)(2,1)}), bf16[32,40,128]{2,1,0:T(8,128)(2,1)S(1)}, u32[]{:S(2)}, u32[]{:S(2)}) async-start(bf16[32,40,128]{2,1,0:T(8,128)(2,1)} %get-tuple-element.41), calls=%async_computation.1 | async-start | bytes 655360 | tf_op jit(solution)/shard_map/all_to_all | solution.py:472
  45.8 2.7 %shard_map.105 = (bf16[8,72,128]{2,1,0:T(8,128)(2,1)S(1)}, bf16[8,72,128]{2,1,0:T(8,128)(2,1)S(1)}) custom-call(s32[1]{0:T(128)} %bitcast.side_ref, bf16[2,4,96,384]{3,2,1,0:T(8,128)(2,1)} %get-tuple-element.42.four_ref, bf16[2,12,96,128]{3,2,1,0:T(8,128)(2,1)} %get-tuple-element.43.w_ref, bf16[2,96,384]{2,1,0:T(8,128)(2,1)} %q_ref.3, bf16[2,96,384]{2,1,0:T(8,128)(2,1)} %g_ref.3), custom_call_target="tpu_custom_call" | custom-call | flops 2500000000 | bytes 8000000 | tf_op jit(solution)/shard_map/pallas_call | solution.py:392
  48.5 1.3 %collective-permute-start.2 = (bf16[8,72,128]{2,1,0:T(8,128)(2,1)S(1)}, bf16[8,72,128]{2,1,0:T(8,128)(2,1)S(1)}, u32[]{:S(2)}, u32[]{:S(2)}) collective-permute-start(bf16[8,72,128]{2,1,0:T(8,128)(2,1)S(1)} %get-tuple-element.45), channel_id=1, source_target_pairs={{0,16},{16,0},{32,48},{48,32},{64,80},{80,64},{96,112},{112,96},{1... | collective-permute-start | bytes 442376 | tf_op jit(solution)/shard_map/ppermute | solution.py:476
  49.8 4.2 %shard_map.106._.refs_5_ = bf16[2,96,96,128]{3,2,1,0:T(8,128)(2,1)} custom-call(bf16[2,12,96,128]{3,2,1,0:T(8,128)(2,1)} %get-tuple-element.46.refs_0_, bf16[2,12,96,128]{3,2,1,0:T(8,128)(2,1)} %get-tuple-element.47.refs_1_, bf16[2,12,96,128]{3,2,1,0:T(8,128)(2,1)} %get-tuple-element.48.refs_2_, bf16[2,12,96,1024]{3,2,1,0:T(8,128)(2,1)} %get-tuple-element.40.n_ref.refs_3_, ...), custom_call_target="tpu_custom_call" | custom-call | flops 2000000000 | bytes 5000000 | tf_op jit(solution)/shard_map/pallas_call | solution.py:407
  54.0 2.2 %collective-permute-done.2.more_ref = bf16[8,72,128]{2,1,0:T(8,128)(2,1)S(1)} collective-permute-done((bf16[8,72,128]{2,1,0:T(8,128)(2,1)S(1)}, bf16[8,72,128]{2,1,0:T(8,128)(2,1)S(1)}, u32[]{:S(2)}, u32[]{:S(2)}) %collective-permute-start.2) | collective-permute-done | bytes 147488 | tf_op jit(solution)/shard_map/ppermute | solution.py:476
  56.1 0.0 all-to-all-done.1.got_ref
  56.1 0.7 %shard_map.107 = (bf16[8,88,128]{2,1,0:T(8,128)(2,1)}, f32[24,128]{1,0:T(8,128)S(1)}, f32[24,128]{1,0:T(8,128)S(1)}) custom-call(s32[1]{0:T(128)} %bitcast.side_ref, bf16[32,40,128]{2,1,0:T(8,128)(2,1)S(1)} %all-to-all-done.1.got_ref, bf16[8,72,128]{2,1,0:T(8,128)(2,1)S(1)} %get-tuple-element.44.keep_ref, ...), custom_call_target="tpu_custom_call" | custom-call | tf_op jit(solution)/shard_map/pallas_call | solution.py:424
  56.9 3.9 %all-to-all-start.2 = ((bf16[8,88,128]{2,1,0:T(8,128)(2,1)}), bf16[8,88,128]{2,1,0:T(8,128)(2,1)S(1)}, u32[]{:S(2)}, u32[]{:S(2)}) async-start(bf16[8,88,128]{2,1,0:T(8,128)(2,1)} %get-tuple-element.51), calls=%async_computation.2 | async-start | bytes 360448 | tf_op jit(solution)/shard_map/all_to_all | solution.py:472
  60.8 0.9 %collective-permute-start.3 = (f32[24,128]{1,0:T(8,128)S(1)}, f32[24,128]{1,0:T(8,128)S(1)}, u32[]{:S(2)}, u32[]{:S(2)}) collective-permute-start(f32[24,128]{1,0:T(8,128)S(1)} %get-tuple-element.50), channel_id=1, source_target_pairs={{0,16},{16,0},{32,48},{48,32},{64,80},{80,64},{96,112},{112,96},{1... | collective-permute-start | bytes 36872 | tf_op jit(solution)/shard_map/ppermute | solution.py:476
  61.7 4.2 %shard_map.110 = bf16[2,96,96,128]{3,2,1,0:T(8,128)(2,1)} custom-call(bf16[2,12,96,128]{3,2,1,0:T(8,128)(2,1)} %get-tuple-element.46.refs_0_, bf16[2,12,96,128]{3,2,1,0:T(8,128)(2,1)} %get-tuple-element.47.refs_1_, bf16[2,12,96,128]{3,2,1,0:T(8,128)(2,1)} %get-tuple-element.48.refs_2_, ...), custom_call_target="tpu_custom_call", output_to_operand_aliasing={{}: (5, {})} | custom-call | flops 2000000000 | bytes 5000000 | tf_op jit(solution)/shard_map/pallas_call | solution.py:407
  65.9 0.0 collective-permute-done.3.other_ref
  65.9 0.6 shard_map.108
  66.5 4.4 %all-to-all-done.2.got_ref = bf16[8,88,128]{2,1,0:T(8,128)(2,1)S(1)} async-done(((bf16[8,88,128]{2,1,0:T(8,128)(2,1)}), bf16[8,88,128]{2,1,0:T(8,128)(2,1)S(1)}, u32[]{:S(2)}, u32[]{:S(2)}) %all-to-all-start.2) | async-done | bytes 180256 | tf_op jit(solution)/shard_map/all_to_all | solution.py:472
  70.9 0.7 shard_map.109
Async XLA Ops:
  0.6 20.1 %collective-permute-start = (bf16[2,96,384]{2,1,0:T(8,128)(2,1)}, bf16[2,96,384]{2,1,0:T(8,128)(2,1)S(1)}, u32[]{:S(2)}, u32[]{:S(2)}) collective-permute-start(bf16[2,96,384]{2,1,0:T(8,128)(2,1)} %param.7), channel_id=1, source_target_pairs={{0,80},{1,128},{2,176},{3,144},{4,32},{5,160},{6,112},{7,48},{8,22... | collective-permute-start | bytes 442376 | tf_op jit(solution)/shard_map/ppermute | solution.py:481
  7.3 13.4 %collective-permute-start.1 = (bf16[2,96,384]{2,1,0:T(8,128)(2,1)}, bf16[2,96,384]{2,1,0:T(8,128)(2,1)S(1)}, u32[]{:S(2)}, u32[]{:S(2)}) collective-permute-start(bf16[2,96,384]{2,1,0:T(8,128)(2,1)} %param.8), channel_id=1, source_target_pairs={{0,80},{1,128},{2,176},{3,144},{4,32},{5,160},{6,112},{7,48},{8,22... | collective-permute-start | bytes 442376 | tf_op jit(solution)/shard_map/ppermute | solution.py:482
  11.7 7.5 %copy-start.1 = (bf16[2,96,384]{2,1,0:T(8,128)(2,1)S(1)}, bf16[2,96,384]{2,1,0:T(8,128)(2,1)}, u32[]{:S(2)}) copy-start(bf16[2,96,384]{2,1,0:T(8,128)(2,1)} %q_ref.3) | copy-start | bytes 442372
  11.7 7.5 %copy-start.2 = (bf16[2,96,384]{2,1,0:T(8,128)(2,1)S(1)}, bf16[2,96,384]{2,1,0:T(8,128)(2,1)}, u32[]{:S(2)}) copy-start(bf16[2,96,384]{2,1,0:T(8,128)(2,1)} %g_ref.3) | copy-start | bytes 442372
  20.8 14.0 %copy-start = (bf16[2,12,96,1024]{3,2,1,0:T(8,128)(2,1)S(1)}, bf16[2,12,96,1024]{3,2,1,0:T(8,128)(2,1)}, u32[]{:S(2)}) copy-start(bf16[2,12,96,1024]{3,2,1,0:T(8,128)(2,1)} %get-tuple-element.40.n_ref.refs_3_) | copy-start | bytes 14155780
  37.6 18.5 %all-to-all-start.1 = ((bf16[32,40,128]{2,1,0:T(8,128)(2,1)}), bf16[32,40,128]{2,1,0:T(8,128)(2,1)S(1)}, u32[]{:S(2)}, u32[]{:S(2)}) async-start(bf16[32,40,128]{2,1,0:T(8,128)(2,1)} %get-tuple-element.41), calls=%async_computation.1 | async-start | bytes 655360 | tf_op jit(solution)/shard_map/all_to_all | solution.py:472
  48.5 7.6 %collective-permute-start.2 = (bf16[8,72,128]{2,1,0:T(8,128)(2,1)S(1)}, bf16[8,72,128]{2,1,0:T(8,128)(2,1)S(1)}, u32[]{:S(2)}, u32[]{:S(2)}) collective-permute-start(bf16[8,72,128]{2,1,0:T(8,128)(2,1)S(1)} %get-tuple-element.45), channel_id=1, source_target_pairs={{0,16},{16,0},{32,48},{48,32},{64,80},{80,64},{96,112},{112,96},{1... | collective-permute-start | bytes 442376 | tf_op jit(solution)/shard_map/ppermute | solution.py:476
  56.9 14.0 %all-to-all-start.2 = ((bf16[8,88,128]{2,1,0:T(8,128)(2,1)}), bf16[8,88,128]{2,1,0:T(8,128)(2,1)S(1)}, u32[]{:S(2)}, u32[]{:S(2)}) async-start(bf16[8,88,128]{2,1,0:T(8,128)(2,1)} %get-tuple-element.51), calls=%async_computation.2 | async-start | bytes 360448 | tf_op jit(solution)/shard_map/all_to_all | solution.py:472
  60.8 5.1 %collective-permute-start.3 = (f32[24,128]{1,0:T(8,128)S(1)}, f32[24,128]{1,0:T(8,128)S(1)}, u32[]{:S(2)}, u32[]{:S(2)}) collective-permute-start(f32[24,128]{1,0:T(8,128)S(1)} %get-tuple-element.50), channel_id=1, source_target_pairs={{0,16},{16,0},{32,48},{48,32},{64,80},{80,64},{96,112},{112,96},{1... | collective-permute-start | bytes 36872 | tf_op jit(solution)/shard_map/ppermute | solution.py:476
